TPU v7x, 256 devices: a whole 4x4x8 slice. The times are simulated.
256 devices in a mesh: lat: 16 (over x, y_lo, core), lon: 16 (over z, y_hi).
Axes of the slice: x: 4, y: 4 (y_hi: 2, y_lo: 2; y = y_hi * 2 + y_lo), z: 8, core: 2. Of those that a mesh axis runs over, the one named last changes fastest.
Arguments:
- tokens: bfloat16 [4, 192, 384, 512], P(None, 'lat', 'lon'), may hold values from -6 to 6
- enc_gain: float32 [512], replicated, may hold values from 0.1 to 1.9
- enc_qkv: bfloat16 [512, 1536], P('lat', 'lon'), as said below
- enc_proj: bfloat16 [512, 512], P('lat', 'lon'), may hold values from -0.25 to 0.25
- merge_gain: float32 [2048], replicated, may hold values from 0.1 to 1.9
- merge_weight: bfloat16 [2048, 1024], P('lat', 'lon'), may hold values from -0.125 to 0.125
- split_weight: bfloat16 [1024, 2048], P('lat', 'lon'), may hold values from -0.1875 to 0.1875
- split_gain: float32 [512], replicated, may hold values from 0.1 to 1.9
- dec_gain: float32 [512], replicated, may hold values from 0.1 to 1.9
- dec_qkv: bfloat16 [512, 1536], P('lat', 'lon'), as said below
- dec_proj: bfloat16 [512, 512], P('lat', 'lon'), may hold values from -0.25 to 0.25
Outputs:
- decoded: bfloat16 [4, 192, 384, 512], P(None, 'lat', 'lon')
Inputs may be any that keep to these rules, and one draw needn't show every extreme that they name: `enc_qkv`: a query, key and value projection of 8 heads. `dec_qkv`: a query, key and value projection of 8 heads.
All inputs are finite; a program needn't handle non-finite values.
Results may differ from a plain program's by a relative error of at most 0.04.
Values may be sent and summed in bfloat16 or wider, within the bound.
No kernel may reach another device: no remote copies, remote signals or barrier semaphores. Data moves between devices by JAX's collectives and lax.ppermute only.
A program may use at most 192 MiB of HBM per device.

v0:
```python
import jax
import jax.numpy as jnp
from jax import lax
from jax.sharding import PartitionSpec as P

HEADS = 8
WL = 2
WA = 6
WO = 12


eps = 1e-05


def passed_along(value, axis, steps):
    count = lax.axis_size(axis)
    pairs = [(source, (source + steps) % count) for source in range(count)]
    return lax.ppermute(value, axis, pairs)


def layer_norm(values, gain):
    center = jnp.mean(values, axis=-1, keepdims=True)
    centred = values - center
    spread = jnp.mean(centred * centred, axis=-1, keepdims=True)
    return centred * lax.rsqrt(spread + eps) * gain


def region_labels(index, count, window):
    return (index >= count - window).astype(jnp.int32) + (index >= count - window // 2).astype(
        jnp.int32
    )


def attend(normed, qkv_weight, proj_weight, level_labels, lat_labels):
    levels, rows, cols, width = normed.shape
    head_dim = width // HEADS
    window_tokens = WL * WA * WO
    projected = jnp.dot(
        normed.reshape(-1, width), qkv_weight, preferred_element_type=jnp.float32
    ).astype(jnp.bfloat16)
    projected = projected.reshape(
        levels // WL, WL, rows // WA, WA, cols // WO, WO, 3, HEADS, head_dim
    )
    projected = projected.transpose(0, 2, 4, 6, 7, 1, 3, 5, 8).reshape(
        -1, 3, HEADS, window_tokens, head_dim
    )
    labels = (
        level_labels[:, None, None] * 3
        + lat_labels[None, :, None]
        + jnp.zeros((1, 1, cols), jnp.int32)
    )
    labels = (
        labels.reshape(levels // WL, WL, rows // WA, WA, cols // WO, WO)
        .transpose(0, 2, 4, 1, 3, 5)
        .reshape(-1, window_tokens)
    )
    scores = jnp.einsum(
        "nhqd,nhkd->nhqk", projected[:, 0], projected[:, 1], preferred_element_type=jnp.float32
    ) * head_dim ** (-0.5)
    same = labels[:, None, :, None] == labels[:, None, None, :]
    scores = jnp.where(same, scores, -jnp.inf)
    weights = jax.nn.softmax(scores, axis=-1).astype(jnp.bfloat16)
    mixed = jnp.einsum(
        "nhqk,nhkd->nhqd", weights, projected[:, 2], preferred_element_type=jnp.float32
    ).astype(jnp.bfloat16)
    mixed = mixed.reshape(levels // WL, rows // WA, cols // WO, HEADS, WL, WA, WO, head_dim)
    mixed = mixed.transpose(0, 4, 1, 5, 2, 6, 3, 7).reshape(-1, width)
    output = jnp.dot(mixed, proj_weight, preferred_element_type=jnp.float32).astype(jnp.bfloat16)
    return output.reshape(levels, rows, cols, width)


def shards(
    tokens,
    enc_gain,
    enc_qkv,
    enc_proj,
    merge_gain,
    merge_weight,
    split_weight,
    split_gain,
    dec_gain,
    dec_qkv,
    dec_proj,
):
    part_a, part_b, part_c, part_d, part_e, part_f = (
        lax.all_gather(enc_qkv, "lat", axis=0, tiled=True),
        lax.all_gather(enc_proj, "lat", axis=0, tiled=True),
        lax.all_gather(merge_weight, "lat", axis=0, tiled=True),
        lax.all_gather(split_weight, "lat", axis=0, tiled=True),
        lax.all_gather(dec_qkv, "lat", axis=0, tiled=True),
        lax.all_gather(dec_proj, "lat", axis=0, tiled=True),
    )
    full_qkv, full_proj, full_merge, full_split, full_dqkv, full_dproj = (
        lax.all_gather(part_a, "lon", axis=1, tiled=True),
        lax.all_gather(part_b, "lon", axis=1, tiled=True),
        lax.all_gather(part_c, "lon", axis=1, tiled=True),
        lax.all_gather(part_d, "lon", axis=1, tiled=True),
        lax.all_gather(part_e, "lon", axis=1, tiled=True),
        lax.all_gather(part_f, "lon", axis=1, tiled=True),
    )
    levels, rows, cols, width = tokens.shape
    total_rows = rows * lax.axis_size("lat")
    row_start = lax.axis_index("lat") * rows
    half_lat = WA // 2
    half_lon = WO // 2
    enc_normed = layer_norm(tokens.astype(jnp.float32), enc_gain).astype(jnp.bfloat16)
    rolled = jnp.roll(enc_normed, -(WL // 2), axis=0)
    level_labels = region_labels(jnp.arange(levels), levels, WL)
    below = passed_along(rolled[:, :half_lat], "lat", -1)
    extended = jnp.concatenate([rolled[:, half_lat:], below], 1)
    beyond = passed_along(extended[:, :, :half_lon], "lon", -1)
    framed = jnp.concatenate([extended[:, :, half_lon:], beyond], 2)
    lat_labels = region_labels(row_start + jnp.arange(rows), total_rows, WA)
    branch = attend(framed, full_qkv, full_proj, level_labels, lat_labels)
    from_left = passed_along(branch[:, :, cols - half_lon :], "lon", 1)
    placed = jnp.concatenate([from_left, branch[:, :, : cols - half_lon]], 2)
    from_above = passed_along(placed[:, rows - half_lat :], "lat", 1)
    restored = jnp.concatenate([from_above, placed[:, : rows - half_lat]], 1)
    enc_branch = jnp.roll(restored, WL // 2, axis=0)
    encoded = (tokens.astype(jnp.float32) + enc_branch.astype(jnp.float32)).astype(jnp.bfloat16)
    quads = jnp.concatenate(
        [
            encoded[:, 0::2, 0::2],
            encoded[:, 1::2, 0::2],
            encoded[:, 0::2, 1::2],
            encoded[:, 1::2, 1::2],
        ],
        -1,
    )
    merged_normed = layer_norm(quads.astype(jnp.float32), merge_gain).astype(jnp.bfloat16)
    middle = jnp.dot(
        merged_normed.reshape(-1, 4 * width), full_merge, preferred_element_type=jnp.float32
    ).astype(jnp.bfloat16)
    split_flat = jnp.dot(middle, full_split, preferred_element_type=jnp.float32)
    split_out = (
        split_flat.reshape(levels, rows // 2, cols // 2, 2, 2, width)
        .transpose(0, 1, 3, 2, 4, 5)
        .reshape(levels, rows, cols, width)
    )
    joined = (layer_norm(split_out, split_gain) + encoded.astype(jnp.float32)).astype(jnp.bfloat16)
    dec_normed = layer_norm(joined.astype(jnp.float32), dec_gain).astype(jnp.bfloat16)
    dec_branch = attend(
        dec_normed,
        full_dqkv,
        full_dproj,
        jnp.zeros((levels,), jnp.int32),
        jnp.zeros((rows,), jnp.int32),
    )
    return (joined.astype(jnp.float32) + dec_branch.astype(jnp.float32)).astype(jnp.bfloat16)


def solution(mesh):
    return jax.shard_map(
        shards,
        mesh=mesh,
        in_specs=(
            P(None, "lat", "lon", None),
            P(),
            P("lat", "lon"),
            P("lat", "lon"),
            P(),
            P("lat", "lon"),
            P("lat", "lon"),
            P(),
            P(),
            P("lat", "lon"),
            P("lat", "lon"),
        ),
        out_specs=P(None, "lat", "lon", None),
        check_vma=False,
    )
```

profile of v0, /device:TPU:1, one launch (start us, length us, event | category | flops | bytes accessed | tf_op | source)
XLA Modules:
  0.0 474.6 jit_solution(12540212380893509986)
XLA Ops:
  6.5 21.7 %all_gather.36 = bf16[512,96]{1,0:T(8,128)(2,1)S(1)} all-gather(bf16[32,96]{1,0:T(8,128)(2,1)} %param.13), channel_id=1, replica_groups=mesh['lat'=16,'lon'=16] {'lat'}, dimensions={0}, use_global_device_ids=true | all-gather | bytes 104448 | tf_op jit(solution)/shard_map/all_gather | solution.py:86
  29.1 18.6 %all_gather.40 = bf16[2048,64]{0,1:T(8,128)(2,1)} all-gather(bf16[128,64]{0,1:T(8,128)(2,1)} %param.16), channel_id=1, replica_groups=mesh['lat'=16,'lon'=16] {'lat'}, dimensions={0}, use_global_device_ids=true | all-gather | bytes 278528 | tf_op jit(solution)/shard_map/all_gather | solution.py:88
  47.8 19.9 %all_gather.42 = bf16[1024,128]{1,0:T(8,128)(2,1)} all-gather(bf16[64,128]{1,0:T(8,128)(2,1)} %param.17), channel_id=1, replica_groups=mesh['lat'=16,'lon'=16] {'lat'}, dimensions={0}, use_global_device_ids=true | all-gather | bytes 278528 | tf_op jit(solution)/shard_map/all_gather | solution.py:89
  71.9 18.4 %all_gather.38 = bf16[512,32]{1,0:T(8,128)(2,1)S(1)} all-gather(bf16[32,32]{1,0:T(8,128)(2,1)S(1)} %copy-done.5), channel_id=1, replica_groups=mesh['lat'=16,'lon'=16] {'lat'}, dimensions={0}, use_global_device_ids=true | all-gather | bytes 34816 | tf_op jit(solution)/shard_map/all_gather | solution.py:87
  90.4 42.7 %all_gather.39 = bf16[512,512]{0,1:T(8,128)(2,1)} all-gather(bf16[512,32]{0,1:T(8,128)(2,1)S(1)} %copy.91), channel_id=1, replica_groups=mesh['lat'=16,'lon'=16] {'lon'}, dimensions={1}, use_global_device_ids=true | all-gather | bytes 557056 | tf_op jit(solution)/shard_map/all_gather | solution.py:95
  134.9 7.2 %collective-permute-done.1 = bf16[4,12,6,512]{3,2,1,0:T(8,128)(2,1)S(1)} collective-permute-done((bf16[4,12,6,512]{3,2,1,0:T(8,128)(2,1)S(1)}, bf16[4,12,6,512]{3,2,1,0:T(8,128)(2,1)S(1)}, u32[]{:S(2)}, u32[]{:S(2)}) %collective-permute-start.1) | collective-permute-done | bytes 294944 | tf_op jit(solution)/shard_map/ppermute | solution.py:18
  142.4 5.2 %convolution_convert_fusion.1 = bf16[1152,1536]{1,0:T(8,128)(2,1)} fusion(bf16[1152,512]{1,0:T(8,128)(2,1)S(1)} %bitcast.71, bf16[512,1536]{0,1:T(8,128)(2,1)} %all-gather.5.cloned.1.call-done), kind=kOutput, calls=%fused_computation.10 | convolution fusion | flops 1813708800 | bytes 6291456 | tf_op jit(solution)/shard_map/dot_general | solution.py:38
  147.6 9.5 %reshape.202 = bf16[2,2,2,6,2,12,3,8,64]{8,7,6,5,4,3,2,1,0:T(8,128)(2,1)} reshape(bf16[1152,1536]{1,0:T(8,128)(2,1)} %convolution_convert_fusion.1) | data formatting | bytes 7077888 | tf_op jit(solution)/shard_map/reshape | solution.py:41
  157.1 4.9 %copy.84 = bf16[2,2,2,6,2,12,3,8,64]{8,7,5,3,1,6,4,2,0:T(8,128)(2,1)S(1)} copy(bf16[2,2,2,6,2,12,3,8,64]{8,7,6,5,4,3,2,1,0:T(8,128)(2,1)} %reshape.202) | data formatting | bytes 7077888 | tf_op jit(solution)/shard_map/reshape | solution.py:41
  180.4 5.0 %fusion.63 = (f32[8,8,144]{2,1,0:T(8,128)S(1)}, f32[8,8,144,144]{2,3,1,0:T(8,128)}) fusion(f32[8,8,144,144]{2,3,1,0:T(8,128)S(1)} %fusion.31, pred[8,144,144]{1,2,0:T(8,128)(4,1)S(1)} %copy-done.4), kind=kOutput, calls=%fused_computation.106 | output fusion | flops 7962767 | bytes 10819584 | tf_op jit(solution)/shard_map/sub | solution.py:62
  185.4 5.9 %fusion.37 = bf16[8,8,144,64]{2,3,1,0:T(8,128)(2,1)} fusion(f32[8,8,144,144]{2,3,1,0:T(8,128)} %get-tuple-element.14, f32[8,8,144]{2,1,0:T(8,128)S(1)} %get-tuple-element.13, bf16[8,1,8,144,64]{3,4,2,0,1:T(8,128)(2,1)S(1)} %copy-done.1), kind=kOutput, calls=%fused_computation.54 | convolution fusion | flops 173113344 | bytes 7704576 | tf_op jit(solution)/shard_map/nhqk,nhkd->nhqd/dot_general | solution.py:63
  203.5 12.2 %collective-permute-done.2 = bf16[4,12,6,512]{3,2,1,0:T(8,128)(2,1)S(1)} collective-permute-done((bf16[4,12,6,512]{3,2,1,0:T(8,128)(2,1)S(1)}, bf16[4,12,6,512]{3,2,1,0:T(8,128)(2,1)S(1)}, u32[]{:S(2)}, u32[]{:S(2)}) %collective-permute-start.2) | collective-permute-done | bytes 294944 | tf_op jit(solution)/shard_map/ppermute | solution.py:18
  216.6 6.0 %collective-permute-start.3 = (bf16[4,3,24,512]{3,2,1,0:T(8,128)(2,1)S(1)}, bf16[4,3,24,512]{3,2,1,0:T(8,128)(2,1)}, u32[]{:S(2)}, u32[]{:S(2)}) collective-permute-start(bf16[4,3,24,512]{3,2,1,0:T(8,128)(2,1)S(1)} %pad_maximum_fusion.7), channel_id=1, source_target_pairs={{0,16},{16,32},{32,48},{48,64},{64,80},{80,96},{96,112},{112,128},... | collective-permute-start | bytes 884744 | tf_op jit(solution)/shard_map/ppermute | solution.py:18
  222.6 17.8 %all_gather.44 = bf16[512,96]{1,0:T(8,128)(2,1)S(1)} all-gather(bf16[32,96]{1,0:T(8,128)(2,1)S(1)} %copy-done.6), channel_id=1, replica_groups=mesh['lat'=16,'lon'=16] {'lat'}, dimensions={0}, use_global_device_ids=true | all-gather | bytes 104448 | tf_op jit(solution)/shard_map/all_gather | solution.py:90
  241.2 16.9 %all_gather.46 = bf16[512,32]{1,0:T(8,128)(2,1)S(1)} all-gather(bf16[32,32]{1,0:T(8,128)(2,1)S(1)} %copy-done.7), channel_id=1, replica_groups=mesh['lat'=16,'lon'=16] {'lat'}, dimensions={0}, use_global_device_ids=true | all-gather | bytes 34816 | tf_op jit(solution)/shard_map/all_gather | solution.py:91
  258.2 37.7 %all_gather.47 = bf16[512,512]{0,1:T(8,128)(2,1)} all-gather(bf16[512,32]{0,1:T(8,128)(2,1)S(1)} %copy.108), channel_id=1, replica_groups=mesh['lat'=16,'lon'=16] {'lon'}, dimensions={1}, use_global_device_ids=true | all-gather | bytes 557056 | tf_op jit(solution)/shard_map/all_gather | solution.py:99
  303.1 22.3 %all-gather.9.cloned.1.call-done = bf16[1024,2048]{1,0:T(8,128)(2,1)} async-done(((bf16[1024,128]{1,0:T(8,128)(2,1)}), bf16[1024,2048]{1,0:T(8,128)(2,1)}) %all-gather.9.cloned.1.call-update) | async-done | bytes 4194320 | tf_op jit(solution)/shard_map/all_gather | solution.py:97
  325.3 7.5 %fusion.52 = f32[288,2048]{1,0:T(8,128)} fusion(bf16[1024,2048]{1,0:T(8,128)(2,1)} %all-gather.9.cloned.1.call-done, bf16[2048,1024]{0,1:T(8,128)(2,1)} %all-gather.7.cloned.1.call-done, bf16[288,512]{1,0:T(8,128)(2,1)S(1)} %concatenate.43, bf16[288,512]{1,0:T(8,128)(2,1)S(1)} %concatenate.42, bf16[288,512]{1,0:T(8,128)(2,1)S(1)} %concatenate.41, ...), kind=kOutput, calls=%fused_computation.77 | convolution fusion | flops 2423291904 | bytes 11938048 | tf_op jit(solution)/shard_map/dot_general | solution.py:134
  361.5 45.7 %all-gather.11.cloned.1.call-done = bf16[512,1536]{0,1:T(8,128)(2,1)} async-done(((bf16[512,96]{0,1:T(8,128)(2,1)}), bf16[512,1536]{0,1:T(8,128)(2,1)}) %all-gather.11.cloned.1.call-update) | async-done | bytes 1572880 | tf_op jit(solution)/shard_map/all_gather | solution.py:98
  407.2 5.3 %convolution_convert_fusion = bf16[1152,1536]{1,0:T(8,128)(2,1)} fusion(bf16[1152,512]{1,0:T(8,128)(2,1)S(1)} %bitcast.70, bf16[512,1536]{0,1:T(8,128)(2,1)} %all-gather.11.cloned.1.call-done), kind=kOutput, calls=%fused_computation.9 | convolution fusion | flops 1813708800 | bytes 6291456 | tf_op jit(solution)/shard_map/dot_general | solution.py:38
  412.5 9.5 %reshape.210 = bf16[2,2,2,6,2,12,3,8,64]{8,7,6,5,4,3,2,1,0:T(8,128)(2,1)} reshape(bf16[1152,1536]{1,0:T(8,128)(2,1)} %convolution_convert_fusion) | data formatting | bytes 7077888 | tf_op jit(solution)/shard_map/reshape | solution.py:41
  422.0 4.9 %copy.101 = bf16[2,2,2,6,2,12,3,8,64]{8,7,5,3,1,6,4,2,0:T(8,128)(2,1)S(1)} copy(bf16[2,2,2,6,2,12,3,8,64]{8,7,6,5,4,3,2,1,0:T(8,128)(2,1)} %reshape.210) | data formatting | bytes 7077888 | tf_op jit(solution)/shard_map/reshape | solution.py:41
  442.3 5.6 %fusion.64 = (f32[8,8,144]{2,1,0:T(8,128)}, f32[8,8,144,144]{2,3,1,0:T(8,128)}) fusion(f32[8,8,144,144]{2,3,1,0:T(8,128)S(1)} %fusion.27), kind=kOutput, calls=%fused_computation.107 | output fusion | flops 5308559 | bytes 10653696 | tf_op jit(solution)/shard_map/sub | solution.py:62
  450.6 6.5 %fusion.34 = bf16[8,8,144,64]{2,3,1,0:T(8,128)(2,1)} fusion(f32[8,8,144,144]{2,3,1,0:T(8,128)} %get-tuple-element.16, f32[8,8,144]{2,1,0:T(8,128)} %get-tuple-element.15, bf16[8,1,8,144,64]{3,4,2,0,1:T(8,128)(2,1)} %copy.114), kind=kOutput, calls=%fused_computation.53 | convolution fusion | flops 173113344 | bytes 7704576 | tf_op jit(solution)/shard_map/nhqk,nhkd->nhqd/dot_general | solution.py:63
  (116 shorter events, 103.6 us)
Async XLA Ops:
  6.5 61.3 %copy-start = (bf16[4,12,24,512]{3,2,1,0:T(8,128)(2,1)S(1)}, bf16[4,12,24,512]{3,2,1,0:T(8,128)(2,1)}, u32[]{:S(2)}) copy-start(bf16[4,12,24,512]{3,2,1,0:T(8,128)(2,1)} %param.11) | copy-start | bytes 3538948
  6.5 62.1 %copy-start.9 = (f32[512]{0:T(512)S(1)}, f32[512]{0:T(512)}, u32[]{:S(2)}) copy-start(f32[512]{0:T(512)} %param.12) | copy-start | bytes 6148
  6.5 135.9 %all-gather.5.cloned.1.call-start = ((), (), s32[]{:S(2)}) async-start(), calls=%async_computation | async-start | bytes 1671168 | tf_op jit(solution)/shard_map/all_gather | solution.py:94
  29.1 274.0 %all-gather.7.cloned.1.call-start = ((), (), s32[]{:S(2)}) async-start(), calls=%async_computation.1 | async-start | bytes 4456448 | tf_op jit(solution)/shard_map/all_gather | solution.py:96
  47.7 277.6 %all-gather.9.cloned.1.call-start = ((), (), s32[]{:S(2)}) async-start(), calls=%async_computation.2 | async-start | bytes 4456448 | tf_op jit(solution)/shard_map/all_gather | solution.py:97
  67.8 339.5 %all-gather.11.cloned.1.call-start = ((), (), s32[]{:S(2)}) async-start(), calls=%async_computation.3 | async-start | bytes 1671168 | tf_op jit(solution)/shard_map/all_gather | solution.py:98
  69.1 2.7 copy-start.5
  69.9 63.2 %collective-permute-start = (bf16[4,3,24,512]{3,2,1,0:T(8,128)(2,1)}, bf16[4,3,24,512]{3,2,1,0:T(8,128)(2,1)S(1)}, u32[]{:S(2)}, u32[]{:S(2)}) collective-permute-start(bf16[4,3,24,512]{3,2,1,0:T(8,128)(2,1)} %pad_maximum_fusion.8), channel_id=1, source_target_pairs={{0,240},{16,0},{32,16},{48,32},{64,48},{80,64},{96,80},{112,96},{1... | collective-permute-start | bytes 884744 | tf_op jit(solution)/shard_map/ppermute | solution.py:18
  133.1 9.0 %collective-permute-start.1 = (bf16[4,12,6,512]{3,2,1,0:T(8,128)(2,1)S(1)}, bf16[4,12,6,512]{3,2,1,0:T(8,128)(2,1)S(1)}, u32[]{:S(2)}, u32[]{:S(2)}) collective-permute-start(bf16[4,12,6,512]{3,2,1,0:T(8,128)(2,1)S(1)} %pad_maximum_fusion.6), channel_id=1, source_target_pairs={{0,15},{1,0},{2,1},{3,2},{4,3},{5,4},{6,5},{7,6},{8,7},{9,8},{10,9... | collective-permute-start | bytes 884744 | tf_op jit(solution)/shard_map/ppermute | solution.py:18
  176.6 3.7 copy-start.4
  180.4 5.0 %copy-start.1 = (bf16[8,1,8,144,64]{3,4,2,0,1:T(8,128)(2,1)S(1)}, bf16[8,1,8,144,64]{3,4,2,0,1:T(8,128)(2,1)}, u32[]{:S(2)}) copy-start(bf16[8,1,8,144,64]{3,4,2,0,1:T(8,128)(2,1)} %copy.111) | copy-start | bytes 3538948
  199.7 22.8 %copy-start.6 = (bf16[32,96]{1,0:T(8,128)(2,1)S(1)}, bf16[32,96]{1,0:T(8,128)(2,1)}, u32[]{:S(2)}) copy-start(bf16[32,96]{1,0:T(8,128)(2,1)} %param.20) | copy-start | bytes 18436
  201.6 39.5 %copy-start.7 = (bf16[32,32]{1,0:T(8,128)(2,1)S(1)}, bf16[32,32]{1,0:T(8,128)(2,1)}, u32[]{:S(2)}) copy-start(bf16[32,32]{1,0:T(8,128)(2,1)} %param.21) | copy-start | bytes 6148
  201.7 14.0 %collective-permute-start.2 = (bf16[4,12,6,512]{3,2,1,0:T(8,128)(2,1)S(1)}, bf16[4,12,6,512]{3,2,1,0:T(8,128)(2,1)S(1)}, u32[]{:S(2)}, u32[]{:S(2)}) collective-permute-start(bf16[4,12,6,512]{3,2,1,0:T(8,128)(2,1)S(1)} %slice.101), channel_id=1, source_target_pairs={{0,1},{1,2},{2,3},{3,4},{4,5},{5,6},{6,7},{7,8},{8,9},{9,10},{10,1... | collective-permute-start | bytes 884744 | tf_op jit(solution)/shard_map/ppermute | solution.py:18
  215.7 0.7 copy-start.2
  216.6 79.3 %collective-permute-start.3 = (bf16[4,3,24,512]{3,2,1,0:T(8,128)(2,1)S(1)}, bf16[4,3,24,512]{3,2,1,0:T(8,128)(2,1)}, u32[]{:S(2)}, u32[]{:S(2)}) collective-permute-start(bf16[4,3,24,512]{3,2,1,0:T(8,128)(2,1)S(1)} %pad_maximum_fusion.7), channel_id=1, source_target_pairs={{0,16},{16,32},{32,48},{48,64},{64,80},{80,96},{96,112},{112,128},... | collective-permute-start | bytes 884744 | tf_op jit(solution)/shard_map/ppermute | solution.py:18
  301.9 23.5 %copy-start.11 = (f32[2048]{0:T(1024)S(1)}, f32[2048]{0:T(1024)}, u32[]{:S(2)}) copy-start(f32[2048]{0:T(1024)} %param.15) | copy-start | bytes 24580
  351.5 6.6 %copy-start.8 = (f32[512]{0:T(512)S(1)}, f32[512]{0:T(512)}, u32[]{:S(2)}) copy-start(f32[512]{0:T(512)} %param.18) | copy-start | bytes 6148
  358.1 2.9 copy-start.10
  462.1 3.5 copy-start.3
Sparse Core Ops, SparseCore 0:
  29.2 79.2 all-gather.4
  111.1 100.1 all-gather.6
  213.8 111.5 all-gather.8
  327.8 79.3 all-gather.10
where the time goes:
time: 482 us; the launch traced here: 475 us
  blocking collectives  194 us (40%)
  local copies, waits for them, and re-layouts  102 us (21%)
  waiting for transfers between devices  87.6 us (18%)
  matrix products  40.5 us (8%)
  other arithmetic  28.6 us (6%)
  between operations  13.8 us (3%)
  starting transfers between devices  8.59 us (2%)
    all_gather x1, waiting for transfers between devices, shards(): lax.all_gather(part_e, 'lon', axis=1, tiled=True)  45.7 us
    all_gather x1, blocking collectives, shards(): lax.all_gather(part_b, 'lon', axis=1, tiled=True)  42.7 us
    all_gather x1, blocking collectives, shards(): lax.all_gather(part_f, 'lon', axis=1, tiled=True)  37.7 us
    reshape x4, local copies, waits for them, and re-layouts, attend(): projected.reshape(levels // WL, WL, rows // WA, WA, cols // WO, WO, 3, HE...  28.9 us
    unnamed x30, local copies, waits for them, and re-layouts  24.4 us
    all_gather x1, waiting for transfers between devices, shards(): lax.all_gather(part_d, 'lon', axis=1, tiled=True)  22.3 us
    all_gather x1, blocking collectives, shards(): lax.all_gather(enc_qkv, 'lat', axis=0, tiled=True)  21.7 us
    all_gather x1, blocking collectives, shards(): lax.all_gather(split_weight, 'lat', axis=0, tiled=True)  19.9 us
  transfers between devices with their start and end apart: 8, of which 4 were waited for; matrix products, arithmetic and copies ran while one was open for 23% of the time, Pallas kernels for 0%

commit v1 on v0

v1 whole, which is shorter than its diff:
```python
import functools

import jax
import jax.numpy as jnp
import numpy as np
from jax import lax
from jax.experimental import pallas as pl
from jax.experimental.pallas import tpu as pltpu
from jax.sharding import PartitionSpec as P

HEADS = 8
WL = 2
WA = 6
WO = 12
WIN = WL * WA * WO
C = 512
HD = C // HEADS
LEV = 4
ROWS = 12
COLS = 24
BAND = 2 * WIN
VMEM_LIMIT = 48 * 1024 * 1024

eps = 1e-05
SCALE = float(HD**-0.5 * np.log2(np.e))


def window_from_natural():
    out = np.zeros((BAND, BAND), np.float32)
    for l in range(WL):
        for r in range(WA):
            for c in range(COLS):
                out[(c // WO) * WIN + (l * WA + r) * WO + c % WO, (l * WA + r) * COLS + c] = 1
    return out


def merged_from_natural():
    out = np.zeros((BAND, BAND), np.float32)
    quarter = BAND // 4
    for l in range(WL):
        for r in range(WA):
            for c in range(COLS):
                part = (c % 2) * 2 + r % 2
                out[part * quarter + (l * (WA // 2) + r // 2) * (COLS // 2) + c // 2, (l * WA + r) * COLS + c] = 1
    return out


MERGE_PART = [0, 2, 1, 3]


def normed(values, gain):
    center = jnp.mean(values, axis=-1, keepdims=True)
    centred = values - center
    spread = jnp.mean(centred * centred, axis=-1, keepdims=True)
    return centred * lax.rsqrt(spread + eps) * gain


def dot(a, b):
    return jnp.dot(a, b, preferred_element_type=jnp.float32)


def window_attention(qkv_ref, mixed_ref, first, same):
    lane = lax.broadcasted_iota(jnp.int32, (WIN, 2 * HD), 1)
    low = lane < HD
    rows = pl.ds(first, WIN)
    for pair in range(HEADS // 2):
        at = pair * 2 * HD
        q = qkv_ref[rows, at : at + 2 * HD]
        k = qkv_ref[rows, C + at : C + at + 2 * HD]
        v = qkv_ref[rows, 2 * C + at : 2 * C + at + 2 * HD]
        vo = jnp.concatenate([v, jnp.ones_like(v)], axis=1)
        halves = []
        for half in range(2):
            own = low if half == 0 else ~low
            scores = lax.dot_general(
                jnp.where(own, q, jnp.zeros_like(q)), k, (((1,), (1,)), ((), ())), preferred_element_type=jnp.float32
            )
            scores = scores * SCALE
            if same is not None:
                scores = jnp.where(same, scores, -jnp.inf)
            top = jnp.max(scores, axis=-1, keepdims=True)
            weights = jnp.exp2(scores - top).astype(jnp.bfloat16)
            summed = dot(weights, vo)
            halves.append(summed[:, : 2 * HD] / summed[:, 2 * HD :])
        mixed_ref[rows, at : at + 2 * HD] = jnp.where(low, halves[0], halves[1]).astype(jnp.bfloat16)


def encode_kernel(last_ref, x_ref, gain_ref, w_ref, to_win_ref, from_win_ref, out_ref, qkv_ref, mixed_ref):
    step = pl.program_id(0)
    pair, band = step // 2, step % 2
    upper, lower = 2 * pair + 1, (2 * pair + 2) % LEV
    x = jnp.concatenate([x_ref[upper, band], x_ref[lower, band]], axis=0).astype(jnp.float32)
    h = normed(x, gain_ref[...]).astype(jnp.bfloat16)
    h = dot(to_win_ref[...], h).astype(jnp.bfloat16)
    for third in range(3):
        qkv_ref[:, third * C : (third + 1) * C] = dot(h, w_ref[:, third].reshape(C, C)).astype(jnp.bfloat16)
    by_level = (pair == 1).astype(jnp.int32)
    by_row = jnp.where(band == 1, last_ref[0], 0)

    def label(dim):
        index = lax.broadcasted_iota(jnp.int32, (WIN, WIN), dim)
        second = (index >= WIN // 2).astype(jnp.int32)
        inner = index - second * (WIN // 2)
        return by_level * 3 * second + by_row * (inner >= WIN // 4).astype(jnp.int32)

    same = label(0) == label(1)
    for window in range(2):
        window_attention(qkv_ref, mixed_ref, window * WIN, same)
    y = dot(mixed_ref[...], w_ref[:, 3].reshape(C, C)).astype(jnp.bfloat16)
    y = dot(from_win_ref[...], y)
    out = (x + y).astype(jnp.bfloat16)
    out_ref[upper, band] = out[:WIN]
    out_ref[lower, band] = out[WIN:]


def merge_split_kernel(x_ref, mgain_ref, sgain_ref, wm_ref, ws_ref, to_merged_ref, out_ref, quads_ref, skip_ref, middle_ref):
    step = pl.program_id(0)
    quarter = BAND // 4

    @pl.when(step == 0)
    def _():
        for pair in range(2):
            for band in range(2):
                x = jnp.concatenate([x_ref[2 * pair, band], x_ref[2 * pair + 1, band]], axis=0)
                m = dot(to_merged_ref[...], x)
                at = (pair * 2 + band) * quarter
                for part in range(4):
                    skip_ref[part, at : at + quarter] = m[part * quarter : (part + 1) * quarter]
        parts = [skip_ref[part] for part in range(4)]
        center = sum(jnp.sum(p, axis=-1, keepdims=True) for p in parts) * (1 / (4 * C))
        spread = sum(jnp.sum((p - center) * (p - center), axis=-1, keepdims=True) for p in parts) * (1 / (4 * C))
        scale = lax.rsqrt(spread + eps)
        for part in range(4):
            quads_ref[:, part * C : (part + 1) * C] = (
                (parts[part] - center) * scale * mgain_ref[:, part * C : (part + 1) * C]
            ).astype(jnp.bfloat16)

    @pl.when(step < 4)
    def _():
        width = wm_ref.shape[-1]
        middle_ref[step] = dot(quads_ref[...], wm_ref[:, 0].reshape(4 * C, width)).astype(jnp.bfloat16)

    @pl.when(step >= 4)
    def _():
        part = step - 4
        width = middle_ref.shape[-1]
        w = ws_ref[:, 0].reshape(2 * C, C)
        total = dot(middle_ref[0], w[:width])
        for chunk in range(1, 4):
            total += dot(middle_ref[chunk], w[chunk * width : (chunk + 1) * width])
        kept = (part % 2) * 2 + part // 2
        joined = (normed(total, sgain_ref[...]) + skip_ref[kept]).astype(jnp.bfloat16)
        out_ref[0] = joined


def decode_kernel(x_ref, gain_ref, w_ref, to_win_ref, from_win_ref, out_ref, qkv_ref, mixed_ref):
    step = pl.program_id(0)
    pair, band = step // 2, step % 2
    quarter = BAND // 4
    x = jnp.concatenate([x_ref[part, step].astype(jnp.float32) for part in range(4)], axis=0).astype(jnp.bfloat16)
    x = dot(to_win_ref[...], x)
    h = normed(x, gain_ref[...]).astype(jnp.bfloat16)
    for third in range(3):
        qkv_ref[:, third * C : (third + 1) * C] = dot(h, w_ref[:, third].reshape(C, C)).astype(jnp.bfloat16)
    for window in range(2):
        window_attention(qkv_ref, mixed_ref, window * WIN, None)
    y = dot(mixed_ref[...], w_ref[:, 3].reshape(C, C)).astype(jnp.bfloat16)
    out = (x + y.astype(jnp.float32)).astype(jnp.bfloat16)
    out = dot(from_win_ref[...], out).astype(jnp.bfloat16)
    out_ref[2 * pair, band] = out[:WIN]
    out_ref[2 * pair + 1, band] = out[WIN:]


def whole(shape):
    return pl.BlockSpec(shape, lambda i: (0,) * len(shape))


PARAMS = pltpu.CompilerParams(vmem_limit_bytes=VMEM_LIMIT)


def encode(framed, gain, weights, last):
    to_win = window_from_natural()
    shape = (LEV, 2, WIN, C)
    return pl.pallas_call(
        encode_kernel,
        grid=(4,),
        in_specs=[
            pl.BlockSpec(memory_space=pltpu.SMEM),
            whole(shape),
            whole((1, C)),
            whole((16, 4, 32, C)),
            whole((BAND, BAND)),
            whole((BAND, BAND)),
        ],
        out_specs=whole(shape),
        out_shape=jax.ShapeDtypeStruct(shape, jnp.bfloat16),
        scratch_shapes=[pltpu.VMEM((BAND, 3 * C), jnp.bfloat16), pltpu.VMEM((BAND, C), jnp.bfloat16)],
        compiler_params=PARAMS,
        name="encode",
    )(last, framed, gain.reshape(1, C), weights, jnp.asarray(to_win, jnp.bfloat16), jnp.asarray(to_win.T, jnp.bfloat16))


def merge_split(encoded, mgain, sgain, weights):
    to_merged = merged_from_natural()
    tokens = LEV * ROWS * COLS // 4
    return pl.pallas_call(
        merge_split_kernel,
        grid=(8,),
        in_specs=[
            whole((LEV, 2, WIN, C)),
            whole((1, 4 * C)),
            whole((1, C)),
            pl.BlockSpec((16, 1, 128, 256), lambda i: (0, jnp.minimum(i, 3) // 2, 0, jnp.minimum(i, 3) % 2)),
            pl.BlockSpec((16, 1, 64, C), lambda i: (0, jnp.maximum(i, 4), 0, 0)),
            whole((BAND, BAND)),
        ],
        out_specs=pl.BlockSpec(
            (1, tokens, C),
            lambda i: ((jnp.maximum(i - 4, 0) % 2) * 2 + jnp.maximum(i - 4, 0) // 2, 0, 0),
        ),
        out_shape=jax.ShapeDtypeStruct((4, tokens, C), jnp.bfloat16),
        scratch_shapes=[
            pltpu.VMEM((tokens, 4 * C), jnp.bfloat16),
            pltpu.VMEM((4, tokens, C), jnp.float32),
            pltpu.VMEM((4, tokens, 256), jnp.bfloat16),
        ],
        compiler_params=PARAMS,
        name="merge_split",
    )(
        encoded,
        mgain.reshape(1, 4 * C),
        sgain.reshape(1, C),
        weights.reshape(16, 4, 128, C),
        weights.reshape(16, 8, 64, C),
        jnp.asarray(to_merged, jnp.bfloat16),
    )


def decode(joined, gain, weights):
    to_win = window_from_natural()
    from_merged = to_win @ merged_from_natural().T
    shape = (LEV, 2, WIN, C)
    return pl.pallas_call(
        decode_kernel,
        grid=(4,),
        in_specs=[
            whole((4, 4, BAND // 4, C)),
            whole((1, C)),
            whole((16, 4, 32, C)),
            whole((BAND, BAND)),
            whole((BAND, BAND)),
        ],
        out_specs=whole(shape),
        out_shape=jax.ShapeDtypeStruct(shape, jnp.bfloat16),
        scratch_shapes=[pltpu.VMEM((BAND, 3 * C), jnp.bfloat16), pltpu.VMEM((BAND, C), jnp.bfloat16)],
        compiler_params=PARAMS,
        name="decode",
    )(
        joined.reshape(4, 4, BAND // 4, C),
        gain.reshape(1, C),
        weights,
        jnp.asarray(from_merged, jnp.bfloat16),
        jnp.asarray(to_win.T, jnp.bfloat16),
    )


def passed_along(value, axis, steps):
    if isinstance(axis, str):
        count = lax.axis_size(axis)
        pairs = [(source, (source + steps) % count) for source in range(count)]
    else:
        rows, cols = (lax.axis_size(name) for name in axis)
        pairs = [
            (i * cols + j, ((i + steps) % rows) * cols + (j + steps) % cols) for i in range(rows) for j in range(cols)
        ]
    return lax.ppermute(value, axis, pairs)


def gathered_cols(block):
    return lax.all_to_all(jnp.broadcast_to(block[None], (16,) + block.shape), "lon", 0, 0, tiled=True)


def pack_attention(qkv, proj):
    return jnp.concatenate([qkv, proj], axis=1)


def unpack_attention(blocks):
    qkv = blocks[:, :, :96].transpose(1, 0, 2).reshape(32, 3, C).transpose(1, 0, 2)
    proj = blocks[:, :, 96:].transpose(1, 0, 2).reshape(1, 32, C)
    return jnp.concatenate([qkv, proj], axis=0)


def shards(
    tokens,
    enc_gain,
    enc_qkv,
    enc_proj,
    merge_gain,
    merge_weight,
    split_weight,
    split_gain,
    dec_gain,
    dec_qkv,
    dec_proj,
):
    half_lat = WA // 2
    half_lon = WO // 2
    packed = jnp.concatenate(
        [
            pack_attention(enc_qkv, enc_proj),
            pack_attention(dec_qkv, dec_proj),
            jnp.concatenate([merge_weight[:64], merge_weight[64:]], axis=1),
            split_weight,
        ],
        axis=0,
    )
    blocks = gathered_cols(packed)
    enc_rows = unpack_attention(blocks[:, :32])
    dec_rows = unpack_attention(blocks[:, 32:64])
    merge_rows = (
        blocks[:, 64:128].reshape(16, 64, 2, 64).transpose(2, 1, 0, 3).reshape(128, 2, C).transpose(1, 0, 2)
    )
    split_rows = blocks[:, 128:].transpose(1, 0, 2).reshape(64, 4, C).transpose(1, 0, 2)
    enc_w = lax.all_gather(enc_rows, "lat", axis=0, tiled=False)
    ms_rows = jnp.concatenate([merge_rows.reshape(256, C), split_rows.reshape(256, C)], axis=0)
    ms_w = lax.all_gather(ms_rows, "lat", axis=0, tiled=False)
    dec_w = lax.all_gather(dec_rows, "lat", axis=0, tiled=False)

    below = passed_along(tokens[:, :half_lat, half_lon:], "lat", -1)
    beyond = passed_along(tokens[:, half_lat:, :half_lon], "lon", -1)
    corner = passed_along(tokens[:, :half_lat, :half_lon], ("lat", "lon"), -1)
    framed = jnp.concatenate(
        [
            jnp.concatenate([tokens[:, half_lat:, half_lon:], beyond], axis=2),
            jnp.concatenate([below, corner], axis=2),
        ],
        axis=1,
    )
    last = (lax.axis_index("lat") == lax.axis_size("lat") - 1).astype(jnp.int32).reshape(1)
    moved = encode(framed.reshape(LEV, 2, WIN, C), enc_gain, enc_w, last).reshape(LEV, ROWS, COLS, C)
    cut_r, cut_c = ROWS - half_lat, COLS - half_lon
    above = passed_along(moved[:, cut_r:, :cut_c], "lat", 1)
    left = passed_along(moved[:, :cut_r, cut_c:], "lon", 1)
    corner = passed_along(moved[:, cut_r:, cut_c:], ("lat", "lon"), 1)
    encoded = jnp.concatenate(
        [
            jnp.concatenate([corner, above], axis=2),
            jnp.concatenate([left, moved[:, :cut_r, :cut_c]], axis=2),
        ],
        axis=1,
    )
    joined = merge_split(encoded.reshape(LEV, 2, WIN, C), merge_gain, split_gain, ms_w)
    return decode(joined, dec_gain, dec_w).reshape(LEV, ROWS, COLS, C)


def solution(mesh):
    return jax.shard_map(
        shards,
        mesh=mesh,
        in_specs=(
            P(None, "lat", "lon", None),
            P(),
            P("lat", "lon"),
            P("lat", "lon"),
            P(),
            P("lat", "lon"),
            P("lat", "lon"),
            P(),
            P(),
            P("lat", "lon"),
            P("lat", "lon"),
        ),
        out_specs=P(None, "lat", "lon", None),
        check_vma=False,
    )
```

time: 482 us -> 204 us (0.42); the launches traced: 475 us -> 204 us
  blocking collectives: 194 us -> 35 us
  local copies, waits for them, and re-layouts: 102 us -> 9.28 us
  matrix products: 40.5 us -> 0 us
  Pallas kernels: 0 us -> 29.9 us
  other arithmetic: 28.6 us -> 3.8 us
  waiting for transfers between devices: 87.6 us -> 102 us
    all_gather x8 -> x0, blocking collectives: 194 us -> none  [the longest x1 42.7 us: shards(): lax.all_gather(part_b, 'lon', axis=1, tiled=True)]
    reshape x8, local copies, waits for them, and re-layouts: 43.2 us -> 1.57 us  [the longest x3 0.86 us: shards(): blocks[:, 64:128].reshape(16, 64, 2, 64).transpose(2, 1, 0, 3)]
    dot_general x9 -> x0, matrix products: 40.5 us -> none  [the longest x2 12.4 us: attend(): jnp.einsum('nhqk,nhkd->nhqd', weights, projected[:, 2], preferred_element...]
    all_to_all x0 -> x1, blocking collectives: none -> 35 us  [gathered_cols(): lax.all_to_all(jnp.broadcast_to(block[None], (16,) + block.shape), 'lon',...]
    pallas_call x0 -> x3, Pallas kernels: none -> 29.9 us  [the longest x1 10.7 us: decode(): pl.pallas_call(decode_kernel, grid=(4,), in_specs=[whole((4, 4, BAND // 4...]
    unnamed x30 -> x24, local copies, waits for them, and re-layouts: 24.4 us -> 3.41 us
    sub x2 -> x0, other arithmetic: 10.6 us -> none  [attend(): weights = jax.nn.softmax(scores, axis=-1).astype(jnp.bfloat16)]
    reduce_sum x8 -> x0, other arithmetic: 10 us -> none  [the longest x4 5.4 us: layer_norm(): spread = jnp.mean(centred * centred, axis=-1, keepdims=True)]
  transfers between devices with their start and end apart: 8 -> 9, of which waited for: 4 -> 7; matrix products, arithmetic and copies ran while one was open for 23% -> 3% of each run, Pallas kernels for 0% -> 9%
where the time goes in v1:
time: 204 us
  waiting for transfers between devices  102 us (50%)
  blocking collectives  35 us (17%)
  Pallas kernels  29.9 us (15%)
  between operations  13.4 us (7%)
  starting transfers between devices  10.2 us (5%)
  local copies, waits for them, and re-layouts  9.28 us (5%)
  other arithmetic  3.8 us (2%)
    all_to_all x1, blocking collectives, gathered_cols(): lax.all_to_all(jnp.broadcast_to(block[None], (16,) + block.shape), 'lon',...  35 us
    all_gather x1, waiting for transfers between devices, shards(): ms_w = lax.all_gather(ms_rows, 'lat', axis=0, tiled=False)  28.6 us
    ppermute x6, waiting for transfers between devices, passed_along(): return lax.ppermute(value, axis, pairs)  27.1 us
    all_gather x1, waiting for transfers between devices, shards(): dec_w = lax.all_gather(dec_rows, 'lat', axis=0, tiled=False)  26.2 us
    all_gather x1, waiting for transfers between devices, shards(): enc_w = lax.all_gather(enc_rows, 'lat', axis=0, tiled=False)  20.1 us
    pallas_call x1, Pallas kernels, decode(): pl.pallas_call(decode_kernel, grid=(4,), in_specs=[whole((4, 4, BAND // 4...  10.7 us
    ppermute x6, starting transfers between devices, passed_along(): return lax.ppermute(value, axis, pairs)  10.1 us
    pallas_call x1, Pallas kernels, merge_split(): pl.pallas_call(merge_split_kernel, grid=(8,), in_specs=[whole((LEV, 2, WI...  9.61 us
  transfers between devices with their start and end apart: 9, of which 7 were waited for; matrix products, arithmetic and copies ran while one was open for 3% of the time, Pallas kernels for 9%

profile of v1, /device:TPU:1, one launch (start us, length us, event | category | flops | bytes accessed | tf_op | source)
XLA Modules:
  0.0 203.6 jit_solution(7018963521020664858)
XLA Ops:
  6.5 0.9 fusion.1
  7.6 0.9 pad_maximum_fusion.3
  8.6 35.0 %all_to_all.5 = bf16[16,192,128]{2,1,0:T(8,128)(2,1)S(1)} all-to-all(bf16[16,192,128]{2,1,0:T(8,128)(2,1)S(1)} %broadcast_in_dim.2), channel_id=1, replica_groups=mesh['lat'=16,'lon'=16] {'lon'}, dimensions={0} | all-to-all | bytes 1572864 | tf_op jit(solution)/shard_map/all_to_all | solution.py:280
  44.4 0.7 copy.52
  46.5 0.8 pad_maximum_fusion
  47.9 0.7 copy.60
  48.9 2.4 %collective-permute-start.1 = (bf16[4,3,18,512]{3,2,1,0:T(8,128)(2,1)S(1)}, bf16[4,3,18,512]{3,2,1,0:T(8,128)(2,1)}, u32[]{:S(2)}, u32[]{:S(2)}) collective-permute-start(bf16[4,3,18,512]{3,2,1,0:T(8,128)(2,1)S(1)} %slice.56), channel_id=1, source_target_pairs={{0,240},{16,0},{32,16},{48,32},{64,48},{80,64},{96,80},{112,96},{1... | collective-permute-start | bytes 663560 | tf_op jit(solution)/shard_map/ppermute | solution.py:276
  51.3 0.6 slice.57
  51.9 3.6 %collective-permute-start.2 = (bf16[4,3,6,512]{3,2,1,0:T(8,128)(2,1)}, bf16[4,3,6,512]{3,2,1,0:T(8,128)(2,1)}, u32[]{:S(2)}, u32[]{:S(2)}) collective-permute-start(bf16[4,3,6,512]{3,2,1,0:T(8,128)(2,1)} %slice.57), channel_id=1, source_target_pairs={{0,255},{1,240},{2,241},{3,242},{4,243},{5,244},{6,245},{7,246},{8... | collective-permute-start | bytes 221192 | tf_op jit(solution)/shard_map/ppermute | solution.py:276
  55.9 3.0 %collective-permute-done.2 = bf16[4,3,6,512]{3,2,1,0:T(8,128)(2,1)} collective-permute-done((bf16[4,3,6,512]{3,2,1,0:T(8,128)(2,1)}, bf16[4,3,6,512]{3,2,1,0:T(8,128)(2,1)}, u32[]{:S(2)}, u32[]{:S(2)}) %collective-permute-start.2) | collective-permute-done | bytes 73760 | tf_op jit(solution)/shard_map/ppermute | solution.py:276
  58.9 4.7 %collective-permute-done.1 = bf16[4,3,18,512]{3,2,1,0:T(8,128)(2,1)} collective-permute-done((bf16[4,3,18,512]{3,2,1,0:T(8,128)(2,1)S(1)}, bf16[4,3,18,512]{3,2,1,0:T(8,128)(2,1)}, u32[]{:S(2)}, u32[]{:S(2)}) %collective-permute-start.1) | collective-permute-done | bytes 221216 | tf_op jit(solution)/shard_map/ppermute | solution.py:276
  63.6 1.2 maximum_maximum_fusion
  64.9 20.1 %all-gather.7.cloned.1.call-done = bf16[64,32,512]{2,1,0:T(8,128)(2,1)} async-done(((bf16[4,32,512]{2,1,0:T(8,128)(2,1)}), bf16[64,32,512]{2,1,0:T(8,128)(2,1)}) %all-gather.7.cloned.1.call-update) | async-done | bytes 2097168 | tf_op jit(solution)/shard_map/all_gather | solution.py:324
  85.0 1.6 copy-done
  86.6 9.6 %encode.1 = bf16[4,2,144,512]{3,2,1,0:T(8,128)(2,1)S(1)} custom-call(s32[1]{0:T(128)} %bitcast.last_ref, bf16[4,2,144,512]{3,2,1,0:T(8,128)(2,1)S(1)} %bitcast.41, f32[1,512]{1,0:T(1,128)S(1)} %bitcast.45, bf16[16,4,32,512]{3,2,1,0:T(8,128)(2,1)S(1)} %bitcast.42, bf16[288,288]{1,0:T(8,128)(2,1)S(1)} %copy-done.5, bf16[288,288]{1,0:T(8,128)(2,1)S(1)} %copy-done.2), custom_call_target="tpu_custom_call" | custom-call | tf_op jit(solution)/shard_map/encode/pallas_call | solution.py:184
  96.8 3.5 %collective-permute-start.3 = (bf16[4,3,6,512]{3,2,1,0:T(8,128)(2,1)S(1)}, bf16[4,3,6,512]{3,2,1,0:T(8,128)(2,1)S(1)}, u32[]{:S(2)}, u32[]{:S(2)}) collective-permute-start(bf16[4,3,6,512]{3,2,1,0:T(8,128)(2,1)S(1)} %slice.72), channel_id=1, source_target_pairs={{0,17},{1,18},{2,19},{3,20},{4,21},{5,22},{6,23},{7,24},{8,25},{9,... | collective-permute-start | bytes 221192 | tf_op jit(solution)/shard_map/ppermute | solution.py:276
  100.4 10.6 %collective-permute-done.3 = bf16[4,3,6,512]{3,2,1,0:T(8,128)(2,1)S(1)} collective-permute-done((bf16[4,3,6,512]{3,2,1,0:T(8,128)(2,1)S(1)}, bf16[4,3,6,512]{3,2,1,0:T(8,128)(2,1)S(1)}, u32[]{:S(2)}, u32[]{:S(2)}) %collective-permute-start.3) | collective-permute-done | bytes 73760 | tf_op jit(solution)/shard_map/ppermute | solution.py:276
  111.0 8.8 %collective-permute-done.5 = bf16[4,9,6,512]{3,2,1,0:T(8,128)(2,1)S(1)} collective-permute-done((bf16[4,9,6,512]{3,2,1,0:T(8,128)(2,1)S(1)}, bf16[4,9,6,512]{3,2,1,0:T(8,128)(2,1)S(1)}, u32[]{:S(2)}, u32[]{:S(2)}) %collective-permute-start.5) | collective-permute-done | bytes 221216 | tf_op jit(solution)/shard_map/ppermute | solution.py:276
  119.8 0.6 maximum_maximum_fusion.1
  120.4 28.6 %all-gather.9.cloned.1.call-done = bf16[8192,512]{1,0:T(8,128)(2,1)} async-done(((bf16[512,512]{1,0:T(8,128)(2,1)}), bf16[8192,512]{1,0:T(8,128)(2,1)}) %all-gather.9.cloned.1.call-update) | async-done | bytes 8388624 | tf_op jit(solution)/shard_map/all_gather | solution.py:326
  148.9 9.6 %merge_split.1 = bf16[4,288,512]{2,1,0:T(8,128)(2,1)S(1)} custom-call(bf16[4,2,144,512]{3,2,1,0:T(8,128)(2,1)S(1)} %bitcast.39, f32[1,2048]{1,0:T(1,128)S(1)} %bitcast.44, f32[1,512]{1,0:T(1,128)S(1)} %bitcast.46, bf16[16,4,128,512]{3,2,1,0:T(8,128)(2,1)} %bitcast.48, bf16[16,8,64,512]{3,2,1,0:T(8,128)(2,1)} %bitcast.49, bf16[288,288]{1,0:T(8,128)(2,1)S(1)} %copy-done.3), custom_call_target="tpu_custom_call" | custom-call | tf_op jit(solution)/shard_map/merge_split/pallas_call | solution.py:206
  158.6 26.2 %all-gather.11.cloned.1.call-done = bf16[64,32,512]{2,1,0:T(8,128)(2,1)} async-done(((bf16[4,32,512]{2,1,0:T(8,128)(2,1)}), bf16[64,32,512]{2,1,0:T(8,128)(2,1)}) %all-gather.11.cloned.1.call-update) | async-done | bytes 2097168 | tf_op jit(solution)/shard_map/all_gather | solution.py:327
  184.8 1.6 copy-done.1
  186.4 10.7 %decode.1 = bf16[4,2,144,512]{3,2,1,0:T(8,128)(2,1)} custom-call(bf16[4,4,72,512]{3,2,1,0:T(8,128)(2,1)S(1)} %bitcast.40, f32[1,512]{1,0:T(1,128)S(1)} %bitcast.47, bf16[16,4,32,512]{3,2,1,0:T(8,128)(2,1)S(1)} %bitcast.43, bf16[288,288]{1,0:T(8,128)(2,1)S(1)} %copy-done.4, bf16[288,288]{1,0:T(8,128)(2,1)S(1)} %copy-done.2), custom_call_target="tpu_custom_call" | custom-call | tf_op jit(solution)/shard_map/decode/pallas_call | solution.py:243
  (61 shorter events, 4.2 us)
Async XLA Ops:
  6.5 78.4 %all-gather.7.cloned.1.call-start = ((), (), s32[]{:S(2)}) async-start(), calls=%async_computation.1 | async-start | bytes 2228224 | tf_op jit(solution)/shard_map/all_gather | solution.py:324
  45.1 103.8 %all-gather.9.cloned.1.call-start = ((), (), s32[]{:S(2)}) async-start(), calls=%async_computation.2 | async-start | bytes 8912896 | tf_op jit(solution)/shard_map/all_gather | solution.py:326
  46.3 2.4 %copy-start.10 = (bf16[4,12,24,512]{3,2,1,0:T(8,128)(2,1)S(1)}, bf16[4,12,24,512]{3,2,1,0:T(8,128)(2,1)}, u32[]{:S(2)}) copy-start(bf16[4,12,24,512]{3,2,1,0:T(8,128)(2,1)} %param.16) | copy-start | bytes 3538948
  47.3 137.5 %all-gather.11.cloned.1.call-start = ((), (), s32[]{:S(2)}) async-start(), calls=%async_computation.3 | async-start | bytes 2228224 | tf_op jit(solution)/shard_map/all_gather | solution.py:327
  48.7 10.2 %collective-permute-start = (bf16[4,9,6,512]{3,2,1,0:T(8,128)(2,1)S(1)}, bf16[4,9,6,512]{3,2,1,0:T(8,128)(2,1)S(1)}, u32[]{:S(2)}, u32[]{:S(2)}) collective-permute-start(bf16[4,9,6,512]{3,2,1,0:T(8,128)(2,1)S(1)} %slice.55), channel_id=1, source_target_pairs={{0,15},{1,0},{2,1},{3,2},{4,3},{5,4},{6,5},{7,6},{8,7},{9,8},{10,9... | collective-permute-start | bytes 663560 | tf_op jit(solution)/shard_map/ppermute | solution.py:276
  48.9 14.8 %collective-permute-start.1 = (bf16[4,3,18,512]{3,2,1,0:T(8,128)(2,1)S(1)}, bf16[4,3,18,512]{3,2,1,0:T(8,128)(2,1)}, u32[]{:S(2)}, u32[]{:S(2)}) collective-permute-start(bf16[4,3,18,512]{3,2,1,0:T(8,128)(2,1)S(1)} %slice.56), channel_id=1, source_target_pairs={{0,240},{16,0},{32,16},{48,32},{64,48},{80,64},{96,80},{112,96},{1... | collective-permute-start | bytes 663560 | tf_op jit(solution)/shard_map/ppermute | solution.py:276
  51.9 33.0 %copy-start.2 = (bf16[288,288]{1,0:T(8,128)(2,1)S(1)}, bf16[288,288]{1,0:T(8,128)(2,1)}, u32[]{:S(2)}) copy-start(bf16[288,288]{1,0:T(8,128)(2,1)} %constant.16.clone.from_win_ref) | copy-start | bytes 497668
  51.9 33.0 %copy-start.5 = (bf16[288,288]{1,0:T(8,128)(2,1)S(1)}, bf16[288,288]{1,0:T(8,128)(2,1)}, u32[]{:S(2)}) copy-start(bf16[288,288]{1,0:T(8,128)(2,1)} %constant.15.clone.to_win_ref) | copy-start | bytes 497668
  51.9 33.0 %copy-start.7 = (f32[512]{0:T(512)S(1)}, f32[512]{0:T(512)}, u32[]{:S(2)}) copy-start(f32[512]{0:T(512)} %param.17) | copy-start | bytes 6148
  51.9 7.0 %collective-permute-start.2 = (bf16[4,3,6,512]{3,2,1,0:T(8,128)(2,1)}, bf16[4,3,6,512]{3,2,1,0:T(8,128)(2,1)}, u32[]{:S(2)}, u32[]{:S(2)}) collective-permute-start(bf16[4,3,6,512]{3,2,1,0:T(8,128)(2,1)} %slice.57), channel_id=1, source_target_pairs={{0,255},{1,240},{2,241},{3,242},{4,243},{5,244},{6,245},{7,246},{8... | collective-permute-start | bytes 221192 | tf_op jit(solution)/shard_map/ppermute | solution.py:276
  85.0 1.6 copy-start
  96.3 14.7 %collective-permute-start.4 = (bf16[4,3,18,512]{3,2,1,0:T(8,128)(2,1)S(1)}, bf16[4,3,18,512]{3,2,1,0:T(8,128)(2,1)S(1)}, u32[]{:S(2)}, u32[]{:S(2)}) collective-permute-start(bf16[4,3,18,512]{3,2,1,0:T(8,128)(2,1)S(1)} %slice.73), channel_id=1, source_target_pairs={{0,16},{16,32},{32,48},{48,64},{64,80},{80,96},{96,112},{112,128},... | collective-permute-start | bytes 663560 | tf_op jit(solution)/shard_map/ppermute | solution.py:276
  96.4 23.4 %collective-permute-start.5 = (bf16[4,9,6,512]{3,2,1,0:T(8,128)(2,1)S(1)}, bf16[4,9,6,512]{3,2,1,0:T(8,128)(2,1)S(1)}, u32[]{:S(2)}, u32[]{:S(2)}) collective-permute-start(bf16[4,9,6,512]{3,2,1,0:T(8,128)(2,1)S(1)} %slice.74), channel_id=1, source_target_pairs={{0,1},{1,2},{2,3},{3,4},{4,5},{5,6},{6,7},{7,8},{8,9},{9,10},{10,1... | collective-permute-start | bytes 663560 | tf_op jit(solution)/shard_map/ppermute | solution.py:276
  96.8 52.1 %copy-start.3 = (bf16[288,288]{1,0:T(8,128)(2,1)S(1)}, bf16[288,288]{1,0:T(8,128)(2,1)}, u32[]{:S(2)}) copy-start(bf16[288,288]{1,0:T(8,128)(2,1)} %constant.17.clone.to_merged_ref) | copy-start | bytes 497668
  96.8 52.1 %copy-start.6 = (f32[2048]{0:T(1024)S(1)}, f32[2048]{0:T(1024)}, u32[]{:S(2)}) copy-start(f32[2048]{0:T(1024)} %param.20) | copy-start | bytes 24580
  96.8 52.1 %copy-start.8 = (f32[512]{0:T(512)S(1)}, f32[512]{0:T(512)}, u32[]{:S(2)}) copy-start(f32[512]{0:T(512)} %param.23) | copy-start | bytes 6148
  96.8 14.2 %collective-permute-start.3 = (bf16[4,3,6,512]{3,2,1,0:T(8,128)(2,1)S(1)}, bf16[4,3,6,512]{3,2,1,0:T(8,128)(2,1)S(1)}, u32[]{:S(2)}, u32[]{:S(2)}) collective-permute-start(bf16[4,3,6,512]{3,2,1,0:T(8,128)(2,1)S(1)} %slice.72), channel_id=1, source_target_pairs={{0,17},{1,18},{2,19},{3,20},{4,21},{5,22},{6,23},{7,24},{8,25},{9,... | collective-permute-start | bytes 221192 | tf_op jit(solution)/shard_map/ppermute | solution.py:276
  148.9 35.9 %copy-start.4 = (bf16[288,288]{1,0:T(8,128)(2,1)S(1)}, bf16[288,288]{1,0:T(8,128)(2,1)}, u32[]{:S(2)}) copy-start(bf16[288,288]{1,0:T(8,128)(2,1)} %constant.18.clone.to_win_ref) | copy-start | bytes 497668
  148.9 35.9 %copy-start.9 = (f32[512]{0:T(512)S(1)}, f32[512]{0:T(512)}, u32[]{:S(2)}) copy-start(f32[512]{0:T(512)} %param.24) | copy-start | bytes 6148
  184.8 1.6 copy-start.1
Sparse Core Ops, SparseCore 0:
  45.2 39.7 all-gather.6
  86.8 62.0 all-gather.8
  150.8 33.9 all-gather.10

commit v2 on v1

--- a/solution.py
+++ b/solution.py
@@ -85,17 +85,59 @@
         mixed_ref[rows, at : at + 2 * HD] = jnp.where(low, halves[0], halves[1]).astype(jnp.bfloat16)
 
 
-def encode_kernel(last_ref, x_ref, gain_ref, w_ref, to_win_ref, from_win_ref, out_ref, qkv_ref, mixed_ref):
+def put_attention(w_ref, rows, group, blocks):
+    w_ref[rows, group * 384 : (group + 1) * 384] = jnp.concatenate([b[:, :96] for b in blocks], axis=1)
+    w_ref[rows, 3 * C + group * 128 : 3 * C + (group + 1) * 128] = jnp.concatenate([b[:, 96:] for b in blocks], axis=1)
+
+
+def slots_of(place_ref, x, yl):
+    px, py = place_ref[0], place_ref[1]
+    return lax.rem(px - x + 4, 4), [lax.rem(py - (2 * yh + yl) + 4, 4) for yh in range(2)]
+
+
+def unpack_encoder(place_ref, raws, w_ref):
+    px, py, pz, me = (place_ref[i] for i in range(4))
+    for side in range(2):
+        near, far = raws[2 * side], raws[2 * side + 1]
+        core = lax.rem(me + side, 2)
+        for slot in range(4):
+            x = lax.rem(px - slot + 4, 4)
+            raw = near if slot == 0 else far.at[slot - 1]
+            for yl in range(2):
+                _, ys = slots_of(place_ref, 0, yl)
+                rows = pl.ds(pl.multiple_of((x * 4 + yl * 2 + core) * 32, 32), 32)
+                for group in range(4):
+                    blocks = [raw[ys[j % 2], lax.rem(2 * group + j // 2 - pz + 12, 8)] for j in range(4)]
+                    put_attention(w_ref, rows, group, blocks)
+
+
+def unpack_decoder(place_ref, raw_ref, w_ref):
+    for x in range(4):
+        for yl in range(2):
+            sx, ys = slots_of(place_ref, x, yl)
+            for core in range(2):
+                first = (x * 4 + yl * 2 + core) * 32
+                for group in range(4):
+                    blocks = [raw_ref[2 * group + j // 2, core, sx, ys[j % 2]] for j in range(4)]
+                    put_attention(w_ref, slice(first, first + 32), group, blocks)
+
+
+def encode_kernel(place_ref, x_ref, gain_ref, r0, r1, r2, r3, to_win_ref, from_win_ref, out_ref, w_ref, qkv_ref, mixed_ref):
     step = pl.program_id(0)
+
+    @pl.when(step == 0)
+    def _():
+        unpack_encoder(place_ref, (r0, r1, r2, r3), w_ref)
+
     pair, band = step // 2, step % 2
     upper, lower = 2 * pair + 1, (2 * pair + 2) % LEV
     x = jnp.concatenate([x_ref[upper, band], x_ref[lower, band]], axis=0).astype(jnp.float32)
     h = normed(x, gain_ref[...]).astype(jnp.bfloat16)
     h = dot(to_win_ref[...], h).astype(jnp.bfloat16)
     for third in range(3):
-        qkv_ref[:, third * C : (third + 1) * C] = dot(h, w_ref[:, third].reshape(C, C)).astype(jnp.bfloat16)
+        qkv_ref[:, third * C : (third + 1) * C] = dot(h, w_ref[:, third * C : (third + 1) * C]).astype(jnp.bfloat16)
     by_level = (pair == 1).astype(jnp.int32)
-    by_row = jnp.where(band == 1, last_ref[0], 0)
+    by_row = jnp.where(band == 1, place_ref[4], 0)
 
     def label(dim):
         index = lax.broadcasted_iota(jnp.int32, (WIN, WIN), dim)
@@ -106,14 +148,16 @@
     same = label(0) == label(1)
     for window in range(2):
         window_attention(qkv_ref, mixed_ref, window * WIN, same)
-    y = dot(mixed_ref[...], w_ref[:, 3].reshape(C, C)).astype(jnp.bfloat16)
+    y = dot(mixed_ref[...], w_ref[:, 3 * C :]).astype(jnp.bfloat16)
     y = dot(from_win_ref[...], y)
     out = (x + y).astype(jnp.bfloat16)
     out_ref[upper, band] = out[:WIN]
     out_ref[lower, band] = out[WIN:]
 
 
-def merge_split_kernel(x_ref, mgain_ref, sgain_ref, wm_ref, ws_ref, to_merged_ref, out_ref, quads_ref, skip_ref, middle_ref):
+def merge_split_kernel(
+    place_ref, x_ref, mgain_ref, sgain_ref, wm_ref, ws_ref, to_merged_ref, out_ref, quads_ref, skip_ref, middle_ref, w_ref, w2_ref
+):
     step = pl.program_id(0)
     quarter = BAND // 4
 
@@ -137,34 +181,57 @@
 
     @pl.when(step < 4)
     def _():
-        width = wm_ref.shape[-1]
-        middle_ref[step] = dot(quads_ref[...], wm_ref[:, 0].reshape(4 * C, width)).astype(jnp.bfloat16)
+        for x in range(4):
+            for yl in range(2):
+                sx, ys = slots_of(place_ref, x, yl)
+                for core in range(2):
+                    first = (x * 4 + yl * 2 + core) * 128
+                    for z in range(2):
+                        left, right = (wm_ref[z, core, sx, y] for y in ys)
+                        cols = slice(z * 128, (z + 1) * 128)
+                        w_ref[first : first + 64, cols] = jnp.concatenate([left[:, :64], right[:, :64]], axis=1)
+                        w_ref[first + 64 : first + 128, cols] = jnp.concatenate([left[:, 64:], right[:, 64:]], axis=1)
+        middle_ref[step] = dot(quads_ref[...], w_ref[...]).astype(jnp.bfloat16)
 
     @pl.when(step >= 4)
     def _():
         part = step - 4
         width = middle_ref.shape[-1]
-        w = ws_ref[:, 0].reshape(2 * C, C)
-        total = dot(middle_ref[0], w[:width])
+        for x in range(4):
+            for yl in range(2):
+                sx, ys = slots_of(place_ref, x, yl)
+                for core in range(2):
+                    first = (x * 4 + yl * 2 + core) * 64
+                    for z in range(2):
+                        for yh in range(2):
+                            lon = 2 * z + yh
+                            w2_ref[first : first + 64, lon * 128 : (lon + 1) * 128] = ws_ref[z, core, sx, ys[yh]]
+        total = dot(middle_ref[0], w2_ref[:width])
         for chunk in range(1, 4):
-            total += dot(middle_ref[chunk], w[chunk * width : (chunk + 1) * width])
+            total += dot(middle_ref[chunk], w2_ref[chunk * width : (chunk + 1) * width])
         kept = (part % 2) * 2 + part // 2
         joined = (normed(total, sgain_ref[...]) + skip_ref[kept]).astype(jnp.bfloat16)
         out_ref[0] = joined
 
 
-def decode_kernel(x_ref, gain_ref, w_ref, to_win_ref, from_win_ref, out_ref, qkv_ref, mixed_ref):
+def decode_kernel(place_ref, x_ref, gain_ref, raw_ref, to_win_ref, from_win_ref, out_ref, w_ref, qkv_ref, mixed_ref):
     step = pl.program_id(0)
+
+    @pl.when(step == 0)
+    def _():
+        unpack_decoder(place_ref, raw_ref, w_ref)
+
+
     pair, band = step // 2, step % 2
     quarter = BAND // 4
     x = jnp.concatenate([x_ref[part, step].astype(jnp.float32) for part in range(4)], axis=0).astype(jnp.bfloat16)
     x = dot(to_win_ref[...], x)
     h = normed(x, gain_ref[...]).astype(jnp.bfloat16)
     for third in range(3):
-        qkv_ref[:, third * C : (third + 1) * C] = dot(h, w_ref[:, third].reshape(C, C)).astype(jnp.bfloat16)
+        qkv_ref[:, third * C : (third + 1) * C] = dot(h, w_ref[:, third * C : (third + 1) * C]).astype(jnp.bfloat16)
     for window in range(2):
         window_attention(qkv_ref, mixed_ref, window * WIN, None)
-    y = dot(mixed_ref[...], w_ref[:, 3].reshape(C, C)).astype(jnp.bfloat16)
+    y = dot(mixed_ref[...], w_ref[:, 3 * C :]).astype(jnp.bfloat16)
     out = (x + y.astype(jnp.float32)).astype(jnp.bfloat16)
     out = dot(from_win_ref[...], out).astype(jnp.bfloat16)
     out_ref[2 * pair, band] = out[:WIN]
@@ -178,7 +245,7 @@
 PARAMS = pltpu.CompilerParams(vmem_limit_bytes=VMEM_LIMIT)
 
 
-def encode(framed, gain, weights, last):
+def encode(framed, gain, weights, place):
     to_win = window_from_natural()
     shape = (LEV, 2, WIN, C)
     return pl.pallas_call(
@@ -188,30 +255,35 @@
             pl.BlockSpec(memory_space=pltpu.SMEM),
             whole(shape),
             whole((1, C)),
-            whole((16, 4, 32, C)),
+            *[whole(raw.shape) for raw in weights],
             whole((BAND, BAND)),
             whole((BAND, BAND)),
         ],
         out_specs=whole(shape),
         out_shape=jax.ShapeDtypeStruct(shape, jnp.bfloat16),
-        scratch_shapes=[pltpu.VMEM((BAND, 3 * C), jnp.bfloat16), pltpu.VMEM((BAND, C), jnp.bfloat16)],
+        scratch_shapes=[
+            pltpu.VMEM((C, 4 * C), jnp.bfloat16),
+            pltpu.VMEM((BAND, 3 * C), jnp.bfloat16),
+            pltpu.VMEM((BAND, C), jnp.bfloat16),
+        ],
         compiler_params=PARAMS,
         name="encode",
-    )(last, framed, gain.reshape(1, C), weights, jnp.asarray(to_win, jnp.bfloat16), jnp.asarray(to_win.T, jnp.bfloat16))
-
-
-def merge_split(encoded, mgain, sgain, weights):
+    )(place, framed, gain.reshape(1, C), *weights, jnp.asarray(to_win, jnp.bfloat16), jnp.asarray(to_win.T, jnp.bfloat16))
+
+
+def merge_split(encoded, mgain, sgain, raw, place):
     to_merged = merged_from_natural()
     tokens = LEV * ROWS * COLS // 4
     return pl.pallas_call(
         merge_split_kernel,
         grid=(8,),
         in_specs=[
+            pl.BlockSpec(memory_space=pltpu.SMEM),
             whole((LEV, 2, WIN, C)),
             whole((1, 4 * C)),
             whole((1, C)),
-            pl.BlockSpec((16, 1, 128, 256), lambda i: (0, jnp.minimum(i, 3) // 2, 0, jnp.minimum(i, 3) % 2)),
-            pl.BlockSpec((16, 1, 64, C), lambda i: (0, jnp.maximum(i, 4), 0, 0)),
+            pl.BlockSpec((2, 2, 4, 4, 64, 128), lambda i: (jnp.minimum(i, 3), 0, 0, 0, 0, 0)),
+            pl.BlockSpec((2, 2, 4, 4, 64, 128), lambda i: (jnp.maximum(i - 4, 0), 0, 0, 0, 1, 0)),
             whole((BAND, BAND)),
         ],
         out_specs=pl.BlockSpec(
@@ -223,20 +295,23 @@
             pltpu.VMEM((tokens, 4 * C), jnp.bfloat16),
             pltpu.VMEM((4, tokens, C), jnp.float32),
             pltpu.VMEM((4, tokens, 256), jnp.bfloat16),
+            pltpu.VMEM((4 * C, 256), jnp.bfloat16),
+            pltpu.VMEM((2 * C, C), jnp.bfloat16),
         ],
         compiler_params=PARAMS,
         name="merge_split",
     )(
+        place,
         encoded,
         mgain.reshape(1, 4 * C),
         sgain.reshape(1, C),
-        weights.reshape(16, 4, 128, C),
-        weights.reshape(16, 8, 64, C),
+        raw,
+        raw,
         jnp.asarray(to_merged, jnp.bfloat16),
     )
 
 
-def decode(joined, gain, weights):
+def decode(joined, gain, weights, place):
     to_win = window_from_natural()
     from_merged = to_win @ merged_from_natural().T
     shape = (LEV, 2, WIN, C)
@@ -244,18 +319,24 @@
         decode_kernel,
         grid=(4,),
         in_specs=[
+            pl.BlockSpec(memory_space=pltpu.SMEM),
             whole((4, 4, BAND // 4, C)),
             whole((1, C)),
-            whole((16, 4, 32, C)),
+            pl.BlockSpec((8, 2, 4, 4, 32, 128), lambda i: (0, 0, 0, 0, 4, 0)),
             whole((BAND, BAND)),
             whole((BAND, BAND)),
         ],
         out_specs=whole(shape),
         out_shape=jax.ShapeDtypeStruct(shape, jnp.bfloat16),
-        scratch_shapes=[pltpu.VMEM((BAND, 3 * C), jnp.bfloat16), pltpu.VMEM((BAND, C), jnp.bfloat16)],
+        scratch_shapes=[
+            pltpu.VMEM((C, 4 * C), jnp.bfloat16),
+            pltpu.VMEM((BAND, 3 * C), jnp.bfloat16),
+            pltpu.VMEM((BAND, C), jnp.bfloat16),
+        ],
         compiler_params=PARAMS,
         name="decode",
     )(
+        place,
         joined.reshape(4, 4, BAND // 4, C),
         gain.reshape(1, C),
         weights,
@@ -276,18 +357,43 @@
     return lax.ppermute(value, axis, pairs)
 
 
-def gathered_cols(block):
-    return lax.all_to_all(jnp.broadcast_to(block[None], (16,) + block.shape), "lon", 0, 0, tiled=True)
-
-
-def pack_attention(qkv, proj):
-    return jnp.concatenate([qkv, proj], axis=1)
-
-
-def unpack_attention(blocks):
-    qkv = blocks[:, :, :96].transpose(1, 0, 2).reshape(32, 3, C).transpose(1, 0, 2)
-    proj = blocks[:, :, 96:].transpose(1, 0, 2).reshape(1, 32, C)
-    return jnp.concatenate([qkv, proj], axis=0)
+def device_index(x, y, z, core):
+    return (x * 4 + (y % 2) * 2 + core) * 16 + z * 2 + y // 2
+
+
+def chips():
+    return [(x, y, z, core) for x in range(4) for y in range(4) for z in range(8) for core in range(2)]
+
+
+def sent(value, to):
+    return lax.ppermute(value, ("lat", "lon"), [(device_index(*at), device_index(*to(*at))) for at in chips()])
+
+
+def from_x(value):
+    return [sent(value, lambda x, y, z, c: ((x + steps) % 4, y, z, c)) for steps in (1, 2, 3)]
+
+
+def from_y(value):
+    return [sent(value, lambda x, y, z, c: (x, (y + steps) % 4, z, c)) for steps in (1, 2, 3)]
+
+
+def from_z(value, steps):
+    return sent(value, lambda x, y, z, c: (x, y, (z + steps) % 8, c))
+
+
+def z_and_cores(value):
+    groups = [
+        [device_index(x, y, z, core) for z in range(8) for core in range(2)] for x in range(4) for y in range(4)
+    ]
+    return lax.all_gather(value, ("lat", "lon"), axis=0, tiled=False, axis_index_groups=groups)
+
+
+def other_core(value):
+    return sent(value, lambda x, y, z, c: (x, y, z, 1 - c))
+
+
+def together(*values):
+    return lax.optimization_barrier(values)
 
 
 def shards(
@@ -305,30 +411,35 @@
 ):
     half_lat = WA // 2
     half_lon = WO // 2
-    packed = jnp.concatenate(
+    lat, lon = lax.axis_index("lat"), lax.axis_index("lon")
+    last = lat == lax.axis_size("lat") - 1
+    place = jnp.stack([lat // 4, (lon % 2) * 2 + (lat // 2) % 2, lon // 2, lat % 2, last.astype(jnp.int32)]).astype(jnp.int32)
+    enc_share = jnp.concatenate([enc_qkv, enc_proj], axis=1)
+    later_share = jnp.concatenate(
         [
-            pack_attention(enc_qkv, enc_proj),
-            pack_attention(dec_qkv, dec_proj),
             jnp.concatenate([merge_weight[:64], merge_weight[64:]], axis=1),
             split_weight,
+            jnp.concatenate([dec_qkv, dec_proj], axis=1),
         ],
         axis=0,
     )
-    blocks = gathered_cols(packed)
-    enc_rows = unpack_attention(blocks[:, :32])
-    dec_rows = unpack_attention(blocks[:, 32:64])
-    merge_rows = (
-        blocks[:, 64:128].reshape(16, 64, 2, 64).transpose(2, 1, 0, 3).reshape(128, 2, C).transpose(1, 0, 2)
-    )
-    split_rows = blocks[:, 128:].transpose(1, 0, 2).reshape(64, 4, C).transpose(1, 0, 2)
-    enc_w = lax.all_gather(enc_rows, "lat", axis=0, tiled=False)
-    ms_rows = jnp.concatenate([merge_rows.reshape(256, C), split_rows.reshape(256, C)], axis=0)
-    ms_w = lax.all_gather(ms_rows, "lat", axis=0, tiled=False)
-    dec_w = lax.all_gather(dec_rows, "lat", axis=0, tiled=False)
-
-    below = passed_along(tokens[:, :half_lat, half_lon:], "lat", -1)
-    beyond = passed_along(tokens[:, half_lat:, :half_lon], "lon", -1)
-    corner = passed_along(tokens[:, :half_lat, :half_lon], ("lat", "lon"), -1)
+
+    later_y = from_y(later_share)
+    enc_near = [from_z(enc_share, 1), from_z(enc_share, -1)]
+    later_near = jnp.stack([later_share, *later_y])
+    later_x = from_x(later_near)
+    enc_three = jnp.stack([enc_near[0], enc_share, enc_near[1]])
+    enc_far = [from_z(enc_three, 3), from_z(enc_three[:2], -3)]
+    tokens_sent, later_x = together(tokens, later_x)
+    later_raw = z_and_cores(jnp.stack([later_near, *later_x])).reshape(8, 2, 4, 4, 160, 128)
+    below = passed_along(tokens_sent[:, :half_lat, half_lon:], "lat", -1)
+    beyond = passed_along(tokens_sent[:, half_lat:, :half_lon], "lon", -1)
+    corner = passed_along(tokens_sent[:, :half_lat, :half_lon], ("lat", "lon"), -1)
+    enc_far, below, beyond, corner = together(enc_far, below, beyond, corner)
+    enc_z = jnp.concatenate([enc_far[0], enc_three, enc_far[1]], axis=0)
+    enc_y = jnp.stack([enc_z, *from_y(enc_z)])
+    enc_x = jnp.stack(from_x(enc_y))
+    enc_raw = [enc_y, enc_x, other_core(enc_y), other_core(enc_x)]
     framed = jnp.concatenate(
         [
             jnp.concatenate([tokens[:, half_lat:, half_lon:], beyond], axis=2),
@@ -336,8 +447,7 @@
         ],
         axis=1,
     )
-    last = (lax.axis_index("lat") == lax.axis_size("lat") - 1).astype(jnp.int32).reshape(1)
-    moved = encode(framed.reshape(LEV, 2, WIN, C), enc_gain, enc_w, last).reshape(LEV, ROWS, COLS, C)
+    moved = encode(framed.reshape(LEV, 2, WIN, C), enc_gain, enc_raw, place).reshape(LEV, ROWS, COLS, C)
     cut_r, cut_c = ROWS - half_lat, COLS - half_lon
     above = passed_along(moved[:, cut_r:, :cut_c], "lat", 1)
     left = passed_along(moved[:, :cut_r, cut_c:], "lon", 1)
@@ -349,8 +459,8 @@
         ],
         axis=1,
     )
-    joined = merge_split(encoded.reshape(LEV, 2, WIN, C), merge_gain, split_gain, ms_w)
-    return decode(joined, dec_gain, dec_w).reshape(LEV, ROWS, COLS, C)
+    joined = merge_split(encoded.reshape(LEV, 2, WIN, C), merge_gain, split_gain, later_raw, place)
+    return decode(joined, dec_gain, later_raw, place).reshape(LEV, ROWS, COLS, C)
 
 
 def solution(mesh):

time: 204 us -> 143 us (0.70)
  waiting for transfers between devices: 102 us -> 41.7 us
  blocking collectives: 35 us -> 0 us
  starting transfers between devices: 10.2 us -> 44.3 us
  local copies, waits for them, and re-layouts: 9.28 us -> 2.51 us
  Pallas kernels: 29.9 us -> 34.9 us
    all_gather x3 -> x1, waiting for transfers between devices: 74.9 us -> 0.02 us  [z_and_cores(): lax.all_gather(value, ('lat', 'lon'), axis=0, tiled=False, axis_index_gro...]
    all_to_all x1 -> x0, blocking collectives: 35 us -> none  [gathered_cols(): lax.all_to_all(jnp.broadcast_to(block[None], (16,) + block.shape), 'lon',...]
    ppermute x0 -> x18, starting transfers between devices: none -> 30.5 us  [sent(): lax.ppermute(value, ('lat', 'lon'), [(device_index(*at), device_index(*to...]
    ppermute x0 -> x18, waiting for transfers between devices: none -> 29.9 us  [sent(): lax.ppermute(value, ('lat', 'lon'), [(device_index(*at), device_index(*to...]
    ppermute x6, waiting for transfers between devices: 27.1 us -> 11.7 us  [passed_along(): return lax.ppermute(value, axis, pairs)]
    ppermute x6, starting transfers between devices: 10.1 us -> 13.8 us  [passed_along(): return lax.ppermute(value, axis, pairs)]
    pallas_call x2, Pallas kernels: 20.3 us -> 23.7 us  [the longest x1 13.3 us: decode(): pl.pallas_call(decode_kernel, grid=(4,), in_specs=[pl.BlockSpec(memory_sp...]
    unnamed x24 -> x34, local copies, waits for them, and re-layouts: 3.41 us -> 0.91 us
  transfers between devices with their start and end apart: 9 -> 25, of which waited for: 7 -> 13; matrix products, arithmetic and copies ran while one was open for 3% -> 3% of each run, Pallas kernels for 9% -> 8%
where the time goes in v2:
time: 143 us; the launch traced here: 142 us
  starting transfers between devices  44.3 us (31%)
  waiting for transfers between devices  41.7 us (29%)
  Pallas kernels  34.9 us (24%)
  between operations  13.8 us (10%)
  other arithmetic  4.72 us (3%)
  local copies, waits for them, and re-layouts  2.51 us (2%)
    ppermute x18, starting transfers between devices, sent(): lax.ppermute(value, ('lat', 'lon'), [(device_index(*at), device_index(*to...  30.5 us
    ppermute x18, waiting for transfers between devices, sent(): lax.ppermute(value, ('lat', 'lon'), [(device_index(*at), device_index(*to...  29.9 us
    ppermute x6, starting transfers between devices, passed_along(): return lax.ppermute(value, axis, pairs)  13.8 us
    pallas_call x1, Pallas kernels, decode(): pl.pallas_call(decode_kernel, grid=(4,), in_specs=[pl.BlockSpec(memory_sp...  13.3 us
    ppermute x6, waiting for transfers between devices, passed_along(): return lax.ppermute(value, axis, pairs)  11.7 us
    pallas_call x1, Pallas kernels, encode(): pl.pallas_call(encode_kernel, grid=(4,), in_specs=[pl.BlockSpec(memory_sp...  11.1 us
    pallas_call x1, Pallas kernels, merge_split(): pl.pallas_call(merge_split_kernel, grid=(8,), in_specs=[pl.BlockSpec(memo...  10.5 us
  transfers between devices with their start and end apart: 25, of which 13 were waited for; matrix products, arithmetic and copies ran while one was open for 3% of the time, Pallas kernels for 8%

profile of v2, /device:TPU:1, one launch (start us, length us, event | category | flops | bytes accessed | tf_op | source)
XLA Modules:
  0.0 141.8 jit_solution(15610611888775359889)
XLA Ops:
  8.4 3.8 %collective-permute-start.5 = (bf16[160,128]{1,0:T(8,128)(2,1)S(1)}, bf16[160,128]{1,0:T(8,128)(2,1)S(1)}, u32[]{:S(2)}, u32[]{:S(2)}) collective-permute-start(bf16[160,128]{1,0:T(8,128)(2,1)S(1)} %maximum_maximum_fusion.2), channel_id=1, source_target_pairs={{0,1},{16,17},{2,3},{18,19},{4,5},{20,21},{6,7},{22,23},{8,9},{24,... | collective-permute-start | bytes 122888 | tf_op jit(solution)/shard_map/ppermute | solution.py:369
  15.5 1.6 %collective-permute-done.4 = bf16[160,128]{1,0:T(8,128)(2,1)S(1)} collective-permute-done((bf16[160,128]{1,0:T(8,128)(2,1)S(1)}, bf16[160,128]{1,0:T(8,128)(2,1)S(1)}, u32[]{:S(2)}, u32[]{:S(2)}) %collective-permute-start.4) | collective-permute-done | bytes 40992 | tf_op jit(solution)/shard_map/ppermute | solution.py:369
  17.1 1.3 collective-permute-start.7
  18.4 2.5 %collective-permute-start.8 = (bf16[4,160,128]{2,1,0:T(8,128)(2,1)S(1)}, bf16[4,160,128]{2,1,0:T(8,128)(2,1)S(1)}, u32[]{:S(2)}, u32[]{:S(2)}) collective-permute-start(bf16[4,160,128]{2,1,0:T(8,128)(2,1)S(1)} %get-tuple-element.24), channel_id=1, source_target_pairs={{0,128},{16,144},{2,130},{18,146},{4,132},{20,148},{6,134},{22,150... | collective-permute-start | bytes 491528 | tf_op jit(solution)/shard_map/ppermute | solution.py:369
  22.6 3.3 %collective-permute-done.8 = bf16[4,160,128]{2,1,0:T(8,128)(2,1)S(1)} collective-permute-done((bf16[4,160,128]{2,1,0:T(8,128)(2,1)S(1)}, bf16[4,160,128]{2,1,0:T(8,128)(2,1)S(1)}, u32[]{:S(2)}, u32[]{:S(2)}) %collective-permute-start.8) | collective-permute-done | bytes 163872 | tf_op jit(solution)/shard_map/ppermute | solution.py:369
  27.0 1.7 %collective-permute-start = (bf16[32,128]{1,0:T(8,128)(2,1)S(1)}, bf16[32,128]{1,0:T(8,128)(2,1)S(1)}, u32[]{:S(2)}, u32[]{:S(2)}) collective-permute-start(bf16[32,128]{1,0:T(8,128)(2,1)S(1)} %pad_maximum_fusion.6), channel_id=1, source_target_pairs={{0,2},{16,18},{2,4},{18,20},{4,6},{20,22},{6,8},{22,24},{8,10},{24... | collective-permute-start | bytes 24584 | tf_op jit(solution)/shard_map/ppermute | solution.py:369
  28.6 4.0 %collective-permute-start.1 = (bf16[32,128]{1,0:T(8,128)(2,1)S(1)}, bf16[32,128]{1,0:T(8,128)(2,1)S(1)}, u32[]{:S(2)}, u32[]{:S(2)}) collective-permute-start(bf16[32,128]{1,0:T(8,128)(2,1)S(1)} %pad_maximum_fusion.6), channel_id=1, source_target_pairs={{0,14},{16,30},{2,0},{18,16},{4,2},{20,18},{6,4},{22,20},{8,6},{24... | collective-permute-start | bytes 24584 | tf_op jit(solution)/shard_map/ppermute | solution.py:369
  32.8 4.0 %collective-permute-start.10 = (bf16[4,3,18,512]{3,2,1,0:T(8,128)(2,1)S(1)}, bf16[4,3,18,512]{3,2,1,0:T(8,128)(2,1)S(1)}, u32[]{:S(2)}, u32[]{:S(2)}) collective-permute-start(bf16[4,3,18,512]{3,2,1,0:T(8,128)(2,1)S(1)} %slice.35), channel_id=1, source_target_pairs={{0,240},{16,0},{32,16},{48,32},{64,48},{80,64},{96,80},{112,96},{1... | collective-permute-start | bytes 663560 | tf_op jit(solution)/shard_map/ppermute | solution.py:357
  36.7 1.8 %collective-permute-start.11 = (bf16[4,9,6,512]{3,2,1,0:T(8,128)(2,1)S(1)}, bf16[4,9,6,512]{3,2,1,0:T(8,128)(2,1)S(1)}, u32[]{:S(2)}, u32[]{:S(2)}) collective-permute-start(bf16[4,9,6,512]{3,2,1,0:T(8,128)(2,1)S(1)} %slice.36), channel_id=1, source_target_pairs={{0,15},{1,0},{2,1},{3,2},{4,3},{5,4},{6,5},{7,6},{8,7},{9,8},{10,9... | collective-permute-start | bytes 663560 | tf_op jit(solution)/shard_map/ppermute | solution.py:357
  38.7 4.4 %collective-permute-start.12 = (bf16[4,3,6,512]{3,2,1,0:T(8,128)(2,1)S(1)}, bf16[4,3,6,512]{3,2,1,0:T(8,128)(2,1)S(1)}, u32[]{:S(2)}, u32[]{:S(2)}) collective-permute-start(bf16[4,3,6,512]{3,2,1,0:T(8,128)(2,1)S(1)} %slice.37), channel_id=1, source_target_pairs={{0,255},{1,240},{2,241},{3,242},{4,243},{5,244},{6,245},{7,246},{8... | collective-permute-start | bytes 221192 | tf_op jit(solution)/shard_map/ppermute | solution.py:357
  43.1 2.0 %collective-permute-start.3 = (bf16[2,32,128]{2,1,0:T(8,128)(2,1)S(1)}, bf16[2,32,128]{2,1,0:T(8,128)(2,1)S(1)}, u32[]{:S(2)}, u32[]{:S(2)}) collective-permute-start(bf16[2,32,128]{2,1,0:T(8,128)(2,1)S(1)} %pad_maximum_fusion.5), channel_id=1, source_target_pairs={{0,10},{16,26},{2,12},{18,28},{4,14},{20,30},{6,0},{22,16},{8,2},{... | collective-permute-start | bytes 49160 | tf_op jit(solution)/shard_map/ppermute | solution.py:369
  45.1 8.8 %collective-permute-done.3 = bf16[2,32,128]{2,1,0:T(8,128)(2,1)S(1)} collective-permute-done((bf16[2,32,128]{2,1,0:T(8,128)(2,1)S(1)}, bf16[2,32,128]{2,1,0:T(8,128)(2,1)S(1)}, u32[]{:S(2)}, u32[]{:S(2)}) %collective-permute-start.3) | collective-permute-done | bytes 16416 | tf_op jit(solution)/shard_map/ppermute | solution.py:369
  54.7 6.9 %collective-permute-start.14 = (bf16[8,32,128]{2,1,0:T(8,128)(2,1)S(1)}, bf16[8,32,128]{2,1,0:T(8,128)(2,1)S(1)}, u32[]{:S(2)}, u32[]{:S(2)}) collective-permute-start(bf16[8,32,128]{2,1,0:T(8,128)(2,1)S(1)} %constant_dynamic-update-slice_fusion), channel_id=1, source_target_pairs={{0,1},{16,17},{2,3},{18,19},{4,5},{20,21},{6,7},{22,23},{8,9},{24,... | collective-permute-start | bytes 196616 | tf_op jit(solution)/shard_map/ppermute | solution.py:369
  62.6 1.4 collective-permute-done.14
  66.3 1.9 %collective-permute-start.17 = (bf16[4,8,32,128]{3,2,1,0:T(8,128)(2,1)S(1)}, bf16[4,8,32,128]{3,2,1,0:T(8,128)(2,1)S(1)}, u32[]{:S(2)}, u32[]{:S(2)}) collective-permute-start(bf16[4,8,32,128]{3,2,1,0:T(8,128)(2,1)S(1)} %pad_maximum_fusion.2.r0), channel_id=1, source_target_pairs={{0,128},{16,144},{2,130},{18,146},{4,132},{20,148},{6,134},{22,150... | collective-permute-start | bytes 786440 | tf_op jit(solution)/shard_map/ppermute | solution.py:369
  68.1 2.0 %collective-permute-start.18 = (bf16[4,8,32,128]{3,2,1,0:T(8,128)(2,1)S(1)}, bf16[4,8,32,128]{3,2,1,0:T(8,128)(2,1)S(1)}, u32[]{:S(2)}, u32[]{:S(2)}) collective-permute-start(bf16[4,8,32,128]{3,2,1,0:T(8,128)(2,1)S(1)} %pad_maximum_fusion.2.r0), channel_id=1, source_target_pairs={{0,192},{16,208},{2,194},{18,210},{4,196},{20,212},{6,198},{22,214... | collective-permute-start | bytes 786440 | tf_op jit(solution)/shard_map/ppermute | solution.py:369
  70.1 4.2 %collective-permute-done.16 = bf16[4,8,32,128]{3,2,1,0:T(8,128)(2,1)S(1)} collective-permute-done((bf16[4,8,32,128]{3,2,1,0:T(8,128)(2,1)S(1)}, bf16[4,8,32,128]{3,2,1,0:T(8,128)(2,1)S(1)}, u32[]{:S(2)}, u32[]{:S(2)}) %collective-permute-start.16) | collective-permute-done | bytes 262176 | tf_op jit(solution)/shard_map/ppermute | solution.py:369
  74.4 6.0 %collective-permute-done.17 = bf16[4,8,32,128]{3,2,1,0:T(8,128)(2,1)S(1)} collective-permute-done((bf16[4,8,32,128]{3,2,1,0:T(8,128)(2,1)S(1)}, bf16[4,8,32,128]{3,2,1,0:T(8,128)(2,1)S(1)}, u32[]{:S(2)}, u32[]{:S(2)}) %collective-permute-start.17) | collective-permute-done | bytes 262176 | tf_op jit(solution)/shard_map/ppermute | solution.py:369
  82.1 1.3 maximum_maximum_fusion
  83.8 11.1 %encode.1 = bf16[4,2,144,512]{3,2,1,0:T(8,128)(2,1)S(1)} custom-call(s32[5]{0:T(128)S(1)} %stack.98.place_ref, bf16[4,2,144,512]{3,2,1,0:T(8,128)(2,1)S(1)} %bitcast.42, f32[1,512]{1,0:T(1,128)S(1)} %bitcast.46, bf16[4,8,32,128]{3,2,1,0:T(8,128)(2,1)S(1)} %pad_maximum_fusion.2.r0, bf16[3,4,8,32,128]{4,3,2,1,0:T(8,128)(2,1)S(1)} %pad_maximum_fusion.r1, ...), custom_call_target="tpu_custom_call" | custom-call | tf_op jit(solution)/shard_map/encode/pallas_call | solution.py:251
  96.1 2.2 %collective-permute-start.23 = (bf16[4,9,6,512]{3,2,1,0:T(8,128)(2,1)S(1)}, bf16[4,9,6,512]{3,2,1,0:T(8,128)(2,1)S(1)}, u32[]{:S(2)}, u32[]{:S(2)}) collective-permute-start(bf16[4,9,6,512]{3,2,1,0:T(8,128)(2,1)S(1)} %slice.44), channel_id=1, source_target_pairs={{0,1},{1,2},{2,3},{3,4},{4,5},{5,6},{6,7},{7,8},{8,9},{9,10},{10,1... | collective-permute-start | bytes 663560 | tf_op jit(solution)/shard_map/ppermute | solution.py:357
  98.8 11.7 %collective-permute-done.21 = bf16[4,3,6,512]{3,2,1,0:T(8,128)(2,1)S(1)} collective-permute-done((bf16[4,3,6,512]{3,2,1,0:T(8,128)(2,1)S(1)}, bf16[4,3,6,512]{3,2,1,0:T(8,128)(2,1)S(1)}, u32[]{:S(2)}, u32[]{:S(2)}) %collective-permute-start.21) | collective-permute-done | bytes 73760 | tf_op jit(solution)/shard_map/ppermute | solution.py:357
  111.1 10.5 %merge_split.1 = bf16[4,288,512]{2,1,0:T(8,128)(2,1)S(1)} custom-call(s32[5]{0:T(128)S(1)} %stack.98.place_ref, bf16[4,2,144,512]{3,2,1,0:T(8,128)(2,1)S(1)} %bitcast.43, f32[1,2048]{1,0:T(1,128)S(1)} %bitcast.45, f32[1,512]{1,0:T(1,128)S(1)} %bitcast.48, bf16[8,2,4,4,160,128]{5,4,3,2,1,0:T(8,128)(2,1)} %bitcast.49, ...), custom_call_target="tpu_custom_call" | custom-call | tf_op jit(solution)/shard_map/merge_split/pallas_call | solution.py:277
  121.6 13.3 %decode.1 = bf16[4,2,144,512]{3,2,1,0:T(8,128)(2,1)} custom-call(s32[5]{0:T(128)S(1)} %stack.98.place_ref, bf16[4,4,72,512]{3,2,1,0:T(8,128)(2,1)S(1)} %bitcast.44, f32[1,512]{1,0:T(1,128)S(1)} %bitcast.47, bf16[8,2,4,4,160,128]{5,4,3,2,1,0:T(8,128)(2,1)} %bitcast.51, bf16[288,288]{1,0:T(8,128)(2,1)S(1)} %copy-done.1, bf16[288,288]{1,0:T(8,128)(2,1)S(1)} %copy-done), custom_call_target="tpu_custom_call" | custom-call | tf_op jit(solution)/shard_map/decode/pallas_call | solution.py:318
  (86 shorter events, 16.4 us)
Async XLA Ops:
  6.5 104.5 %all-gather.3.cloned.1.call-start = ((), (), s32[]{:S(2)}) async-start(), calls=%async_computation | async-start | bytes 11141120 | tf_op jit(solution)/shard_map/all_gather | solution.py:388
  8.4 6.1 %collective-permute-start.5 = (bf16[160,128]{1,0:T(8,128)(2,1)S(1)}, bf16[160,128]{1,0:T(8,128)(2,1)S(1)}, u32[]{:S(2)}, u32[]{:S(2)}) collective-permute-start(bf16[160,128]{1,0:T(8,128)(2,1)S(1)} %maximum_maximum_fusion.2), channel_id=1, source_target_pairs={{0,1},{16,17},{2,3},{18,19},{4,5},{20,21},{6,7},{22,23},{8,9},{24,... | collective-permute-start | bytes 122888 | tf_op jit(solution)/shard_map/ppermute | solution.py:369
  12.3 3.2 %collective-permute-start.6 = (bf16[160,128]{1,0:T(8,128)(2,1)S(1)}, bf16[160,128]{1,0:T(8,128)(2,1)S(1)}, u32[]{:S(2)}, u32[]{:S(2)}) collective-permute-start(bf16[160,128]{1,0:T(8,128)(2,1)S(1)} %maximum_maximum_fusion.2), channel_id=1, source_target_pairs={{0,33},{16,49},{2,35},{18,51},{4,37},{20,53},{6,39},{22,55},{8,41}... | collective-permute-start | bytes 122888 | tf_op jit(solution)/shard_map/ppermute | solution.py:369
  13.0 4.1 %collective-permute-start.4 = (bf16[160,128]{1,0:T(8,128)(2,1)S(1)}, bf16[160,128]{1,0:T(8,128)(2,1)S(1)}, u32[]{:S(2)}, u32[]{:S(2)}) collective-permute-start(bf16[160,128]{1,0:T(8,128)(2,1)S(1)} %maximum_maximum_fusion.2), channel_id=1, source_target_pairs={{0,32},{16,48},{2,34},{18,50},{4,36},{20,52},{6,38},{22,54},{8,40}... | collective-permute-start | bytes 122888 | tf_op jit(solution)/shard_map/ppermute | solution.py:369
  17.1 5.5 %collective-permute-start.7 = (bf16[4,160,128]{2,1,0:T(8,128)(2,1)S(1)}, bf16[4,160,128]{2,1,0:T(8,128)(2,1)S(1)}, u32[]{:S(2)}, u32[]{:S(2)}) collective-permute-start(bf16[4,160,128]{2,1,0:T(8,128)(2,1)S(1)} %get-tuple-element.24), channel_id=1, source_target_pairs={{0,64},{16,80},{2,66},{18,82},{4,68},{20,84},{6,70},{22,86},{8,72}... | collective-permute-start | bytes 491528 | tf_op jit(solution)/shard_map/ppermute | solution.py:369
  18.4 7.5 %collective-permute-start.8 = (bf16[4,160,128]{2,1,0:T(8,128)(2,1)S(1)}, bf16[4,160,128]{2,1,0:T(8,128)(2,1)S(1)}, u32[]{:S(2)}, u32[]{:S(2)}) collective-permute-start(bf16[4,160,128]{2,1,0:T(8,128)(2,1)S(1)} %get-tuple-element.24), channel_id=1, source_target_pairs={{0,128},{16,144},{2,130},{18,146},{4,132},{20,148},{6,134},{22,150... | collective-permute-start | bytes 491528 | tf_op jit(solution)/shard_map/ppermute | solution.py:369
  20.9 5.1 %collective-permute-start.9 = (bf16[4,160,128]{2,1,0:T(8,128)(2,1)S(1)}, bf16[4,160,128]{2,1,0:T(8,128)(2,1)S(1)}, u32[]{:S(2)}, u32[]{:S(2)}) collective-permute-start(bf16[4,160,128]{2,1,0:T(8,128)(2,1)S(1)} %get-tuple-element.24), channel_id=1, source_target_pairs={{0,192},{16,208},{2,194},{18,210},{4,196},{20,212},{6,198},{22,214... | collective-permute-start | bytes 491528 | tf_op jit(solution)/shard_map/ppermute | solution.py:369
  27.0 11.6 %collective-permute-start = (bf16[32,128]{1,0:T(8,128)(2,1)S(1)}, bf16[32,128]{1,0:T(8,128)(2,1)S(1)}, u32[]{:S(2)}, u32[]{:S(2)}) collective-permute-start(bf16[32,128]{1,0:T(8,128)(2,1)S(1)} %pad_maximum_fusion.6), channel_id=1, source_target_pairs={{0,2},{16,18},{2,4},{18,20},{4,6},{20,22},{6,8},{22,24},{8,10},{24... | collective-permute-start | bytes 24584 | tf_op jit(solution)/shard_map/ppermute | solution.py:369
  28.6 9.9 %collective-permute-start.1 = (bf16[32,128]{1,0:T(8,128)(2,1)S(1)}, bf16[32,128]{1,0:T(8,128)(2,1)S(1)}, u32[]{:S(2)}, u32[]{:S(2)}) collective-permute-start(bf16[32,128]{1,0:T(8,128)(2,1)S(1)} %pad_maximum_fusion.6), channel_id=1, source_target_pairs={{0,14},{16,30},{2,0},{18,16},{4,2},{20,18},{6,4},{22,20},{8,6},{24... | collective-permute-start | bytes 24584 | tf_op jit(solution)/shard_map/ppermute | solution.py:369
  32.8 21.1 %collective-permute-start.10 = (bf16[4,3,18,512]{3,2,1,0:T(8,128)(2,1)S(1)}, bf16[4,3,18,512]{3,2,1,0:T(8,128)(2,1)S(1)}, u32[]{:S(2)}, u32[]{:S(2)}) collective-permute-start(bf16[4,3,18,512]{3,2,1,0:T(8,128)(2,1)S(1)} %slice.35), channel_id=1, source_target_pairs={{0,240},{16,0},{32,16},{48,32},{64,48},{80,64},{96,80},{112,96},{1... | collective-permute-start | bytes 663560 | tf_op jit(solution)/shard_map/ppermute | solution.py:357
  36.7 17.8 %collective-permute-start.11 = (bf16[4,9,6,512]{3,2,1,0:T(8,128)(2,1)S(1)}, bf16[4,9,6,512]{3,2,1,0:T(8,128)(2,1)S(1)}, u32[]{:S(2)}, u32[]{:S(2)}) collective-permute-start(bf16[4,9,6,512]{3,2,1,0:T(8,128)(2,1)S(1)} %slice.36), channel_id=1, source_target_pairs={{0,15},{1,0},{2,1},{3,2},{4,3},{5,4},{6,5},{7,6},{8,7},{9,8},{10,9... | collective-permute-start | bytes 663560 | tf_op jit(solution)/shard_map/ppermute | solution.py:357
  38.6 15.4 %collective-permute-start.2 = (bf16[3,32,128]{2,1,0:T(8,128)(2,1)S(1)}, bf16[3,32,128]{2,1,0:T(8,128)(2,1)S(1)}, u32[]{:S(2)}, u32[]{:S(2)}) collective-permute-start(bf16[3,32,128]{2,1,0:T(8,128)(2,1)S(1)} %pad_maximum_fusion.4), channel_id=1, source_target_pairs={{0,6},{16,22},{2,8},{18,24},{4,10},{20,26},{6,12},{22,28},{8,14},{... | collective-permute-start | bytes 73736 | tf_op jit(solution)/shard_map/ppermute | solution.py:369
  38.7 15.2 %collective-permute-start.12 = (bf16[4,3,6,512]{3,2,1,0:T(8,128)(2,1)S(1)}, bf16[4,3,6,512]{3,2,1,0:T(8,128)(2,1)S(1)}, u32[]{:S(2)}, u32[]{:S(2)}) collective-permute-start(bf16[4,3,6,512]{3,2,1,0:T(8,128)(2,1)S(1)} %slice.37), channel_id=1, source_target_pairs={{0,255},{1,240},{2,241},{3,242},{4,243},{5,244},{6,245},{7,246},{8... | collective-permute-start | bytes 221192 | tf_op jit(solution)/shard_map/ppermute | solution.py:357
  43.1 10.8 %collective-permute-start.3 = (bf16[2,32,128]{2,1,0:T(8,128)(2,1)S(1)}, bf16[2,32,128]{2,1,0:T(8,128)(2,1)S(1)}, u32[]{:S(2)}, u32[]{:S(2)}) collective-permute-start(bf16[2,32,128]{2,1,0:T(8,128)(2,1)S(1)} %pad_maximum_fusion.5), channel_id=1, source_target_pairs={{0,10},{16,26},{2,12},{18,28},{4,14},{20,30},{6,0},{22,16},{8,2},{... | collective-permute-start | bytes 49160 | tf_op jit(solution)/shard_map/ppermute | solution.py:369
  54.6 8.0 %collective-permute-start.13 = (bf16[8,32,128]{2,1,0:T(8,128)(2,1)S(1)}, bf16[8,32,128]{2,1,0:T(8,128)(2,1)S(1)}, u32[]{:S(2)}, u32[]{:S(2)}) collective-permute-start(bf16[8,32,128]{2,1,0:T(8,128)(2,1)S(1)} %constant_dynamic-update-slice_fusion), channel_id=1, source_target_pairs={{0,32},{16,48},{2,34},{18,50},{4,36},{20,52},{6,38},{22,54},{8,40}... | collective-permute-start | bytes 196616 | tf_op jit(solution)/shard_map/ppermute | solution.py:369
  54.7 9.3 %collective-permute-start.14 = (bf16[8,32,128]{2,1,0:T(8,128)(2,1)S(1)}, bf16[8,32,128]{2,1,0:T(8,128)(2,1)S(1)}, u32[]{:S(2)}, u32[]{:S(2)}) collective-permute-start(bf16[8,32,128]{2,1,0:T(8,128)(2,1)S(1)} %constant_dynamic-update-slice_fusion), channel_id=1, source_target_pairs={{0,1},{16,17},{2,3},{18,19},{4,5},{20,21},{6,7},{22,23},{8,9},{24,... | collective-permute-start | bytes 196616 | tf_op jit(solution)/shard_map/ppermute | solution.py:369
  61.6 3.5 %collective-permute-start.15 = (bf16[8,32,128]{2,1,0:T(8,128)(2,1)S(1)}, bf16[8,32,128]{2,1,0:T(8,128)(2,1)S(1)}, u32[]{:S(2)}, u32[]{:S(2)}) collective-permute-start(bf16[8,32,128]{2,1,0:T(8,128)(2,1)S(1)} %constant_dynamic-update-slice_fusion), channel_id=1, source_target_pairs={{0,33},{16,49},{2,35},{18,51},{4,37},{20,53},{6,39},{22,55},{8,41}... | collective-permute-start | bytes 196616 | tf_op jit(solution)/shard_map/ppermute | solution.py:369
  65.2 9.2 %collective-permute-start.16 = (bf16[4,8,32,128]{3,2,1,0:T(8,128)(2,1)S(1)}, bf16[4,8,32,128]{3,2,1,0:T(8,128)(2,1)S(1)}, u32[]{:S(2)}, u32[]{:S(2)}) collective-permute-start(bf16[4,8,32,128]{3,2,1,0:T(8,128)(2,1)S(1)} %pad_maximum_fusion.2.r0), channel_id=1, source_target_pairs={{0,64},{16,80},{2,66},{18,82},{4,68},{20,84},{6,70},{22,86},{8,72}... | collective-permute-start | bytes 786440 | tf_op jit(solution)/shard_map/ppermute | solution.py:369
  66.3 14.1 %collective-permute-start.17 = (bf16[4,8,32,128]{3,2,1,0:T(8,128)(2,1)S(1)}, bf16[4,8,32,128]{3,2,1,0:T(8,128)(2,1)S(1)}, u32[]{:S(2)}, u32[]{:S(2)}) collective-permute-start(bf16[4,8,32,128]{3,2,1,0:T(8,128)(2,1)S(1)} %pad_maximum_fusion.2.r0), channel_id=1, source_target_pairs={{0,128},{16,144},{2,130},{18,146},{4,132},{20,148},{6,134},{22,150... | collective-permute-start | bytes 786440 | tf_op jit(solution)/shard_map/ppermute | solution.py:369
  68.1 12.7 %collective-permute-start.18 = (bf16[4,8,32,128]{3,2,1,0:T(8,128)(2,1)S(1)}, bf16[4,8,32,128]{3,2,1,0:T(8,128)(2,1)S(1)}, u32[]{:S(2)}, u32[]{:S(2)}) collective-permute-start(bf16[4,8,32,128]{3,2,1,0:T(8,128)(2,1)S(1)} %pad_maximum_fusion.2.r0), channel_id=1, source_target_pairs={{0,192},{16,208},{2,194},{18,210},{4,196},{20,212},{6,198},{22,214... | collective-permute-start | bytes 786440 | tf_op jit(solution)/shard_map/ppermute | solution.py:369
  81.0 2.8 %collective-permute-start.20 = (bf16[3,4,8,32,128]{4,3,2,1,0:T(8,128)(2,1)S(1)}, bf16[3,4,8,32,128]{4,3,2,1,0:T(8,128)(2,1)S(1)}, u32[]{:S(2)}, u32[]{:S(2)}) collective-permute-start(bf16[3,4,8,32,128]{4,3,2,1,0:T(8,128)(2,1)S(1)} %pad_maximum_fusion.r1), channel_id=1, source_target_pairs={{0,16},{16,0},{2,18},{18,2},{4,20},{20,4},{6,22},{22,6},{8,24},{24... | collective-permute-start | bytes 2359304 | tf_op jit(solution)/shard_map/ppermute | solution.py:369
  95.0 15.5 %collective-permute-start.22 = (bf16[4,3,18,512]{3,2,1,0:T(8,128)(2,1)S(1)}, bf16[4,3,18,512]{3,2,1,0:T(8,128)(2,1)S(1)}, u32[]{:S(2)}, u32[]{:S(2)}) collective-permute-start(bf16[4,3,18,512]{3,2,1,0:T(8,128)(2,1)S(1)} %slice.43), channel_id=1, source_target_pairs={{0,16},{16,32},{32,48},{48,64},{64,80},{80,96},{96,112},{112,128},... | collective-permute-start | bytes 663560 | tf_op jit(solution)/shard_map/ppermute | solution.py:357
  96.1 14.3 %collective-permute-start.23 = (bf16[4,9,6,512]{3,2,1,0:T(8,128)(2,1)S(1)}, bf16[4,9,6,512]{3,2,1,0:T(8,128)(2,1)S(1)}, u32[]{:S(2)}, u32[]{:S(2)}) collective-permute-start(bf16[4,9,6,512]{3,2,1,0:T(8,128)(2,1)S(1)} %slice.44), channel_id=1, source_target_pairs={{0,1},{1,2},{2,3},{3,4},{4,5},{5,6},{6,7},{7,8},{8,9},{9,10},{10,1... | collective-permute-start | bytes 663560 | tf_op jit(solution)/shard_map/ppermute | solution.py:357
  98.4 12.1 %collective-permute-start.21 = (bf16[4,3,6,512]{3,2,1,0:T(8,128)(2,1)S(1)}, bf16[4,3,6,512]{3,2,1,0:T(8,128)(2,1)S(1)}, u32[]{:S(2)}, u32[]{:S(2)}) collective-permute-start(bf16[4,3,6,512]{3,2,1,0:T(8,128)(2,1)S(1)} %slice.42), channel_id=1, source_target_pairs={{0,17},{1,18},{2,19},{3,20},{4,21},{5,22},{6,23},{7,24},{8,25},{9,... | collective-permute-start | bytes 221192 | tf_op jit(solution)/shard_map/ppermute | solution.py:357
  (15 other events, 170.6 us)
Sparse Core Ops, SparseCore 0:
  27.0 74.5 all-gather.2

commit v3 on v2

--- a/solution.py
+++ b/solution.py
@@ -32,6 +32,10 @@
             for c in range(COLS):
                 out[(c // WO) * WIN + (l * WA + r) * WO + c % WO, (l * WA + r) * COLS + c] = 1
     return out
+
+
+def level_windows():
+    return window_from_natural().reshape(2, WL, WIN // 2, WL, WIN)[:, 0, :, 0].reshape(WIN, WIN)
 
 
 def merged_from_natural():
@@ -90,11 +94,6 @@
     w_ref[rows, 3 * C + group * 128 : 3 * C + (group + 1) * 128] = jnp.concatenate([b[:, 96:] for b in blocks], axis=1)
 
 
-def slots_of(place_ref, x, yl):
-    px, py = place_ref[0], place_ref[1]
-    return lax.rem(px - x + 4, 4), [lax.rem(py - (2 * yh + yl) + 4, 4) for yh in range(2)]
-
-
 def unpack_encoder(place_ref, raws, w_ref):
     px, py, pz, me = (place_ref[i] for i in range(4))
     for side in range(2):
@@ -104,40 +103,55 @@
             x = lax.rem(px - slot + 4, 4)
             raw = near if slot == 0 else far.at[slot - 1]
             for yl in range(2):
-                _, ys = slots_of(place_ref, 0, yl)
+                ys = [lax.rem(py - (2 * yh + yl) + 4, 4) for yh in range(2)]
                 rows = pl.ds(pl.multiple_of((x * 4 + yl * 2 + core) * 32, 32), 32)
                 for group in range(4):
                     blocks = [raw[ys[j % 2], lax.rem(2 * group + j // 2 - pz + 12, 8)] for j in range(4)]
                     put_attention(w_ref, rows, group, blocks)
 
 
-def unpack_decoder(place_ref, raw_ref, w_ref):
-    for x in range(4):
-        for yl in range(2):
-            sx, ys = slots_of(place_ref, x, yl)
-            for core in range(2):
-                first = (x * 4 + yl * 2 + core) * 32
-                for group in range(4):
-                    blocks = [raw_ref[2 * group + j // 2, core, sx, ys[j % 2]] for j in range(4)]
-                    put_attention(w_ref, slice(first, first + 32), group, blocks)
-
-
-def encode_kernel(place_ref, x_ref, gain_ref, r0, r1, r2, r3, to_win_ref, from_win_ref, out_ref, w_ref, qkv_ref, mixed_ref):
-    step = pl.program_id(0)
-
-    @pl.when(step == 0)
-    def _():
-        unpack_encoder(place_ref, (r0, r1, r2, r3), w_ref)
-
-    pair, band = step // 2, step % 2
+def unpack_decoder(raw_ref, w_ref, x):
+    for yl in range(2):
+        sx, ys = x, (yl, 2 + yl)
+        for core in range(2):
+            rows = pl.ds(pl.multiple_of((x * 4 + yl * 2 + core) * 32, 32), 32)
+            for group in range(4):
+                blocks = [raw_ref[2 * group + j // 2, core, sx, ys[j % 2]] for j in range(4)]
+                put_attention(w_ref, rows, group, blocks)
+
+
+def to_windows(level_ref, first, second):
+    first, second = dot(level_ref[...], first), dot(level_ref[...], second)
+    half = WIN // 2
+    return jnp.concatenate([first[:half], second[:half], first[half:], second[half:]], axis=0)
+
+
+def from_windows(level_ref, values):
+    half = WIN // 2
+    first = jnp.concatenate([values[:half], values[WIN : WIN + half]], axis=0).astype(jnp.bfloat16)
+    second = jnp.concatenate([values[half:WIN], values[WIN + half :]], axis=0).astype(jnp.bfloat16)
+    return dot(level_ref[...], first), dot(level_ref[...], second)
+
+
+def encode_kernel(band, place_ref, x_ref, gain_ref, to_win_ref, from_win_ref, *refs):
+    pair = pl.program_id(0)
+    if band == 1:
+        *raws, out_ref, w_ref, qkv_ref, mixed_ref = refs
+
+        @pl.when(pair == 0)
+        def _():
+            unpack_encoder(place_ref, raws, w_ref)
+    else:
+        w_ref, out_ref, qkv_ref, mixed_ref = refs
+
     upper, lower = 2 * pair + 1, (2 * pair + 2) % LEV
-    x = jnp.concatenate([x_ref[upper, band], x_ref[lower, band]], axis=0).astype(jnp.float32)
-    h = normed(x, gain_ref[...]).astype(jnp.bfloat16)
-    h = dot(to_win_ref[...], h).astype(jnp.bfloat16)
+    x = [x_ref[level].astype(jnp.float32) for level in (upper, lower)]
+    h = [normed(level, gain_ref[...]).astype(jnp.bfloat16) for level in x]
+    h = to_windows(to_win_ref, *h).astype(jnp.bfloat16)
     for third in range(3):
         qkv_ref[:, third * C : (third + 1) * C] = dot(h, w_ref[:, third * C : (third + 1) * C]).astype(jnp.bfloat16)
     by_level = (pair == 1).astype(jnp.int32)
-    by_row = jnp.where(band == 1, place_ref[4], 0)
+    by_row = place_ref[4] if band == 1 else 0
 
     def label(dim):
         index = lax.broadcasted_iota(jnp.int32, (WIN, WIN), dim)
@@ -148,15 +162,26 @@
     same = label(0) == label(1)
     for window in range(2):
         window_attention(qkv_ref, mixed_ref, window * WIN, same)
-    y = dot(mixed_ref[...], w_ref[:, 3 * C :]).astype(jnp.bfloat16)
-    y = dot(from_win_ref[...], y)
-    out = (x + y).astype(jnp.bfloat16)
-    out_ref[upper, band] = out[:WIN]
-    out_ref[lower, band] = out[WIN:]
+    y = from_windows(from_win_ref, dot(mixed_ref[...], w_ref[:, 3 * C :]))
+    out_ref[upper] = (x[0] + y[0]).astype(jnp.bfloat16)
+    out_ref[lower] = (x[1] + y[1]).astype(jnp.bfloat16)
 
 
 def merge_split_kernel(
-    place_ref, x_ref, mgain_ref, sgain_ref, wm_ref, ws_ref, to_merged_ref, out_ref, quads_ref, skip_ref, middle_ref, w_ref, w2_ref
+    x_ref,
+    mgain_ref,
+    sgain_ref,
+    wm_ref,
+    ws_ref,
+    wd_ref,
+    to_merged_ref,
+    out_ref,
+    dec_ref,
+    quads_ref,
+    skip_ref,
+    middle_ref,
+    w_ref,
+    w2_ref,
 ):
     step = pl.program_id(0)
     quarter = BAND // 4
@@ -183,7 +208,7 @@
     def _():
         for x in range(4):
             for yl in range(2):
-                sx, ys = slots_of(place_ref, x, yl)
+                sx, ys = x, (yl, 2 + yl)
                 for core in range(2):
                     first = (x * 4 + yl * 2 + core) * 128
                     for z in range(2):
@@ -199,7 +224,7 @@
         width = middle_ref.shape[-1]
         for x in range(4):
             for yl in range(2):
-                sx, ys = slots_of(place_ref, x, yl)
+                sx, ys = x, (yl, 2 + yl)
                 for core in range(2):
                     first = (x * 4 + yl * 2 + core) * 64
                     for z in range(2):
@@ -209,19 +234,14 @@
         total = dot(middle_ref[0], w2_ref[:width])
         for chunk in range(1, 4):
             total += dot(middle_ref[chunk], w2_ref[chunk * width : (chunk + 1) * width])
+        unpack_decoder(wd_ref, dec_ref, part)
         kept = (part % 2) * 2 + part // 2
         joined = (normed(total, sgain_ref[...]) + skip_ref[kept]).astype(jnp.bfloat16)
         out_ref[0] = joined
 
 
-def decode_kernel(place_ref, x_ref, gain_ref, raw_ref, to_win_ref, from_win_ref, out_ref, w_ref, qkv_ref, mixed_ref):
+def decode_kernel(x_ref, gain_ref, w_ref, to_win_ref, from_win_ref, out_ref, qkv_ref, mixed_ref):
     step = pl.program_id(0)
-
-    @pl.when(step == 0)
-    def _():
-        unpack_decoder(place_ref, raw_ref, w_ref)
-
-
     pair, band = step // 2, step % 2
     quarter = BAND // 4
     x = jnp.concatenate([x_ref[part, step].astype(jnp.float32) for part in range(4)], axis=0).astype(jnp.bfloat16)
@@ -232,10 +252,9 @@
     for window in range(2):
         window_attention(qkv_ref, mixed_ref, window * WIN, None)
     y = dot(mixed_ref[...], w_ref[:, 3 * C :]).astype(jnp.bfloat16)
-    out = (x + y.astype(jnp.float32)).astype(jnp.bfloat16)
-    out = dot(from_win_ref[...], out).astype(jnp.bfloat16)
-    out_ref[2 * pair, band] = out[:WIN]
-    out_ref[2 * pair + 1, band] = out[WIN:]
+    first, second = from_windows(from_win_ref, x + y.astype(jnp.float32))
+    out_ref[2 * pair, band] = first.astype(jnp.bfloat16)
+    out_ref[2 * pair + 1, band] = second.astype(jnp.bfloat16)
 
 
 def whole(shape):
@@ -245,52 +264,66 @@
 PARAMS = pltpu.CompilerParams(vmem_limit_bytes=VMEM_LIMIT)
 
 
-def encode(framed, gain, weights, place):
-    to_win = window_from_natural()
-    shape = (LEV, 2, WIN, C)
+def encode(band, framed, gain, weights, place):
+    to_win = level_windows()
+    shape = (LEV, WIN, C)
+    out_shapes, out_specs = [jax.ShapeDtypeStruct(shape, jnp.bfloat16)], [whole(shape)]
+    if band == 1:
+        out_shapes.append(jax.ShapeDtypeStruct((C, 4 * C), jnp.bfloat16))
+        out_specs.append(whole((C, 4 * C)))
     return pl.pallas_call(
-        encode_kernel,
-        grid=(4,),
+        functools.partial(encode_kernel, band),
+        grid=(2,),
         in_specs=[
             pl.BlockSpec(memory_space=pltpu.SMEM),
             whole(shape),
             whole((1, C)),
+            whole((WIN, WIN)),
+            whole((WIN, WIN)),
             *[whole(raw.shape) for raw in weights],
-            whole((BAND, BAND)),
-            whole((BAND, BAND)),
-        ],
-        out_specs=whole(shape),
-        out_shape=jax.ShapeDtypeStruct(shape, jnp.bfloat16),
-        scratch_shapes=[
-            pltpu.VMEM((C, 4 * C), jnp.bfloat16),
-            pltpu.VMEM((BAND, 3 * C), jnp.bfloat16),
-            pltpu.VMEM((BAND, C), jnp.bfloat16),
-        ],
+        ],
+        out_specs=out_specs,
+        out_shape=out_shapes,
+        scratch_shapes=[pltpu.VMEM((BAND, 3 * C), jnp.bfloat16), pltpu.VMEM((BAND, C), jnp.bfloat16)],
         compiler_params=PARAMS,
-        name="encode",
-    )(place, framed, gain.reshape(1, C), *weights, jnp.asarray(to_win, jnp.bfloat16), jnp.asarray(to_win.T, jnp.bfloat16))
-
-
-def merge_split(encoded, mgain, sgain, raw, place):
+        cost_estimate=pl.CostEstimate(flops=2 * 10**9, bytes_accessed=4 * 10**6, transcendentals=700_000),
+        name=f"encode_band{band}",
+    )(
+        place,
+        framed.reshape(shape),
+        gain.reshape(1, C),
+        jnp.asarray(to_win, jnp.bfloat16),
+        jnp.asarray(to_win.T, jnp.bfloat16),
+        *weights,
+    )
+
+
+def merge_split(encoded, mgain, sgain, raw):
     to_merged = merged_from_natural()
     tokens = LEV * ROWS * COLS // 4
     return pl.pallas_call(
         merge_split_kernel,
         grid=(8,),
         in_specs=[
-            pl.BlockSpec(memory_space=pltpu.SMEM),
             whole((LEV, 2, WIN, C)),
             whole((1, 4 * C)),
             whole((1, C)),
             pl.BlockSpec((2, 2, 4, 4, 64, 128), lambda i: (jnp.minimum(i, 3), 0, 0, 0, 0, 0)),
             pl.BlockSpec((2, 2, 4, 4, 64, 128), lambda i: (jnp.maximum(i - 4, 0), 0, 0, 0, 1, 0)),
+            pl.BlockSpec((8, 2, 4, 4, 32, 128), lambda i: (0, 0, 0, 0, 4, 0)),
             whole((BAND, BAND)),
         ],
-        out_specs=pl.BlockSpec(
-            (1, tokens, C),
-            lambda i: ((jnp.maximum(i - 4, 0) % 2) * 2 + jnp.maximum(i - 4, 0) // 2, 0, 0),
-        ),
-        out_shape=jax.ShapeDtypeStruct((4, tokens, C), jnp.bfloat16),
+        out_specs=[
+            pl.BlockSpec(
+                (1, tokens, C),
+                lambda i: ((jnp.maximum(i - 4, 0) % 2) * 2 + jnp.maximum(i - 4, 0) // 2, 0, 0),
+            ),
+            whole((C, 4 * C)),
+        ],
+        out_shape=[
+            jax.ShapeDtypeStruct((4, tokens, C), jnp.bfloat16),
+            jax.ShapeDtypeStruct((C, 4 * C), jnp.bfloat16),
+        ],
         scratch_shapes=[
             pltpu.VMEM((tokens, 4 * C), jnp.bfloat16),
             pltpu.VMEM((4, tokens, C), jnp.float32),
@@ -301,17 +334,17 @@
         compiler_params=PARAMS,
         name="merge_split",
     )(
-        place,
         encoded,
         mgain.reshape(1, 4 * C),
         sgain.reshape(1, C),
         raw,
         raw,
+        raw,
         jnp.asarray(to_merged, jnp.bfloat16),
     )
 
 
-def decode(joined, gain, weights, place):
+def decode(joined, gain, weights):
     to_win = window_from_natural()
     from_merged = to_win @ merged_from_natural().T
     shape = (LEV, 2, WIN, C)
@@ -319,29 +352,26 @@
         decode_kernel,
         grid=(4,),
         in_specs=[
-            pl.BlockSpec(memory_space=pltpu.SMEM),
             whole((4, 4, BAND // 4, C)),
             whole((1, C)),
-            pl.BlockSpec((8, 2, 4, 4, 32, 128), lambda i: (0, 0, 0, 0, 4, 0)),
+            whole((C, 4 * C)),
             whole((BAND, BAND)),
-            whole((BAND, BAND)),
+            whole((WIN, WIN)),
         ],
         out_specs=whole(shape),
         out_shape=jax.ShapeDtypeStruct(shape, jnp.bfloat16),
         scratch_shapes=[
-            pltpu.VMEM((C, 4 * C), jnp.bfloat16),
             pltpu.VMEM((BAND, 3 * C), jnp.bfloat16),
             pltpu.VMEM((BAND, C), jnp.bfloat16),
         ],
         compiler_params=PARAMS,
         name="decode",
     )(
-        place,
         joined.reshape(4, 4, BAND // 4, C),
         gain.reshape(1, C),
         weights,
         jnp.asarray(from_merged, jnp.bfloat16),
-        jnp.asarray(to_win.T, jnp.bfloat16),
+        jnp.asarray(level_windows().T, jnp.bfloat16),
     )
 
 
@@ -379,6 +409,15 @@
 
 def from_z(value, steps):
     return sent(value, lambda x, y, z, c: (x, y, (z + steps) % 8, c))
+
+
+def x_and_y(value):
+    groups = [
+        [device_index(x, y, z, core) for x in range(4) for y in range(4)] for z in range(8) for core in range(2)
+    ]
+    blocks = jnp.broadcast_to(value[None], (16,) + value.shape)
+    blocks = lax.all_to_all(blocks, ("lat", "lon"), 0, 0, tiled=True, axis_index_groups=groups)
+    return blocks.reshape((4, 4) + value.shape)
 
 
 def z_and_cores(value):
@@ -424,43 +463,34 @@
         axis=0,
     )
 
-    later_y = from_y(later_share)
+    later = x_and_y(later_share)
     enc_near = [from_z(enc_share, 1), from_z(enc_share, -1)]
-    later_near = jnp.stack([later_share, *later_y])
-    later_x = from_x(later_near)
     enc_three = jnp.stack([enc_near[0], enc_share, enc_near[1]])
-    enc_far = [from_z(enc_three, 3), from_z(enc_three[:2], -3)]
-    tokens_sent, later_x = together(tokens, later_x)
-    later_raw = z_and_cores(jnp.stack([later_near, *later_x])).reshape(8, 2, 4, 4, 160, 128)
-    below = passed_along(tokens_sent[:, :half_lat, half_lon:], "lat", -1)
-    beyond = passed_along(tokens_sent[:, half_lat:, :half_lon], "lon", -1)
-    corner = passed_along(tokens_sent[:, :half_lat, :half_lon], ("lat", "lon"), -1)
-    enc_far, below, beyond, corner = together(enc_far, below, beyond, corner)
+    tokens_sent, enc_three = together(tokens[:, :half_lat], enc_three)
+    enc_far, below, later = together(
+        [from_z(enc_three, 3), from_z(enc_three[:2], -3)], passed_along(tokens_sent, "lat", -1), later
+    )
+    later_raw = z_and_cores(later).reshape(8, 2, 4, 4, 160, 128)
     enc_z = jnp.concatenate([enc_far[0], enc_three, enc_far[1]], axis=0)
-    enc_y = jnp.stack([enc_z, *from_y(enc_z)])
+    edge = jnp.concatenate([tokens[:, half_lat:, :half_lon], below[:, :, :half_lon]], axis=1)
+    enc_y, beyond = together(from_y(enc_z), passed_along(edge, "lon", -1))
+    enc_y = jnp.stack([enc_z, *enc_y])
     enc_x = jnp.stack(from_x(enc_y))
     enc_raw = [enc_y, enc_x, other_core(enc_y), other_core(enc_x)]
     framed = jnp.concatenate(
-        [
-            jnp.concatenate([tokens[:, half_lat:, half_lon:], beyond], axis=2),
-            jnp.concatenate([below, corner], axis=2),
-        ],
-        axis=1,
-    )
-    moved = encode(framed.reshape(LEV, 2, WIN, C), enc_gain, enc_raw, place).reshape(LEV, ROWS, COLS, C)
-    cut_r, cut_c = ROWS - half_lat, COLS - half_lon
-    above = passed_along(moved[:, cut_r:, :cut_c], "lat", 1)
-    left = passed_along(moved[:, :cut_r, cut_c:], "lon", 1)
-    corner = passed_along(moved[:, cut_r:, cut_c:], ("lat", "lon"), 1)
-    encoded = jnp.concatenate(
-        [
-            jnp.concatenate([corner, above], axis=2),
-            jnp.concatenate([left, moved[:, :cut_r, :cut_c]], axis=2),
-        ],
-        axis=1,
-    )
-    joined = merge_split(encoded.reshape(LEV, 2, WIN, C), merge_gain, split_gain, later_raw, place)
-    return decode(joined, dec_gain, later_raw, place).reshape(LEV, ROWS, COLS, C)
+        [jnp.concatenate([tokens[:, half_lat + WA :], below], axis=1)[:, :, half_lon:], beyond[:, WA:]], axis=2
+    )
+    second, enc_w = encode(1, framed, enc_gain, enc_raw, place)
+    second = second.reshape(LEV, WA, COLS, C)
+    above = passed_along(second[:, WA - half_lat :], "lat", 1)
+    framed = jnp.concatenate([tokens[:, half_lat : half_lat + WA, half_lon:], beyond[:, :WA]], axis=2)
+    (first,) = encode(0, framed, enc_gain, [enc_w], place)
+    first = first.reshape(LEV, WA, COLS, C)
+    rows = jnp.concatenate([above, first, second[:, : WA - half_lat]], axis=1)
+    left = passed_along(rows[:, :, COLS - half_lon :], "lon", 1)
+    encoded = jnp.concatenate([left, rows[:, :, : COLS - half_lon]], axis=2)
+    joined, dec_w = merge_split(encoded.reshape(LEV, 2, WIN, C), merge_gain, split_gain, later_raw)
+    return decode(joined, dec_gain, dec_w).reshape(LEV, ROWS, COLS, C)
 
 
 def solution(mesh):

time: 143 us -> 139 us (0.972)
  starting transfers between devices: 44.3 us -> 36.1 us
  waiting for transfers between devices: 41.7 us -> 46.3 us
  local copies, waits for them, and re-layouts: 2.51 us -> 5.36 us
  Pallas kernels: 34.9 us -> 32.3 us
  other arithmetic: 4.72 us -> 3.11 us
    ppermute x6 -> x4, waiting for transfers between devices: 11.7 us -> 24.9 us  [passed_along(): return lax.ppermute(value, axis, pairs)]
    ppermute x18 -> x12, starting transfers between devices: 30.5 us -> 20.3 us  [sent(): lax.ppermute(value, ('lat', 'lon'), [(device_index(*at), device_index(*to...]
    ppermute x18 -> x12, waiting for transfers between devices: 29.9 us -> 21.3 us  [sent(): lax.ppermute(value, ('lat', 'lon'), [(device_index(*at), device_index(*to...]
    all_to_all x0 -> x1, starting transfers between devices: none -> 6.89 us  [x_and_y(): lax.all_to_all(blocks, ('lat', 'lon'), 0, 0, tiled=True, axis_index_group...]
    ppermute x6 -> x4, starting transfers between devices: 13.8 us -> 8.92 us  [passed_along(): return lax.ppermute(value, axis, pairs)]
    pallas_call x3 -> x4, Pallas kernels: 34.9 us -> 32.3 us  [the longest x1 11.1 us: merge_split(): pl.pallas_call(merge_split_kernel, grid=(8,), in_specs=[whole((LEV, 2, WI...]
    another operation x4 -> x1, other arithmetic: 1.82 us -> 0.04 us  [shards(): enc_y = jnp.stack([enc_z, *enc_y])]
    slice x8 -> x7, local copies, waits for them, and re-layouts: 0.64 us -> 2.38 us  [the longest x1 1.22 us: shards(): tokens[:, half_lat:half_lat + WA, half_lon:]]
  transfers between devices with their start and end apart: 25 -> 18, of which waited for: 13 -> 10; matrix products, arithmetic and copies ran while one was open for 3% -> 5% of each run, Pallas kernels for 8% -> 8%
where the time goes in v3:
time: 139 us; the launch traced here: 137 us
  waiting for transfers between devices  46.3 us (33%)
  starting transfers between devices  36.1 us (26%)
  Pallas kernels  32.3 us (23%)
  between operations  13.8 us (10%)
  local copies, waits for them, and re-layouts  5.36 us (4%)
  other arithmetic  3.11 us (2%)
    ppermute x4, waiting for transfers between devices, passed_along(): return lax.ppermute(value, axis, pairs)  24.9 us
    ppermute x12, waiting for transfers between devices, sent(): lax.ppermute(value, ('lat', 'lon'), [(device_index(*at), device_index(*to...  21.3 us
    ppermute x12, starting transfers between devices, sent(): lax.ppermute(value, ('lat', 'lon'), [(device_index(*at), device_index(*to...  20.3 us
    pallas_call x1, Pallas kernels, merge_split(): pl.pallas_call(merge_split_kernel, grid=(8,), in_specs=[whole((LEV, 2, WI...  11.1 us
    pallas_call x2, Pallas kernels, encode(): pl.pallas_call(functools.partial(encode_kernel, band), grid=(2,), in_spec...  10.9 us
    pallas_call x1, Pallas kernels, decode(): pl.pallas_call(decode_kernel, grid=(4,), in_specs=[whole((4, 4, BAND // 4...  10.3 us
    ppermute x4, starting transfers between devices, passed_along(): return lax.ppermute(value, axis, pairs)  8.92 us
    all_to_all x1, starting transfers between devices, x_and_y(): lax.all_to_all(blocks, ('lat', 'lon'), 0, 0, tiled=True, axis_index_group...  6.89 us
  transfers between devices with their start and end apart: 18, of which 10 were waited for; matrix products, arithmetic and copies ran while one was open for 5% of the time, Pallas kernels for 8%

profile of v3, /device:TPU:1, one launch (start us, length us, event | category | flops | bytes accessed | tf_op | source)
XLA Modules:
  0.0 136.9 jit_solution(17450800975873919912)
XLA Ops:
  7.4 2.5 %collective-permute-start = (bf16[32,128]{1,0:T(8,128)(2,1)S(1)}, bf16[32,128]{1,0:T(8,128)(2,1)S(1)}, u32[]{:S(2)}, u32[]{:S(2)}) collective-permute-start(bf16[32,128]{1,0:T(8,128)(2,1)S(1)} %pad_maximum_fusion.9), channel_id=1, source_target_pairs={{0,2},{16,18},{2,4},{18,20},{4,6},{20,22},{6,8},{22,24},{8,10},{24... | collective-permute-start | bytes 24584 | tf_op jit(solution)/shard_map/ppermute | solution.py:399
  9.9 4.0 %collective-permute-start.1 = (bf16[32,128]{1,0:T(8,128)(2,1)S(1)}, bf16[32,128]{1,0:T(8,128)(2,1)S(1)}, u32[]{:S(2)}, u32[]{:S(2)}) collective-permute-start(bf16[32,128]{1,0:T(8,128)(2,1)S(1)} %pad_maximum_fusion.9), channel_id=1, source_target_pairs={{0,14},{16,30},{2,0},{18,16},{4,2},{20,18},{6,4},{22,20},{8,6},{24... | collective-permute-start | bytes 24584 | tf_op jit(solution)/shard_map/ppermute | solution.py:399
  16.8 6.9 %all-to-all-start = ((bf16[16,160,128]{2,1,0:T(8,128)(2,1)}), bf16[16,160,128]{2,1,0:T(8,128)(2,1)S(1)}, u32[]{:S(2)}, u32[]{:S(2)}) async-start(bf16[16,160,128]{2,1,0:T(8,128)(2,1)} %broadcast_in_dim.2), calls=%async_computation | async-start | bytes 1310720 | tf_op jit(solution)/shard_map/all_to_all | solution.py:419
  23.9 1.3 collective-permute-start.4
  25.2 1.5 %collective-permute-start.2 = (bf16[3,32,128]{2,1,0:T(8,128)(2,1)S(1)}, bf16[3,32,128]{2,1,0:T(8,128)(2,1)S(1)}, u32[]{:S(2)}, u32[]{:S(2)}) collective-permute-start(bf16[3,32,128]{2,1,0:T(8,128)(2,1)S(1)} %pad_maximum_fusion.8), channel_id=1, source_target_pairs={{0,6},{16,22},{2,8},{18,24},{4,10},{20,26},{6,12},{22,28},{8,14},{... | collective-permute-start | bytes 73736 | tf_op jit(solution)/shard_map/ppermute | solution.py:399
  26.7 2.9 %collective-permute-start.3 = (bf16[2,32,128]{2,1,0:T(8,128)(2,1)S(1)}, bf16[2,32,128]{2,1,0:T(8,128)(2,1)S(1)}, u32[]{:S(2)}, u32[]{:S(2)}) collective-permute-start(bf16[2,32,128]{2,1,0:T(8,128)(2,1)S(1)} %slice.47), channel_id=1, source_target_pairs={{0,10},{16,26},{2,12},{18,28},{4,14},{20,30},{6,0},{22,16},{8,2},{... | collective-permute-start | bytes 49160 | tf_op jit(solution)/shard_map/ppermute | solution.py:399
  29.7 1.4 %collective-permute-done.3 = bf16[2,32,128]{2,1,0:T(8,128)(2,1)S(1)} collective-permute-done((bf16[2,32,128]{2,1,0:T(8,128)(2,1)S(1)}, bf16[2,32,128]{2,1,0:T(8,128)(2,1)S(1)}, u32[]{:S(2)}, u32[]{:S(2)}) %collective-permute-start.3) | collective-permute-done | bytes 16416 | tf_op jit(solution)/shard_map/ppermute | solution.py:399
  31.1 6.1 %collective-permute-done.4 = bf16[4,3,24,512]{3,2,1,0:T(8,128)(2,1)S(1)} collective-permute-done((bf16[4,3,24,512]{3,2,1,0:T(8,128)(2,1)S(1)}, bf16[4,3,24,512]{3,2,1,0:T(8,128)(2,1)S(1)}, u32[]{:S(2)}, u32[]{:S(2)}) %collective-permute-start.4) | collective-permute-done | bytes 294944 | tf_op jit(solution)/shard_map/ppermute | solution.py:387
  38.2 3.6 %collective-permute-start.8 = (bf16[4,12,6,512]{3,2,1,0:T(8,128)(2,1)S(1)}, bf16[4,12,6,512]{3,2,1,0:T(8,128)(2,1)S(1)}, u32[]{:S(2)}, u32[]{:S(2)}) collective-permute-start(bf16[4,12,6,512]{3,2,1,0:T(8,128)(2,1)S(1)} %pad_maximum_fusion.6), channel_id=1, source_target_pairs={{0,15},{1,0},{2,1},{3,2},{4,3},{5,4},{6,5},{7,6},{8,7},{9,8},{10,9... | collective-permute-start | bytes 884744 | tf_op jit(solution)/shard_map/ppermute | solution.py:387
  41.8 1.3 collective-permute-start.5
  43.1 2.5 %collective-permute-start.7 = (bf16[8,32,128]{2,1,0:T(8,128)(2,1)S(1)}, bf16[8,32,128]{2,1,0:T(8,128)(2,1)S(1)}, u32[]{:S(2)}, u32[]{:S(2)}) collective-permute-start(bf16[8,32,128]{2,1,0:T(8,128)(2,1)S(1)} %constant_dynamic-update-slice_fusion), channel_id=1, source_target_pairs={{0,33},{16,49},{2,35},{18,51},{4,37},{20,53},{6,39},{22,55},{8,41}... | collective-permute-start | bytes 196616 | tf_op jit(solution)/shard_map/ppermute | solution.py:399
  45.6 7.4 %collective-permute-done.5 = bf16[8,32,128]{2,1,0:T(8,128)(2,1)S(1)} collective-permute-done((bf16[8,32,128]{2,1,0:T(8,128)(2,1)S(1)}, bf16[8,32,128]{2,1,0:T(8,128)(2,1)S(1)}, u32[]{:S(2)}, u32[]{:S(2)}) %collective-permute-start.5) | collective-permute-done | bytes 65568 | tf_op jit(solution)/shard_map/ppermute | solution.py:399
  54.7 2.1 %collective-permute-start.10 = (bf16[4,8,32,128]{3,2,1,0:T(8,128)(2,1)S(1)}, bf16[4,8,32,128]{3,2,1,0:T(8,128)(2,1)S(1)}, u32[]{:S(2)}, u32[]{:S(2)}) collective-permute-start(bf16[4,8,32,128]{3,2,1,0:T(8,128)(2,1)S(1)} %pad_maximum_fusion.7.refs_0_), channel_id=1, source_target_pairs={{0,128},{16,144},{2,130},{18,146},{4,132},{20,148},{6,134},{22,150... | collective-permute-start | bytes 786440 | tf_op jit(solution)/shard_map/ppermute | solution.py:399
  56.8 1.5 %collective-permute-start.11 = (bf16[4,8,32,128]{3,2,1,0:T(8,128)(2,1)S(1)}, bf16[4,8,32,128]{3,2,1,0:T(8,128)(2,1)S(1)}, u32[]{:S(2)}, u32[]{:S(2)}) collective-permute-start(bf16[4,8,32,128]{3,2,1,0:T(8,128)(2,1)S(1)} %pad_maximum_fusion.7.refs_0_), channel_id=1, source_target_pairs={{0,192},{16,208},{2,194},{18,210},{4,196},{20,212},{6,198},{22,214... | collective-permute-start | bytes 786440 | tf_op jit(solution)/shard_map/ppermute | solution.py:399
  58.2 5.6 %collective-permute-done.9 = bf16[4,8,32,128]{3,2,1,0:T(8,128)(2,1)S(1)} collective-permute-done((bf16[4,8,32,128]{3,2,1,0:T(8,128)(2,1)S(1)}, bf16[4,8,32,128]{3,2,1,0:T(8,128)(2,1)S(1)}, u32[]{:S(2)}, u32[]{:S(2)}) %collective-permute-start.9) | collective-permute-done | bytes 262176 | tf_op jit(solution)/shard_map/ppermute | solution.py:399
  63.8 4.6 %collective-permute-done.10 = bf16[4,8,32,128]{3,2,1,0:T(8,128)(2,1)S(1)} collective-permute-done((bf16[4,8,32,128]{3,2,1,0:T(8,128)(2,1)S(1)}, bf16[4,8,32,128]{3,2,1,0:T(8,128)(2,1)S(1)}, u32[]{:S(2)}, u32[]{:S(2)}) %collective-permute-start.10) | collective-permute-done | bytes 262176 | tf_op jit(solution)/shard_map/ppermute | solution.py:399
  69.4 1.4 %collective-permute-start.13 = (bf16[3,4,8,32,128]{4,3,2,1,0:T(8,128)(2,1)S(1)}, bf16[3,4,8,32,128]{4,3,2,1,0:T(8,128)(2,1)S(1)}, u32[]{:S(2)}, u32[]{:S(2)}) collective-permute-start(bf16[3,4,8,32,128]{4,3,2,1,0:T(8,128)(2,1)S(1)} %pad_maximum_fusion.2.refs_1_), channel_id=1, source_target_pairs={{0,16},{16,0},{2,18},{18,2},{4,20},{20,4},{6,22},{22,6},{8,24},{24... | collective-permute-start | bytes 2359304 | tf_op jit(solution)/shard_map/ppermute | solution.py:399
  70.8 1.2 slice.55
  73.9 5.9 %encode_band1.1 = (bf16[4,144,512]{2,1,0:T(8,128)(2,1)S(1)}, bf16[512,2048]{1,0:T(8,128)(2,1)S(1)}) custom-call(s32[5]{0:T(128)S(1)} %stack.66.place_ref, bf16[4,144,512]{2,1,0:T(8,128)(2,1)S(1)} %bitcast.34, f32[1,512]{1,0:T(1,128)S(1)} %bitcast.39, bf16[144,144]{1,0:T(8,128)(2,1)S(1)} %copy-done.7, bf16[144,144]{1,0:T(8,128)(2,1)S(1)} %copy-done.2, ...), custom_call_target="tpu_custom_call" | custom-call | flops 2000000000 | bytes 4000000 | tf_op jit(solution)/shard_map/encode_band1/pallas_call | solution.py:274
  80.6 5.0 %encode_band0.1 = bf16[4,144,512]{2,1,0:T(8,128)(2,1)S(1)} custom-call(s32[5]{0:T(128)S(1)} %stack.66.place_ref, bf16[4,144,512]{2,1,0:T(8,128)(2,1)S(1)} %bitcast.35, f32[1,512]{1,0:T(1,128)S(1)} %bitcast.40, bf16[144,144]{1,0:T(8,128)(2,1)S(1)} %copy-done.7, bf16[144,144]{1,0:T(8,128)(2,1)S(1)} %copy-done.2, bf16[512,2048]{1,0:T(8,128)(2,1)S(1)} %get-tuple-element.29.refs_0_), custom_call_target="tpu_custom_call" | custom-call | flops 2000000000 | bytes 4000000 | tf_op jit(solution)/shard_map/encode_band0/pallas_call | solution.py:274
  85.7 3.4 %collective-permute-start.15 = (bf16[4,12,6,512]{3,2,1,0:T(8,128)(2,1)S(1)}, bf16[4,12,6,512]{3,2,1,0:T(8,128)(2,1)S(1)}, u32[]{:S(2)}, u32[]{:S(2)}) collective-permute-start(bf16[4,12,6,512]{3,2,1,0:T(8,128)(2,1)S(1)} %pad_maximum_fusion.5), channel_id=1, source_target_pairs={{0,1},{1,2},{2,3},{3,4},{4,5},{5,6},{6,7},{7,8},{8,9},{9,10},{10,1... | collective-permute-start | bytes 884744 | tf_op jit(solution)/shard_map/ppermute | solution.py:387
  89.1 18.9 %collective-permute-done.15 = bf16[4,12,6,512]{3,2,1,0:T(8,128)(2,1)S(1)} collective-permute-done((bf16[4,12,6,512]{3,2,1,0:T(8,128)(2,1)S(1)}, bf16[4,12,6,512]{3,2,1,0:T(8,128)(2,1)S(1)}, u32[]{:S(2)}, u32[]{:S(2)}) %collective-permute-start.15) | collective-permute-done | bytes 294944 | tf_op jit(solution)/shard_map/ppermute | solution.py:387
  108.6 11.1 %merge_split.1 = (bf16[4,288,512]{2,1,0:T(8,128)(2,1)S(1)}, bf16[512,2048]{1,0:T(8,128)(2,1)S(1)}) custom-call(bf16[4,2,144,512]{3,2,1,0:T(8,128)(2,1)S(1)} %bitcast.29, f32[1,2048]{1,0:T(1,128)S(1)} %bitcast.36, f32[1,512]{1,0:T(1,128)S(1)} %bitcast.37, bf16[8,2,4,4,160,128]{5,4,3,2,1,0:T(8,128)(2,1)} %bitcast.41, ...), custom_call_target="tpu_custom_call" | custom-call | tf_op jit(solution)/shard_map/merge_split/pallas_call | solution.py:304
  119.7 10.3 %decode.1 = bf16[4,2,144,512]{3,2,1,0:T(8,128)(2,1)} custom-call(bf16[4,4,72,512]{3,2,1,0:T(8,128)(2,1)S(1)} %bitcast.32, f32[1,512]{1,0:T(1,128)S(1)} %bitcast.38, bf16[512,2048]{1,0:T(8,128)(2,1)S(1)} %get-tuple-element.32.w_ref, bf16[288,288]{1,0:T(8,128)(2,1)S(1)} %copy-done.1, bf16[144,144]{1,0:T(8,128)(2,1)S(1)} %copy-done.2), custom_call_target="tpu_custom_call" | custom-call | tf_op jit(solution)/shard_map/decode/pallas_call | solution.py:351
  (69 shorter events, 10.7 us)
Async XLA Ops:
  6.5 17.2 %copy-start.9 = (bf16[4,12,24,512]{3,2,1,0:T(8,128)(2,1)S(1)}, bf16[4,12,24,512]{3,2,1,0:T(8,128)(2,1)}, u32[]{:S(2)}) copy-start(bf16[4,12,24,512]{3,2,1,0:T(8,128)(2,1)} %param.18) | copy-start | bytes 3538948
  7.4 16.4 %collective-permute-start = (bf16[32,128]{1,0:T(8,128)(2,1)S(1)}, bf16[32,128]{1,0:T(8,128)(2,1)S(1)}, u32[]{:S(2)}, u32[]{:S(2)}) collective-permute-start(bf16[32,128]{1,0:T(8,128)(2,1)S(1)} %pad_maximum_fusion.9), channel_id=1, source_target_pairs={{0,2},{16,18},{2,4},{18,20},{4,6},{20,22},{6,8},{22,24},{8,10},{24... | collective-permute-start | bytes 24584 | tf_op jit(solution)/shard_map/ppermute | solution.py:399
  9.9 14.0 %collective-permute-start.1 = (bf16[32,128]{1,0:T(8,128)(2,1)S(1)}, bf16[32,128]{1,0:T(8,128)(2,1)S(1)}, u32[]{:S(2)}, u32[]{:S(2)}) collective-permute-start(bf16[32,128]{1,0:T(8,128)(2,1)S(1)} %pad_maximum_fusion.9), channel_id=1, source_target_pairs={{0,14},{16,30},{2,0},{18,16},{4,2},{20,18},{6,4},{22,20},{8,6},{24... | collective-permute-start | bytes 24584 | tf_op jit(solution)/shard_map/ppermute | solution.py:399
  16.8 20.4 %all-to-all-start = ((bf16[16,160,128]{2,1,0:T(8,128)(2,1)}), bf16[16,160,128]{2,1,0:T(8,128)(2,1)S(1)}, u32[]{:S(2)}, u32[]{:S(2)}) async-start(bf16[16,160,128]{2,1,0:T(8,128)(2,1)} %broadcast_in_dim.2), calls=%async_computation | async-start | bytes 1310720 | tf_op jit(solution)/shard_map/all_to_all | solution.py:419
  23.7 84.9 %all-gather.3.cloned.1.call-start = ((), (), s32[]{:S(2)}) async-start(), calls=%async_computation.1 | async-start | bytes 11141120 | tf_op jit(solution)/shard_map/all_gather | solution.py:427
  23.9 13.3 %collective-permute-start.4 = (bf16[4,3,24,512]{3,2,1,0:T(8,128)(2,1)S(1)}, bf16[4,3,24,512]{3,2,1,0:T(8,128)(2,1)S(1)}, u32[]{:S(2)}, u32[]{:S(2)}) collective-permute-start(bf16[4,3,24,512]{3,2,1,0:T(8,128)(2,1)S(1)} %get-tuple-element.20), channel_id=1, source_target_pairs={{0,240},{16,0},{32,16},{48,32},{64,48},{80,64},{96,80},{112,96},{1... | collective-permute-start | bytes 884744 | tf_op jit(solution)/shard_map/ppermute | solution.py:387
  25.2 5.9 %collective-permute-start.2 = (bf16[3,32,128]{2,1,0:T(8,128)(2,1)S(1)}, bf16[3,32,128]{2,1,0:T(8,128)(2,1)S(1)}, u32[]{:S(2)}, u32[]{:S(2)}) collective-permute-start(bf16[3,32,128]{2,1,0:T(8,128)(2,1)S(1)} %pad_maximum_fusion.8), channel_id=1, source_target_pairs={{0,6},{16,22},{2,8},{18,24},{4,10},{20,26},{6,12},{22,28},{8,14},{... | collective-permute-start | bytes 73736 | tf_op jit(solution)/shard_map/ppermute | solution.py:399
  26.7 4.4 %collective-permute-start.3 = (bf16[2,32,128]{2,1,0:T(8,128)(2,1)S(1)}, bf16[2,32,128]{2,1,0:T(8,128)(2,1)S(1)}, u32[]{:S(2)}, u32[]{:S(2)}) collective-permute-start(bf16[2,32,128]{2,1,0:T(8,128)(2,1)S(1)} %slice.47), channel_id=1, source_target_pairs={{0,10},{16,26},{2,12},{18,28},{4,14},{20,30},{6,0},{22,16},{8,2},{... | collective-permute-start | bytes 49160 | tf_op jit(solution)/shard_map/ppermute | solution.py:399
  38.2 16.1 %collective-permute-start.8 = (bf16[4,12,6,512]{3,2,1,0:T(8,128)(2,1)S(1)}, bf16[4,12,6,512]{3,2,1,0:T(8,128)(2,1)S(1)}, u32[]{:S(2)}, u32[]{:S(2)}) collective-permute-start(bf16[4,12,6,512]{3,2,1,0:T(8,128)(2,1)S(1)} %pad_maximum_fusion.6), channel_id=1, source_target_pairs={{0,15},{1,0},{2,1},{3,2},{4,3},{5,4},{6,5},{7,6},{8,7},{9,8},{10,9... | collective-permute-start | bytes 884744 | tf_op jit(solution)/shard_map/ppermute | solution.py:387
  41.8 11.2 %collective-permute-start.5 = (bf16[8,32,128]{2,1,0:T(8,128)(2,1)S(1)}, bf16[8,32,128]{2,1,0:T(8,128)(2,1)S(1)}, u32[]{:S(2)}, u32[]{:S(2)}) collective-permute-start(bf16[8,32,128]{2,1,0:T(8,128)(2,1)S(1)} %constant_dynamic-update-slice_fusion), channel_id=1, source_target_pairs={{0,32},{16,48},{2,34},{18,50},{4,36},{20,52},{6,38},{22,54},{8,40}... | collective-permute-start | bytes 196616 | tf_op jit(solution)/shard_map/ppermute | solution.py:399
  43.1 10.0 %collective-permute-start.6 = (bf16[8,32,128]{2,1,0:T(8,128)(2,1)S(1)}, bf16[8,32,128]{2,1,0:T(8,128)(2,1)S(1)}, u32[]{:S(2)}, u32[]{:S(2)}) collective-permute-start(bf16[8,32,128]{2,1,0:T(8,128)(2,1)S(1)} %constant_dynamic-update-slice_fusion), channel_id=1, source_target_pairs={{0,1},{16,17},{2,3},{18,19},{4,5},{20,21},{6,7},{22,23},{8,9},{24,... | collective-permute-start | bytes 196616 | tf_op jit(solution)/shard_map/ppermute | solution.py:399
  43.1 11.2 %collective-permute-start.7 = (bf16[8,32,128]{2,1,0:T(8,128)(2,1)S(1)}, bf16[8,32,128]{2,1,0:T(8,128)(2,1)S(1)}, u32[]{:S(2)}, u32[]{:S(2)}) collective-permute-start(bf16[8,32,128]{2,1,0:T(8,128)(2,1)S(1)} %constant_dynamic-update-slice_fusion), channel_id=1, source_target_pairs={{0,33},{16,49},{2,35},{18,51},{4,37},{20,53},{6,39},{22,55},{8,41}... | collective-permute-start | bytes 196616 | tf_op jit(solution)/shard_map/ppermute | solution.py:399
  54.3 15.0 %copy-start.10 = (bf16[4,12,6,512]{3,2,1,0:T(8,128)(2,1)}, bf16[4,12,6,512]{3,2,1,0:T(8,128)(2,1)S(1)}, u32[]{:S(2)}) copy-start(bf16[4,12,6,512]{3,2,1,0:T(8,128)(2,1)S(1)} %collective-permute-done.8) | copy-start | bytes 884740
  54.3 9.5 %collective-permute-start.9 = (bf16[4,8,32,128]{3,2,1,0:T(8,128)(2,1)S(1)}, bf16[4,8,32,128]{3,2,1,0:T(8,128)(2,1)S(1)}, u32[]{:S(2)}, u32[]{:S(2)}) collective-permute-start(bf16[4,8,32,128]{3,2,1,0:T(8,128)(2,1)S(1)} %pad_maximum_fusion.7.refs_0_), channel_id=1, source_target_pairs={{0,64},{16,80},{2,66},{18,82},{4,68},{20,84},{6,70},{22,86},{8,72}... | collective-permute-start | bytes 786440 | tf_op jit(solution)/shard_map/ppermute | solution.py:399
  54.7 13.8 %collective-permute-start.10 = (bf16[4,8,32,128]{3,2,1,0:T(8,128)(2,1)S(1)}, bf16[4,8,32,128]{3,2,1,0:T(8,128)(2,1)S(1)}, u32[]{:S(2)}, u32[]{:S(2)}) collective-permute-start(bf16[4,8,32,128]{3,2,1,0:T(8,128)(2,1)S(1)} %pad_maximum_fusion.7.refs_0_), channel_id=1, source_target_pairs={{0,128},{16,144},{2,130},{18,146},{4,132},{20,148},{6,134},{22,150... | collective-permute-start | bytes 786440 | tf_op jit(solution)/shard_map/ppermute | solution.py:399
  56.8 12.5 %collective-permute-start.11 = (bf16[4,8,32,128]{3,2,1,0:T(8,128)(2,1)S(1)}, bf16[4,8,32,128]{3,2,1,0:T(8,128)(2,1)S(1)}, u32[]{:S(2)}, u32[]{:S(2)}) collective-permute-start(bf16[4,8,32,128]{3,2,1,0:T(8,128)(2,1)S(1)} %pad_maximum_fusion.7.refs_0_), channel_id=1, source_target_pairs={{0,192},{16,208},{2,194},{18,210},{4,196},{20,212},{6,198},{22,214... | collective-permute-start | bytes 786440 | tf_op jit(solution)/shard_map/ppermute | solution.py:399
  69.4 4.5 %collective-permute-start.13 = (bf16[3,4,8,32,128]{4,3,2,1,0:T(8,128)(2,1)S(1)}, bf16[3,4,8,32,128]{4,3,2,1,0:T(8,128)(2,1)S(1)}, u32[]{:S(2)}, u32[]{:S(2)}) collective-permute-start(bf16[3,4,8,32,128]{4,3,2,1,0:T(8,128)(2,1)S(1)} %pad_maximum_fusion.2.refs_1_), channel_id=1, source_target_pairs={{0,16},{16,0},{2,18},{18,2},{4,20},{20,4},{6,22},{22,6},{8,24},{24... | collective-permute-start | bytes 2359304 | tf_op jit(solution)/shard_map/ppermute | solution.py:399
  72.2 1.7 %collective-permute-start.12 = (bf16[4,8,32,128]{3,2,1,0:T(8,128)(2,1)S(1)}, bf16[4,8,32,128]{3,2,1,0:T(8,128)(2,1)S(1)}, u32[]{:S(2)}, u32[]{:S(2)}) collective-permute-start(bf16[4,8,32,128]{3,2,1,0:T(8,128)(2,1)S(1)} %pad_maximum_fusion.7.refs_0_), channel_id=1, source_target_pairs={{0,16},{16,0},{2,18},{18,2},{4,20},{20,4},{6,22},{22,6},{8,24},{24... | collective-permute-start | bytes 786440 | tf_op jit(solution)/shard_map/ppermute | solution.py:399
  79.9 5.6 %collective-permute-start.14 = (bf16[4,3,24,512]{3,2,1,0:T(8,128)(2,1)S(1)}, bf16[4,3,24,512]{3,2,1,0:T(8,128)(2,1)S(1)}, u32[]{:S(2)}, u32[]{:S(2)}) collective-permute-start(bf16[4,3,24,512]{3,2,1,0:T(8,128)(2,1)S(1)} %get-tuple-element.35), channel_id=1, source_target_pairs={{0,16},{16,32},{32,48},{48,64},{64,80},{80,96},{96,112},{112,128},... | collective-permute-start | bytes 884744 | tf_op jit(solution)/shard_map/ppermute | solution.py:387
  85.6 22.9 %copy-start = (bf16[288,288]{1,0:T(8,128)(2,1)S(1)}, bf16[288,288]{1,0:T(8,128)(2,1)}, u32[]{:S(2)}) copy-start(bf16[288,288]{1,0:T(8,128)(2,1)} %constant.68.clone.to_merged_ref) | copy-start | bytes 497668
  85.6 22.9 %copy-start.3 = (f32[2048]{0:T(1024)S(1)}, f32[2048]{0:T(1024)}, u32[]{:S(2)}) copy-start(f32[2048]{0:T(1024)} %param.22) | copy-start | bytes 24580
  85.6 22.9 %copy-start.4 = (f32[512]{0:T(512)S(1)}, f32[512]{0:T(512)}, u32[]{:S(2)}) copy-start(f32[512]{0:T(512)} %param.25) | copy-start | bytes 6148
  85.7 22.3 %collective-permute-start.15 = (bf16[4,12,6,512]{3,2,1,0:T(8,128)(2,1)S(1)}, bf16[4,12,6,512]{3,2,1,0:T(8,128)(2,1)S(1)}, u32[]{:S(2)}, u32[]{:S(2)}) collective-permute-start(bf16[4,12,6,512]{3,2,1,0:T(8,128)(2,1)S(1)} %pad_maximum_fusion.5), channel_id=1, source_target_pairs={{0,1},{1,2},{2,3},{3,4},{4,5},{5,6},{6,7},{7,8},{8,9},{9,10},{10,1... | collective-permute-start | bytes 884744 | tf_op jit(solution)/shard_map/ppermute | solution.py:387
  108.6 11.1 %copy-start.1 = (bf16[288,288]{1,0:T(8,128)(2,1)S(1)}, bf16[288,288]{1,0:T(8,128)(2,1)}, u32[]{:S(2)}) copy-start(bf16[288,288]{1,0:T(8,128)(2,1)} %constant.69.clone.to_win_ref) | copy-start | bytes 497668
  (7 other events, 31.7 us)
Sparse Core Ops, SparseCore 0:
  38.2 64.4 all-gather.2

commit v4 on v3

--- a/solution.py
+++ b/solution.py
@@ -110,13 +110,16 @@
                     put_attention(w_ref, rows, group, blocks)
 
 
-def unpack_decoder(raw_ref, w_ref, x):
-    for yl in range(2):
-        sx, ys = x, (yl, 2 + yl)
-        for core in range(2):
+def unpack_decoder(place_ref, raws, w_ref, slot):
+    px, py, pz, me = (place_ref[i] for i in range(4))
+    x = lax.rem(px - slot + 4, 4)
+    for side in range(2):
+        core = lax.rem(me + side, 2)
+        for yl in range(2):
+            ys = [lax.rem(py - (2 * yh + yl) + 4, 4) for yh in range(2)]
             rows = pl.ds(pl.multiple_of((x * 4 + yl * 2 + core) * 32, 32), 32)
             for group in range(4):
-                blocks = [raw_ref[2 * group + j // 2, core, sx, ys[j % 2]] for j in range(4)]
+                blocks = [raws[side][0, ys[j % 2], lax.rem(2 * group + j // 2 - pz + 12, 8)] for j in range(4)]
                 put_attention(w_ref, rows, group, blocks)
 
 
@@ -168,12 +171,13 @@
 
 
 def merge_split_kernel(
+    place_ref,
     x_ref,
     mgain_ref,
     sgain_ref,
-    wm_ref,
-    ws_ref,
-    wd_ref,
+    raw_ref,
+    own_ref,
+    other_ref,
     to_merged_ref,
     out_ref,
     dec_ref,
@@ -212,7 +216,7 @@
                 for core in range(2):
                     first = (x * 4 + yl * 2 + core) * 128
                     for z in range(2):
-                        left, right = (wm_ref[z, core, sx, y] for y in ys)
+                        left, right = (raw_ref[z, core, sx, y] for y in ys)
                         cols = slice(z * 128, (z + 1) * 128)
                         w_ref[first : first + 64, cols] = jnp.concatenate([left[:, :64], right[:, :64]], axis=1)
                         w_ref[first + 64 : first + 128, cols] = jnp.concatenate([left[:, 64:], right[:, 64:]], axis=1)
@@ -230,11 +234,11 @@
                     for z in range(2):
                         for yh in range(2):
                             lon = 2 * z + yh
-                            w2_ref[first : first + 64, lon * 128 : (lon + 1) * 128] = ws_ref[z, core, sx, ys[yh]]
+                            w2_ref[first : first + 64, lon * 128 : (lon + 1) * 128] = raw_ref[z, core, sx, ys[yh]]
         total = dot(middle_ref[0], w2_ref[:width])
         for chunk in range(1, 4):
             total += dot(middle_ref[chunk], w2_ref[chunk * width : (chunk + 1) * width])
-        unpack_decoder(wd_ref, dec_ref, part)
+        unpack_decoder(place_ref, (own_ref, other_ref), dec_ref, part)
         kept = (part % 2) * 2 + part // 2
         joined = (normed(total, sgain_ref[...]) + skip_ref[kept]).astype(jnp.bfloat16)
         out_ref[0] = joined
@@ -298,19 +302,19 @@
     )
 
 
-def merge_split(encoded, mgain, sgain, raw):
+def merge_split(encoded, mgain, sgain, raw, dec_raw, place):
     to_merged = merged_from_natural()
     tokens = LEV * ROWS * COLS // 4
     return pl.pallas_call(
         merge_split_kernel,
         grid=(8,),
         in_specs=[
+            pl.BlockSpec(memory_space=pltpu.SMEM),
             whole((LEV, 2, WIN, C)),
             whole((1, 4 * C)),
             whole((1, C)),
-            pl.BlockSpec((2, 2, 4, 4, 64, 128), lambda i: (jnp.minimum(i, 3), 0, 0, 0, 0, 0)),
-            pl.BlockSpec((2, 2, 4, 4, 64, 128), lambda i: (jnp.maximum(i - 4, 0), 0, 0, 0, 1, 0)),
-            pl.BlockSpec((8, 2, 4, 4, 32, 128), lambda i: (0, 0, 0, 0, 4, 0)),
+            pl.BlockSpec((2, 2, 4, 4, 64, 128), lambda i: (i % 4, 0, 0, 0, i // 4, 0)),
+            *[pl.BlockSpec((1, 4, 8, 32, 128), lambda i: (jnp.maximum(i - 4, 0), 0, 0, 0, 0))] * 2,
             whole((BAND, BAND)),
         ],
         out_specs=[
@@ -334,12 +338,12 @@
         compiler_params=PARAMS,
         name="merge_split",
     )(
+        place,
         encoded,
         mgain.reshape(1, 4 * C),
         sgain.reshape(1, C),
         raw,
-        raw,
-        raw,
+        *dec_raw,
         jnp.asarray(to_merged, jnp.bfloat16),
     )
 
@@ -453,43 +457,54 @@
     lat, lon = lax.axis_index("lat"), lax.axis_index("lon")
     last = lat == lax.axis_size("lat") - 1
     place = jnp.stack([lat // 4, (lon % 2) * 2 + (lat // 2) % 2, lon // 2, lat % 2, last.astype(jnp.int32)]).astype(jnp.int32)
-    enc_share = jnp.concatenate([enc_qkv, enc_proj], axis=1)
+    share = jnp.concatenate(
+        [jnp.concatenate([enc_qkv, enc_proj], axis=1), jnp.concatenate([dec_qkv, dec_proj], axis=1)], axis=0
+    )
     later_share = jnp.concatenate(
-        [
-            jnp.concatenate([merge_weight[:64], merge_weight[64:]], axis=1),
-            split_weight,
-            jnp.concatenate([dec_qkv, dec_proj], axis=1),
-        ],
-        axis=0,
-    )
-
+        [jnp.concatenate([merge_weight[:64], merge_weight[64:]], axis=1), split_weight], axis=0
+    )
+
+    later_share, share = together(later_share, share)
     later = x_and_y(later_share)
-    enc_near = [from_z(enc_share, 1), from_z(enc_share, -1)]
-    enc_three = jnp.stack([enc_near[0], enc_share, enc_near[1]])
-    tokens_sent, enc_three = together(tokens[:, :half_lat], enc_three)
-    enc_far, below, later = together(
-        [from_z(enc_three, 3), from_z(enc_three[:2], -3)], passed_along(tokens_sent, "lat", -1), later
-    )
-    later_raw = z_and_cores(later).reshape(8, 2, 4, 4, 160, 128)
-    enc_z = jnp.concatenate([enc_far[0], enc_three, enc_far[1]], axis=0)
+    near = [from_z(share, 1), from_z(share, -1)]
+    three = jnp.stack([near[0], share, near[1]])
+    tokens_sent, three = together(tokens[:, :half_lat], three)
+    far, below, later = together(
+        [from_z(three, 3), from_z(three[:2], -3)], passed_along(tokens_sent, "lat", -1), later
+    )
+    later_raw = z_and_cores(later).reshape(8, 2, 4, 4, 128, 128)
+    by_z = jnp.concatenate([far[0], three, far[1]], axis=0)
     edge = jnp.concatenate([tokens[:, half_lat:, :half_lon], below[:, :, :half_lon]], axis=1)
-    enc_y, beyond = together(from_y(enc_z), passed_along(edge, "lon", -1))
-    enc_y = jnp.stack([enc_z, *enc_y])
-    enc_x = jnp.stack(from_x(enc_y))
+    by_y, beyond = together(from_y(by_z), passed_along(edge, "lon", -1))
+    by_y = jnp.stack([by_z, *by_y])
+    enc_y, dec_y = by_y[:, :, :32], by_y[:, :, 32:]
+    framed = [
+        jnp.concatenate([tokens[:, half_lat : half_lat + WA, half_lon:], beyond[:, :WA]], axis=2),
+        jnp.concatenate(
+            [jnp.concatenate([tokens[:, half_lat + WA :], below], axis=1)[:, :, half_lon:], beyond[:, WA:]], axis=2
+        ),
+    ]
+    enc_x, framed = together(from_x(enc_y), framed)
+    enc_x = jnp.stack(enc_x)
     enc_raw = [enc_y, enc_x, other_core(enc_y), other_core(enc_x)]
-    framed = jnp.concatenate(
-        [jnp.concatenate([tokens[:, half_lat + WA :], below], axis=1)[:, :, half_lon:], beyond[:, WA:]], axis=2
-    )
-    second, enc_w = encode(1, framed, enc_gain, enc_raw, place)
+    second, enc_w = encode(1, framed[1], enc_gain, enc_raw, place)
     second = second.reshape(LEV, WA, COLS, C)
-    above = passed_along(second[:, WA - half_lat :], "lat", 1)
-    framed = jnp.concatenate([tokens[:, half_lat : half_lat + WA, half_lon:], beyond[:, :WA]], axis=2)
-    (first,) = encode(0, framed, enc_gain, [enc_w], place)
+    (first,) = encode(0, framed[0], enc_gain, [enc_w], place)
     first = first.reshape(LEV, WA, COLS, C)
-    rows = jnp.concatenate([above, first, second[:, : WA - half_lat]], axis=1)
-    left = passed_along(rows[:, :, COLS - half_lon :], "lon", 1)
-    encoded = jnp.concatenate([left, rows[:, :, : COLS - half_lon]], axis=2)
-    joined, dec_w = merge_split(encoded.reshape(LEV, 2, WIN, C), merge_gain, split_gain, later_raw)
+    dec_x, first = together(from_x(dec_y), first)
+    dec_own = jnp.stack([dec_y, *dec_x])
+    dec_raw = [dec_own, other_core(dec_own)]
+    cut_r, cut_c = WA - half_lat, COLS - half_lon
+    rows = jnp.concatenate([first, second[:, :cut_r]], axis=1)
+    left = passed_along(rows[:, :, cut_c:], "lon", 1)
+    above = passed_along(second[:, cut_r:, :cut_c], "lat", 1)
+    corner = passed_along(second[:, cut_r:, cut_c:], ("lat", "lon"), 1)
+    encoded = jnp.concatenate(
+        [jnp.concatenate([corner, above], axis=2), jnp.concatenate([left, rows[:, :, :cut_c]], axis=2)], axis=1
+    )
+    joined, dec_w = merge_split(
+        encoded.reshape(LEV, 2, WIN, C), merge_gain, split_gain, later_raw, dec_raw, place
+    )
     return decode(joined, dec_gain, dec_w).reshape(LEV, ROWS, COLS, C)
 
 

time: 139 us -> 138 us (level)
  waiting for transfers between devices: 46.3 us -> 38.3 us
  starting transfers between devices: 36.1 us -> 41.9 us
    ppermute x4 -> x5, waiting for transfers between devices: 24.9 us -> 13.7 us  [passed_along(): return lax.ppermute(value, axis, pairs)]
    ppermute x12 -> x16, starting transfers between devices: 20.3 us -> 25.2 us  [sent(): lax.ppermute(value, ('lat', 'lon'), [(device_index(*at), device_index(*to...]
    ppermute x12 -> x16, waiting for transfers between devices: 21.3 us -> 24.5 us  [sent(): lax.ppermute(value, ('lat', 'lon'), [(device_index(*at), device_index(*to...]
    unnamed x30, local copies, waits for them, and re-layouts: 1.1 us -> 2.64 us
    ppermute x4 -> x5, starting transfers between devices: 8.92 us -> 9.91 us  [passed_along(): return lax.ppermute(value, axis, pairs)]
  transfers between devices with their start and end apart: 18 -> 23, of which waited for: 10 -> 10; matrix products, arithmetic and copies ran while one was open for 5% -> 3% of each run, Pallas kernels for 8% -> 8%
where the time goes in v4:
time: 138 us; the launch traced here: 136 us
  starting transfers between devices  41.9 us (30%)
  waiting for transfers between devices  38.3 us (28%)
  Pallas kernels  32.9 us (24%)
  between operations  13.8 us (10%)
  local copies, waits for them, and re-layouts  5.81 us (4%)
  other arithmetic  3.06 us (2%)
    ppermute x16, starting transfers between devices, sent(): lax.ppermute(value, ('lat', 'lon'), [(device_index(*at), device_index(*to...  25.2 us
    ppermute x16, waiting for transfers between devices, sent(): lax.ppermute(value, ('lat', 'lon'), [(device_index(*at), device_index(*to...  24.5 us
    ppermute x5, waiting for transfers between devices, passed_along(): return lax.ppermute(value, axis, pairs)  13.7 us
    pallas_call x1, Pallas kernels, merge_split(): pl.pallas_call(merge_split_kernel, grid=(8,), in_specs=[pl.BlockSpec(memo...  11.6 us
    pallas_call x2, Pallas kernels, encode(): pl.pallas_call(functools.partial(encode_kernel, band), grid=(2,), in_spec...  10.9 us
    pallas_call x1, Pallas kernels, decode(): pl.pallas_call(decode_kernel, grid=(4,), in_specs=[whole((4, 4, BAND // 4...  10.4 us
    ppermute x5, starting transfers between devices, passed_along(): return lax.ppermute(value, axis, pairs)  9.91 us
    all_to_all x1, starting transfers between devices, x_and_y(): lax.all_to_all(blocks, ('lat', 'lon'), 0, 0, tiled=True, axis_index_group...  6.75 us
  transfers between devices with their start and end apart: 23, of which 10 were waited for; matrix products, arithmetic and copies ran while one was open for 3% of the time, Pallas kernels for 8%

profile of v4, /device:TPU:1, one launch (start us, length us, event | category | flops | bytes accessed | tf_op | source)
XLA Modules:
  0.0 135.7 jit_solution(1638866709019654578)
XLA Ops:
  9.3 2.5 %collective-permute-start = (bf16[64,128]{1,0:T(8,128)(2,1)S(1)}, bf16[64,128]{1,0:T(8,128)(2,1)S(1)}, u32[]{:S(2)}, u32[]{:S(2)}) collective-permute-start(bf16[64,128]{1,0:T(8,128)(2,1)S(1)} %maximum_maximum_fusion), channel_id=1, source_target_pairs={{0,2},{16,18},{2,4},{18,20},{4,6},{20,22},{6,8},{22,24},{8,10},{24... | collective-permute-start | bytes 49160 | tf_op jit(solution)/shard_map/ppermute | solution.py:403
  11.8 4.0 %collective-permute-start.1 = (bf16[64,128]{1,0:T(8,128)(2,1)S(1)}, bf16[64,128]{1,0:T(8,128)(2,1)S(1)}, u32[]{:S(2)}, u32[]{:S(2)}) collective-permute-start(bf16[64,128]{1,0:T(8,128)(2,1)S(1)} %maximum_maximum_fusion), channel_id=1, source_target_pairs={{0,14},{16,30},{2,0},{18,16},{4,2},{20,18},{6,4},{22,20},{8,6},{24... | collective-permute-start | bytes 49160 | tf_op jit(solution)/shard_map/ppermute | solution.py:403
  16.7 6.8 %all-to-all-start = ((bf16[16,128,128]{2,1,0:T(8,128)(2,1)}), bf16[16,128,128]{2,1,0:T(8,128)(2,1)S(1)}, u32[]{:S(2)}, u32[]{:S(2)}) async-start(bf16[16,128,128]{2,1,0:T(8,128)(2,1)} %broadcast_in_dim.2), calls=%async_computation | async-start | bytes 1048576 | tf_op jit(solution)/shard_map/all_to_all | solution.py:423
  24.9 1.5 %collective-permute-start.2 = (bf16[3,64,128]{2,1,0:T(8,128)(2,1)S(1)}, bf16[3,64,128]{2,1,0:T(8,128)(2,1)S(1)}, u32[]{:S(2)}, u32[]{:S(2)}) collective-permute-start(bf16[3,64,128]{2,1,0:T(8,128)(2,1)S(1)} %pad_maximum_fusion.8), channel_id=1, source_target_pairs={{0,6},{16,22},{2,8},{18,24},{4,10},{20,26},{6,12},{22,28},{8,14},{... | collective-permute-start | bytes 147464 | tf_op jit(solution)/shard_map/ppermute | solution.py:403
  26.5 2.9 %collective-permute-start.3 = (bf16[2,64,128]{2,1,0:T(8,128)(2,1)S(1)}, bf16[2,64,128]{2,1,0:T(8,128)(2,1)S(1)}, u32[]{:S(2)}, u32[]{:S(2)}) collective-permute-start(bf16[2,64,128]{2,1,0:T(8,128)(2,1)S(1)} %slice.57), channel_id=1, source_target_pairs={{0,10},{16,26},{2,12},{18,28},{4,14},{20,30},{6,0},{22,16},{8,2},{... | collective-permute-start | bytes 98312 | tf_op jit(solution)/shard_map/ppermute | solution.py:403
  29.4 1.9 %collective-permute-done.3 = bf16[2,64,128]{2,1,0:T(8,128)(2,1)S(1)} collective-permute-done((bf16[2,64,128]{2,1,0:T(8,128)(2,1)S(1)}, bf16[2,64,128]{2,1,0:T(8,128)(2,1)S(1)}, u32[]{:S(2)}, u32[]{:S(2)}) %collective-permute-start.3) | collective-permute-done | bytes 32800 | tf_op jit(solution)/shard_map/ppermute | solution.py:403
  31.5 4.3 %collective-permute-done.4 = bf16[4,3,24,512]{3,2,1,0:T(8,128)(2,1)S(1)} collective-permute-done((bf16[4,3,24,512]{3,2,1,0:T(8,128)(2,1)S(1)}, bf16[4,3,24,512]{3,2,1,0:T(8,128)(2,1)S(1)}, u32[]{:S(2)}, u32[]{:S(2)}) %collective-permute-start.4) | collective-permute-done | bytes 294944 | tf_op jit(solution)/shard_map/ppermute | solution.py:391
  36.7 3.5 %collective-permute-start.8 = (bf16[4,12,6,512]{3,2,1,0:T(8,128)(2,1)S(1)}, bf16[4,12,6,512]{3,2,1,0:T(8,128)(2,1)S(1)}, u32[]{:S(2)}, u32[]{:S(2)}) collective-permute-start(bf16[4,12,6,512]{3,2,1,0:T(8,128)(2,1)S(1)} %pad_maximum_fusion.6), channel_id=1, source_target_pairs={{0,15},{1,0},{2,1},{3,2},{4,3},{5,4},{6,5},{7,6},{8,7},{9,8},{10,9... | collective-permute-start | bytes 884744 | tf_op jit(solution)/shard_map/ppermute | solution.py:391
  41.3 2.5 %collective-permute-start.7 = (bf16[8,64,128]{2,1,0:T(8,128)(2,1)S(1)}, bf16[8,64,128]{2,1,0:T(8,128)(2,1)S(1)}, u32[]{:S(2)}, u32[]{:S(2)}) collective-permute-start(bf16[8,64,128]{2,1,0:T(8,128)(2,1)S(1)} %constant_dynamic-update-slice_fusion), channel_id=1, source_target_pairs={{0,33},{16,49},{2,35},{18,51},{4,37},{20,53},{6,39},{22,55},{8,41}... | collective-permute-start | bytes 393224 | tf_op jit(solution)/shard_map/ppermute | solution.py:403
  44.0 9.8 %collective-permute-done.5 = bf16[8,64,128]{2,1,0:T(8,128)(2,1)S(1)} collective-permute-done((bf16[8,64,128]{2,1,0:T(8,128)(2,1)S(1)}, bf16[8,64,128]{2,1,0:T(8,128)(2,1)S(1)}, u32[]{:S(2)}, u32[]{:S(2)}) %collective-permute-start.5) | collective-permute-done | bytes 131104 | tf_op jit(solution)/shard_map/ppermute | solution.py:403
  56.4 2.5 %collective-permute-start.10 = (bf16[4,8,32,128]{3,2,1,0:T(8,128)(2,1)S(1)}, bf16[4,8,32,128]{3,2,1,0:T(8,128)(2,1)S(1)}, u32[]{:S(2)}, u32[]{:S(2)}) collective-permute-start(bf16[4,8,32,128]{3,2,1,0:T(8,128)(2,1)S(1)} %get-tuple-element.59.refs_0_), channel_id=1, source_target_pairs={{0,128},{16,144},{2,130},{18,146},{4,132},{20,148},{6,134},{22,150... | collective-permute-start | bytes 786440 | tf_op jit(solution)/shard_map/ppermute | solution.py:403
  60.8 4.7 %collective-permute-done.10 = bf16[4,8,32,128]{3,2,1,0:T(8,128)(2,1)S(1)} collective-permute-done((bf16[4,8,32,128]{3,2,1,0:T(8,128)(2,1)S(1)}, bf16[4,8,32,128]{3,2,1,0:T(8,128)(2,1)S(1)}, u32[]{:S(2)}, u32[]{:S(2)}) %collective-permute-start.10) | collective-permute-done | bytes 262176 | tf_op jit(solution)/shard_map/ppermute | solution.py:403
  65.5 5.0 %collective-permute-done.11 = bf16[4,8,32,128]{3,2,1,0:T(8,128)(2,1)S(1)} collective-permute-done((bf16[4,8,32,128]{3,2,1,0:T(8,128)(2,1)S(1)}, bf16[4,8,32,128]{3,2,1,0:T(8,128)(2,1)S(1)}, u32[]{:S(2)}, u32[]{:S(2)}) %collective-permute-start.11) | collective-permute-done | bytes 262176 | tf_op jit(solution)/shard_map/ppermute | solution.py:403
  73.8 2.0 %collective-permute-start.17 = (bf16[4,8,32,128]{3,2,1,0:T(8,128)(2,1)}, bf16[4,8,32,128]{3,2,1,0:T(8,128)(2,1)S(1)}, u32[]{:S(2)}, u32[]{:S(2)}) collective-permute-start(bf16[4,8,32,128]{3,2,1,0:T(8,128)(2,1)} %get-tuple-element.58), channel_id=1, source_target_pairs={{0,128},{16,144},{2,130},{18,146},{4,132},{20,148},{6,134},{22,150... | collective-permute-start | bytes 786440 | tf_op jit(solution)/shard_map/ppermute | solution.py:403
  75.8 1.6 %collective-permute-start.18 = (bf16[4,8,32,128]{3,2,1,0:T(8,128)(2,1)}, bf16[4,8,32,128]{3,2,1,0:T(8,128)(2,1)S(1)}, u32[]{:S(2)}, u32[]{:S(2)}) collective-permute-start(bf16[4,8,32,128]{3,2,1,0:T(8,128)(2,1)} %get-tuple-element.58), channel_id=1, source_target_pairs={{0,192},{16,208},{2,194},{18,210},{4,196},{20,212},{6,198},{22,214... | collective-permute-start | bytes 786440 | tf_op jit(solution)/shard_map/ppermute | solution.py:403
  77.4 5.9 %encode_band1.1 = (bf16[4,144,512]{2,1,0:T(8,128)(2,1)S(1)}, bf16[512,2048]{1,0:T(8,128)(2,1)S(1)}) custom-call(s32[5]{0:T(128)S(1)} %stack.81.place_ref, bf16[4,144,512]{2,1,0:T(8,128)(2,1)S(1)} %bitcast.41, f32[1,512]{1,0:T(1,128)S(1)} %bitcast.45, bf16[144,144]{1,0:T(8,128)(2,1)S(1)} %copy-done.9, bf16[144,144]{1,0:T(8,128)(2,1)S(1)} %copy-done.3, ...), custom_call_target="tpu_custom_call" | custom-call | flops 2000000000 | bytes 4000000 | tf_op jit(solution)/shard_map/encode_band1/pallas_call | solution.py:278
  83.3 5.0 %encode_band0.1 = bf16[4,144,512]{2,1,0:T(8,128)(2,1)S(1)} custom-call(s32[5]{0:T(128)S(1)} %stack.81.place_ref, bf16[4,144,512]{2,1,0:T(8,128)(2,1)S(1)} %bitcast.40, f32[1,512]{1,0:T(1,128)S(1)} %bitcast.46, bf16[144,144]{1,0:T(8,128)(2,1)S(1)} %copy-done.9, bf16[144,144]{1,0:T(8,128)(2,1)S(1)} %copy-done.3, bf16[512,2048]{1,0:T(8,128)(2,1)S(1)} %get-tuple-element.47.refs_0_), custom_call_target="tpu_custom_call" | custom-call | flops 2000000000 | bytes 4000000 | tf_op jit(solution)/shard_map/encode_band0/pallas_call | solution.py:278
  88.5 1.3 collective-permute-start.20
  89.9 2.7 %collective-permute-start.19 = (bf16[4,9,6,512]{3,2,1,0:T(8,128)(2,1)S(1)}, bf16[4,9,6,512]{3,2,1,0:T(8,128)(2,1)S(1)}, u32[]{:S(2)}, u32[]{:S(2)}) collective-permute-start(bf16[4,9,6,512]{3,2,1,0:T(8,128)(2,1)S(1)} %pad_maximum_fusion.7), channel_id=1, source_target_pairs={{0,1},{1,2},{2,3},{3,4},{4,5},{5,6},{6,7},{7,8},{8,9},{9,10},{10,1... | collective-permute-start | bytes 663560 | tf_op jit(solution)/shard_map/ppermute | solution.py:391
  93.2 1.9 %collective-permute-start.14 = (bf16[4,3,6,512]{3,2,1,0:T(8,128)(2,1)S(1)}, bf16[4,3,6,512]{3,2,1,0:T(8,128)(2,1)S(1)}, u32[]{:S(2)}, u32[]{:S(2)}) collective-permute-start(bf16[4,3,6,512]{3,2,1,0:T(8,128)(2,1)S(1)} %slice.73), channel_id=1, source_target_pairs={{0,17},{1,18},{2,19},{3,20},{4,21},{5,22},{6,23},{7,24},{8,25},{9,... | collective-permute-start | bytes 221192 | tf_op jit(solution)/shard_map/ppermute | solution.py:391
  95.1 9.4 %collective-permute-done.14 = bf16[4,3,6,512]{3,2,1,0:T(8,128)(2,1)S(1)} collective-permute-done((bf16[4,3,6,512]{3,2,1,0:T(8,128)(2,1)S(1)}, bf16[4,3,6,512]{3,2,1,0:T(8,128)(2,1)S(1)}, u32[]{:S(2)}, u32[]{:S(2)}) %collective-permute-start.14) | collective-permute-done | bytes 73760 | tf_op jit(solution)/shard_map/ppermute | solution.py:391
  105.2 11.6 %merge_split.1 = (bf16[4,288,512]{2,1,0:T(8,128)(2,1)S(1)}, bf16[512,2048]{1,0:T(8,128)(2,1)}) custom-call(s32[5]{0:T(128)S(1)} %stack.81.place_ref, bf16[4,2,144,512]{3,2,1,0:T(8,128)(2,1)S(1)} %bitcast.33, f32[1,2048]{1,0:T(1,128)S(1)} %bitcast.42, f32[1,512]{1,0:T(1,128)S(1)} %bitcast.43, bf16[8,2,4,4,128,128]{5,4,3,2,1,0:T(8,128)(2,1)} %bitcast.47, ...), custom_call_target="tpu_custom_call" | custom-call | tf_op jit(solution)/shard_map/merge_split/pallas_call | solution.py:308
  116.8 1.6 %copy-done = bf16[512,2048]{1,0:T(8,128)(2,1)S(1)} copy-done((bf16[512,2048]{1,0:T(8,128)(2,1)S(1)}, bf16[512,2048]{1,0:T(8,128)(2,1)}, u32[]{:S(2)}) %copy-start) | copy-done | bytes 2097176
  118.4 10.4 %decode.1 = bf16[4,2,144,512]{3,2,1,0:T(8,128)(2,1)} custom-call(bf16[4,4,72,512]{3,2,1,0:T(8,128)(2,1)S(1)} %bitcast.36, f32[1,512]{1,0:T(1,128)S(1)} %bitcast.44, bf16[512,2048]{1,0:T(8,128)(2,1)S(1)} %copy-done, bf16[288,288]{1,0:T(8,128)(2,1)S(1)} %copy-done.2, bf16[144,144]{1,0:T(8,128)(2,1)S(1)} %copy-done.4), custom_call_target="tpu_custom_call" | custom-call | tf_op jit(solution)/shard_map/decode/pallas_call | solution.py:355
  (82 shorter events, 16.6 us)
Async XLA Ops:
  6.5 17.0 %copy-start.11 = (bf16[4,12,24,512]{3,2,1,0:T(8,128)(2,1)S(1)}, bf16[4,12,24,512]{3,2,1,0:T(8,128)(2,1)}, u32[]{:S(2)}) copy-start(bf16[4,12,24,512]{3,2,1,0:T(8,128)(2,1)} %param.18) | copy-start | bytes 3538948
  9.3 14.3 %collective-permute-start = (bf16[64,128]{1,0:T(8,128)(2,1)S(1)}, bf16[64,128]{1,0:T(8,128)(2,1)S(1)}, u32[]{:S(2)}, u32[]{:S(2)}) collective-permute-start(bf16[64,128]{1,0:T(8,128)(2,1)S(1)} %maximum_maximum_fusion), channel_id=1, source_target_pairs={{0,2},{16,18},{2,4},{18,20},{4,6},{20,22},{6,8},{22,24},{8,10},{24... | collective-permute-start | bytes 49160 | tf_op jit(solution)/shard_map/ppermute | solution.py:403
  11.8 11.8 %collective-permute-start.1 = (bf16[64,128]{1,0:T(8,128)(2,1)S(1)}, bf16[64,128]{1,0:T(8,128)(2,1)S(1)}, u32[]{:S(2)}, u32[]{:S(2)}) collective-permute-start(bf16[64,128]{1,0:T(8,128)(2,1)S(1)} %maximum_maximum_fusion), channel_id=1, source_target_pairs={{0,14},{16,30},{2,0},{18,16},{4,2},{20,18},{6,4},{22,20},{8,6},{24... | collective-permute-start | bytes 49160 | tf_op jit(solution)/shard_map/ppermute | solution.py:403
  16.7 19.1 %all-to-all-start = ((bf16[16,128,128]{2,1,0:T(8,128)(2,1)}), bf16[16,128,128]{2,1,0:T(8,128)(2,1)S(1)}, u32[]{:S(2)}, u32[]{:S(2)}) async-start(bf16[16,128,128]{2,1,0:T(8,128)(2,1)} %broadcast_in_dim.2), calls=%async_computation | async-start | bytes 1048576 | tf_op jit(solution)/shard_map/all_to_all | solution.py:423
  23.5 81.7 %all-gather.3.cloned.1.call-start = ((), (), s32[]{:S(2)}) async-start(), calls=%async_computation.1 | async-start | bytes 8912896 | tf_op jit(solution)/shard_map/all_gather | solution.py:431
  23.6 12.1 %collective-permute-start.4 = (bf16[4,3,24,512]{3,2,1,0:T(8,128)(2,1)S(1)}, bf16[4,3,24,512]{3,2,1,0:T(8,128)(2,1)S(1)}, u32[]{:S(2)}, u32[]{:S(2)}) collective-permute-start(bf16[4,3,24,512]{3,2,1,0:T(8,128)(2,1)S(1)} %get-tuple-element.32), channel_id=1, source_target_pairs={{0,240},{16,0},{32,16},{48,32},{64,48},{80,64},{96,80},{112,96},{1... | collective-permute-start | bytes 884744 | tf_op jit(solution)/shard_map/ppermute | solution.py:391
  24.9 6.6 %collective-permute-start.2 = (bf16[3,64,128]{2,1,0:T(8,128)(2,1)S(1)}, bf16[3,64,128]{2,1,0:T(8,128)(2,1)S(1)}, u32[]{:S(2)}, u32[]{:S(2)}) collective-permute-start(bf16[3,64,128]{2,1,0:T(8,128)(2,1)S(1)} %pad_maximum_fusion.8), channel_id=1, source_target_pairs={{0,6},{16,22},{2,8},{18,24},{4,10},{20,26},{6,12},{22,28},{8,14},{... | collective-permute-start | bytes 147464 | tf_op jit(solution)/shard_map/ppermute | solution.py:403
  26.5 4.9 %collective-permute-start.3 = (bf16[2,64,128]{2,1,0:T(8,128)(2,1)S(1)}, bf16[2,64,128]{2,1,0:T(8,128)(2,1)S(1)}, u32[]{:S(2)}, u32[]{:S(2)}) collective-permute-start(bf16[2,64,128]{2,1,0:T(8,128)(2,1)S(1)} %slice.57), channel_id=1, source_target_pairs={{0,10},{16,26},{2,12},{18,28},{4,14},{20,30},{6,0},{22,16},{8,2},{... | collective-permute-start | bytes 98312 | tf_op jit(solution)/shard_map/ppermute | solution.py:403
  36.7 18.6 %collective-permute-start.8 = (bf16[4,12,6,512]{3,2,1,0:T(8,128)(2,1)S(1)}, bf16[4,12,6,512]{3,2,1,0:T(8,128)(2,1)S(1)}, u32[]{:S(2)}, u32[]{:S(2)}) collective-permute-start(bf16[4,12,6,512]{3,2,1,0:T(8,128)(2,1)S(1)} %pad_maximum_fusion.6), channel_id=1, source_target_pairs={{0,15},{1,0},{2,1},{3,2},{4,3},{5,4},{6,5},{7,6},{8,7},{9,8},{10,9... | collective-permute-start | bytes 884744 | tf_op jit(solution)/shard_map/ppermute | solution.py:391
  40.2 13.5 %collective-permute-start.5 = (bf16[8,64,128]{2,1,0:T(8,128)(2,1)S(1)}, bf16[8,64,128]{2,1,0:T(8,128)(2,1)S(1)}, u32[]{:S(2)}, u32[]{:S(2)}) collective-permute-start(bf16[8,64,128]{2,1,0:T(8,128)(2,1)S(1)} %constant_dynamic-update-slice_fusion), channel_id=1, source_target_pairs={{0,32},{16,48},{2,34},{18,50},{4,36},{20,52},{6,38},{22,54},{8,40}... | collective-permute-start | bytes 393224 | tf_op jit(solution)/shard_map/ppermute | solution.py:403
  41.3 13.3 %collective-permute-start.6 = (bf16[8,64,128]{2,1,0:T(8,128)(2,1)S(1)}, bf16[8,64,128]{2,1,0:T(8,128)(2,1)S(1)}, u32[]{:S(2)}, u32[]{:S(2)}) collective-permute-start(bf16[8,64,128]{2,1,0:T(8,128)(2,1)S(1)} %constant_dynamic-update-slice_fusion), channel_id=1, source_target_pairs={{0,1},{16,17},{2,3},{18,19},{4,5},{20,21},{6,7},{22,23},{8,9},{24,... | collective-permute-start | bytes 393224 | tf_op jit(solution)/shard_map/ppermute | solution.py:403
  41.3 14.0 %collective-permute-start.7 = (bf16[8,64,128]{2,1,0:T(8,128)(2,1)S(1)}, bf16[8,64,128]{2,1,0:T(8,128)(2,1)S(1)}, u32[]{:S(2)}, u32[]{:S(2)}) collective-permute-start(bf16[8,64,128]{2,1,0:T(8,128)(2,1)S(1)} %constant_dynamic-update-slice_fusion), channel_id=1, source_target_pairs={{0,33},{16,49},{2,35},{18,51},{4,37},{20,53},{6,39},{22,55},{8,41}... | collective-permute-start | bytes 393224 | tf_op jit(solution)/shard_map/ppermute | solution.py:403
  56.4 9.2 %collective-permute-start.10 = (bf16[4,8,32,128]{3,2,1,0:T(8,128)(2,1)S(1)}, bf16[4,8,32,128]{3,2,1,0:T(8,128)(2,1)S(1)}, u32[]{:S(2)}, u32[]{:S(2)}) collective-permute-start(bf16[4,8,32,128]{3,2,1,0:T(8,128)(2,1)S(1)} %get-tuple-element.59.refs_0_), channel_id=1, source_target_pairs={{0,128},{16,144},{2,130},{18,146},{4,132},{20,148},{6,134},{22,150... | collective-permute-start | bytes 786440 | tf_op jit(solution)/shard_map/ppermute | solution.py:403
  58.9 11.7 %collective-permute-start.11 = (bf16[4,8,32,128]{3,2,1,0:T(8,128)(2,1)S(1)}, bf16[4,8,32,128]{3,2,1,0:T(8,128)(2,1)S(1)}, u32[]{:S(2)}, u32[]{:S(2)}) collective-permute-start(bf16[4,8,32,128]{3,2,1,0:T(8,128)(2,1)S(1)} %get-tuple-element.59.refs_0_), channel_id=1, source_target_pairs={{0,192},{16,208},{2,194},{18,210},{4,196},{20,212},{6,198},{22,214... | collective-permute-start | bytes 786440 | tf_op jit(solution)/shard_map/ppermute | solution.py:403
  59.7 12.1 %collective-permute-start.9 = (bf16[4,8,32,128]{3,2,1,0:T(8,128)(2,1)S(1)}, bf16[4,8,32,128]{3,2,1,0:T(8,128)(2,1)S(1)}, u32[]{:S(2)}, u32[]{:S(2)}) collective-permute-start(bf16[4,8,32,128]{3,2,1,0:T(8,128)(2,1)S(1)} %get-tuple-element.59.refs_0_), channel_id=1, source_target_pairs={{0,64},{16,80},{2,66},{18,82},{4,68},{20,84},{6,70},{22,86},{8,72}... | collective-permute-start | bytes 786440 | tf_op jit(solution)/shard_map/ppermute | solution.py:403
  71.9 5.4 %collective-permute-start.13 = (bf16[3,4,8,32,128]{4,3,2,1,0:T(8,128)(2,1)S(1)}, bf16[3,4,8,32,128]{4,3,2,1,0:T(8,128)(2,1)S(1)}, u32[]{:S(2)}, u32[]{:S(2)}) collective-permute-start(bf16[3,4,8,32,128]{4,3,2,1,0:T(8,128)(2,1)S(1)} %pad_maximum_fusion.2.refs_1_), channel_id=1, source_target_pairs={{0,16},{16,0},{2,18},{18,2},{4,20},{20,4},{6,22},{22,6},{8,24},{24... | collective-permute-start | bytes 2359304 | tf_op jit(solution)/shard_map/ppermute | solution.py:403
  72.4 4.9 %collective-permute-start.12 = (bf16[4,8,32,128]{3,2,1,0:T(8,128)(2,1)S(1)}, bf16[4,8,32,128]{3,2,1,0:T(8,128)(2,1)S(1)}, u32[]{:S(2)}, u32[]{:S(2)}) collective-permute-start(bf16[4,8,32,128]{3,2,1,0:T(8,128)(2,1)S(1)} %get-tuple-element.59.refs_0_), channel_id=1, source_target_pairs={{0,16},{16,0},{2,18},{18,2},{4,20},{20,4},{6,22},{22,6},{8,24},{24... | collective-permute-start | bytes 786440 | tf_op jit(solution)/shard_map/ppermute | solution.py:403
  72.6 15.7 %collective-permute-start.16 = (bf16[4,8,32,128]{3,2,1,0:T(8,128)(2,1)}, bf16[4,8,32,128]{3,2,1,0:T(8,128)(2,1)S(1)}, u32[]{:S(2)}, u32[]{:S(2)}) collective-permute-start(bf16[4,8,32,128]{3,2,1,0:T(8,128)(2,1)} %get-tuple-element.58), channel_id=1, source_target_pairs={{0,64},{16,80},{2,66},{18,82},{4,68},{20,84},{6,70},{22,86},{8,72}... | collective-permute-start | bytes 786440 | tf_op jit(solution)/shard_map/ppermute | solution.py:403
  73.8 14.5 %collective-permute-start.17 = (bf16[4,8,32,128]{3,2,1,0:T(8,128)(2,1)}, bf16[4,8,32,128]{3,2,1,0:T(8,128)(2,1)S(1)}, u32[]{:S(2)}, u32[]{:S(2)}) collective-permute-start(bf16[4,8,32,128]{3,2,1,0:T(8,128)(2,1)} %get-tuple-element.58), channel_id=1, source_target_pairs={{0,128},{16,144},{2,130},{18,146},{4,132},{20,148},{6,134},{22,150... | collective-permute-start | bytes 786440 | tf_op jit(solution)/shard_map/ppermute | solution.py:403
  75.8 12.5 %collective-permute-start.18 = (bf16[4,8,32,128]{3,2,1,0:T(8,128)(2,1)}, bf16[4,8,32,128]{3,2,1,0:T(8,128)(2,1)S(1)}, u32[]{:S(2)}, u32[]{:S(2)}) collective-permute-start(bf16[4,8,32,128]{3,2,1,0:T(8,128)(2,1)} %get-tuple-element.58), channel_id=1, source_target_pairs={{0,192},{16,208},{2,194},{18,210},{4,196},{20,212},{6,198},{22,214... | collective-permute-start | bytes 786440 | tf_op jit(solution)/shard_map/ppermute | solution.py:403
  88.5 16.7 %collective-permute-start.20 = (bf16[4,4,8,32,128]{4,3,2,1,0:T(8,128)(2,1)S(1)}, bf16[4,4,8,32,128]{4,3,2,1,0:T(8,128)(2,1)S(1)}, u32[]{:S(2)}, u32[]{:S(2)}) collective-permute-start(bf16[4,4,8,32,128]{4,3,2,1,0:T(8,128)(2,1)S(1)} %pad_maximum_fusion.1.own_ref), channel_id=1, source_target_pairs={{0,16},{16,0},{2,18},{18,2},{4,20},{20,4},{6,22},{22,6},{8,24},{24... | collective-permute-start | bytes 3145736 | tf_op jit(solution)/shard_map/ppermute | solution.py:403
  89.9 14.6 %collective-permute-start.19 = (bf16[4,9,6,512]{3,2,1,0:T(8,128)(2,1)S(1)}, bf16[4,9,6,512]{3,2,1,0:T(8,128)(2,1)S(1)}, u32[]{:S(2)}, u32[]{:S(2)}) collective-permute-start(bf16[4,9,6,512]{3,2,1,0:T(8,128)(2,1)S(1)} %pad_maximum_fusion.7), channel_id=1, source_target_pairs={{0,1},{1,2},{2,3},{3,4},{4,5},{5,6},{6,7},{7,8},{8,9},{9,10},{10,1... | collective-permute-start | bytes 663560 | tf_op jit(solution)/shard_map/ppermute | solution.py:391
  92.6 12.0 %collective-permute-start.15 = (bf16[4,3,18,512]{3,2,1,0:T(8,128)(2,1)S(1)}, bf16[4,3,18,512]{3,2,1,0:T(8,128)(2,1)S(1)}, u32[]{:S(2)}, u32[]{:S(2)}) collective-permute-start(bf16[4,3,18,512]{3,2,1,0:T(8,128)(2,1)S(1)} %slice.74), channel_id=1, source_target_pairs={{0,16},{16,32},{32,48},{48,64},{64,80},{80,96},{96,112},{112,128},... | collective-permute-start | bytes 663560 | tf_op jit(solution)/shard_map/ppermute | solution.py:391
  93.2 11.4 %collective-permute-start.14 = (bf16[4,3,6,512]{3,2,1,0:T(8,128)(2,1)S(1)}, bf16[4,3,6,512]{3,2,1,0:T(8,128)(2,1)S(1)}, u32[]{:S(2)}, u32[]{:S(2)}) collective-permute-start(bf16[4,3,6,512]{3,2,1,0:T(8,128)(2,1)S(1)} %slice.73), channel_id=1, source_target_pairs={{0,17},{1,18},{2,19},{3,20},{4,21},{5,22},{6,23},{7,24},{8,25},{9,... | collective-permute-start | bytes 221192 | tf_op jit(solution)/shard_map/ppermute | solution.py:391
  (12 other events, 128.0 us)
Sparse Core Ops, SparseCore 0:
  36.7 55.6 all-gather.2

commit v5 on v4

--- a/solution.py
+++ b/solution.py
@@ -19,7 +19,7 @@
 ROWS = 12
 COLS = 24
 BAND = 2 * WIN
-VMEM_LIMIT = 48 * 1024 * 1024
+VMEM_LIMIT = 28 * 1024 * 1024
 
 eps = 1e-05
 SCALE = float(HD**-0.5 * np.log2(np.e))

time: 138 us -> 136 us (0.986)
  Pallas kernels: 32.9 us -> 29.6 us
  local copies, waits for them, and re-layouts: 5.81 us -> 7.59 us
    pallas_call x1, Pallas kernels: 11.6 us -> 8.34 us  [merge_split(): pl.pallas_call(merge_split_kernel, grid=(8,), in_specs=[pl.BlockSpec(memo...]
    unnamed x30, local copies, waits for them, and re-layouts: 2.64 us -> 4.43 us
where the time goes in v5:
time: 136 us; the launch traced here: 134 us
  starting transfers between devices  41.9 us (31%)
  waiting for transfers between devices  38.3 us (28%)
  Pallas kernels  29.6 us (22%)
  between operations  13.8 us (10%)
  local copies, waits for them, and re-layouts  7.59 us (6%)
  other arithmetic  3.06 us (2%)
    ppermute x16, starting transfers between devices, sent(): lax.ppermute(value, ('lat', 'lon'), [(device_index(*at), device_index(*to...  25.2 us
    ppermute x16, waiting for transfers between devices, sent(): lax.ppermute(value, ('lat', 'lon'), [(device_index(*at), device_index(*to...  24.5 us
    ppermute x5, waiting for transfers between devices, passed_along(): return lax.ppermute(value, axis, pairs)  13.7 us
    pallas_call x2, Pallas kernels, encode(): pl.pallas_call(functools.partial(encode_kernel, band), grid=(2,), in_spec...  10.9 us
    pallas_call x1, Pallas kernels, decode(): pl.pallas_call(decode_kernel, grid=(4,), in_specs=[whole((4, 4, BAND // 4...  10.4 us
    ppermute x5, starting transfers between devices, passed_along(): return lax.ppermute(value, axis, pairs)  9.91 us
    pallas_call x1, Pallas kernels, merge_split(): pl.pallas_call(merge_split_kernel, grid=(8,), in_specs=[pl.BlockSpec(memo...  8.34 us
    all_to_all x1, starting transfers between devices, x_and_y(): lax.all_to_all(blocks, ('lat', 'lon'), 0, 0, tiled=True, axis_index_group...  6.75 us
  transfers between devices with their start and end apart: 23, of which 10 were waited for; matrix products, arithmetic and copies ran while one was open for 3% of the time, Pallas kernels for 8%

profile of v5, /device:TPU:1, one launch (start us, length us, event | category | flops | bytes accessed | tf_op | source)
XLA Modules:
  0.0 134.2 jit_solution(2154904502942599101)
XLA Ops:
  9.3 2.5 %collective-permute-start = (bf16[64,128]{1,0:T(8,128)(2,1)S(1)}, bf16[64,128]{1,0:T(8,128)(2,1)S(1)}, u32[]{:S(2)}, u32[]{:S(2)}) collective-permute-start(bf16[64,128]{1,0:T(8,128)(2,1)S(1)} %maximum_maximum_fusion), channel_id=1, source_target_pairs={{0,2},{16,18},{2,4},{18,20},{4,6},{20,22},{6,8},{22,24},{8,10},{24... | collective-permute-start | bytes 49160 | tf_op jit(solution)/shard_map/ppermute | solution.py:403
  11.8 4.0 %collective-permute-start.1 = (bf16[64,128]{1,0:T(8,128)(2,1)S(1)}, bf16[64,128]{1,0:T(8,128)(2,1)S(1)}, u32[]{:S(2)}, u32[]{:S(2)}) collective-permute-start(bf16[64,128]{1,0:T(8,128)(2,1)S(1)} %maximum_maximum_fusion), channel_id=1, source_target_pairs={{0,14},{16,30},{2,0},{18,16},{4,2},{20,18},{6,4},{22,20},{8,6},{24... | collective-permute-start | bytes 49160 | tf_op jit(solution)/shard_map/ppermute | solution.py:403
  16.7 6.8 %all-to-all-start = ((bf16[16,128,128]{2,1,0:T(8,128)(2,1)}), bf16[16,128,128]{2,1,0:T(8,128)(2,1)S(1)}, u32[]{:S(2)}, u32[]{:S(2)}) async-start(bf16[16,128,128]{2,1,0:T(8,128)(2,1)} %broadcast_in_dim.2), calls=%async_computation | async-start | bytes 1048576 | tf_op jit(solution)/shard_map/all_to_all | solution.py:423
  24.9 1.5 %collective-permute-start.2 = (bf16[3,64,128]{2,1,0:T(8,128)(2,1)S(1)}, bf16[3,64,128]{2,1,0:T(8,128)(2,1)S(1)}, u32[]{:S(2)}, u32[]{:S(2)}) collective-permute-start(bf16[3,64,128]{2,1,0:T(8,128)(2,1)S(1)} %pad_maximum_fusion.8), channel_id=1, source_target_pairs={{0,6},{16,22},{2,8},{18,24},{4,10},{20,26},{6,12},{22,28},{8,14},{... | collective-permute-start | bytes 147464 | tf_op jit(solution)/shard_map/ppermute | solution.py:403
  26.5 2.9 %collective-permute-start.3 = (bf16[2,64,128]{2,1,0:T(8,128)(2,1)S(1)}, bf16[2,64,128]{2,1,0:T(8,128)(2,1)S(1)}, u32[]{:S(2)}, u32[]{:S(2)}) collective-permute-start(bf16[2,64,128]{2,1,0:T(8,128)(2,1)S(1)} %slice.57), channel_id=1, source_target_pairs={{0,10},{16,26},{2,12},{18,28},{4,14},{20,30},{6,0},{22,16},{8,2},{... | collective-permute-start | bytes 98312 | tf_op jit(solution)/shard_map/ppermute | solution.py:403
  29.4 1.9 %collective-permute-done.3 = bf16[2,64,128]{2,1,0:T(8,128)(2,1)S(1)} collective-permute-done((bf16[2,64,128]{2,1,0:T(8,128)(2,1)S(1)}, bf16[2,64,128]{2,1,0:T(8,128)(2,1)S(1)}, u32[]{:S(2)}, u32[]{:S(2)}) %collective-permute-start.3) | collective-permute-done | bytes 32800 | tf_op jit(solution)/shard_map/ppermute | solution.py:403
  31.5 4.3 %collective-permute-done.4 = bf16[4,3,24,512]{3,2,1,0:T(8,128)(2,1)S(1)} collective-permute-done((bf16[4,3,24,512]{3,2,1,0:T(8,128)(2,1)S(1)}, bf16[4,3,24,512]{3,2,1,0:T(8,128)(2,1)S(1)}, u32[]{:S(2)}, u32[]{:S(2)}) %collective-permute-start.4) | collective-permute-done | bytes 294944 | tf_op jit(solution)/shard_map/ppermute | solution.py:391
  36.7 3.5 %collective-permute-start.8 = (bf16[4,12,6,512]{3,2,1,0:T(8,128)(2,1)S(1)}, bf16[4,12,6,512]{3,2,1,0:T(8,128)(2,1)S(1)}, u32[]{:S(2)}, u32[]{:S(2)}) collective-permute-start(bf16[4,12,6,512]{3,2,1,0:T(8,128)(2,1)S(1)} %pad_maximum_fusion.6), channel_id=1, source_target_pairs={{0,15},{1,0},{2,1},{3,2},{4,3},{5,4},{6,5},{7,6},{8,7},{9,8},{10,9... | collective-permute-start | bytes 884744 | tf_op jit(solution)/shard_map/ppermute | solution.py:391
  41.3 2.5 %collective-permute-start.7 = (bf16[8,64,128]{2,1,0:T(8,128)(2,1)S(1)}, bf16[8,64,128]{2,1,0:T(8,128)(2,1)S(1)}, u32[]{:S(2)}, u32[]{:S(2)}) collective-permute-start(bf16[8,64,128]{2,1,0:T(8,128)(2,1)S(1)} %constant_dynamic-update-slice_fusion), channel_id=1, source_target_pairs={{0,33},{16,49},{2,35},{18,51},{4,37},{20,53},{6,39},{22,55},{8,41}... | collective-permute-start | bytes 393224 | tf_op jit(solution)/shard_map/ppermute | solution.py:403
  44.0 9.8 %collective-permute-done.5 = bf16[8,64,128]{2,1,0:T(8,128)(2,1)S(1)} collective-permute-done((bf16[8,64,128]{2,1,0:T(8,128)(2,1)S(1)}, bf16[8,64,128]{2,1,0:T(8,128)(2,1)S(1)}, u32[]{:S(2)}, u32[]{:S(2)}) %collective-permute-start.5) | collective-permute-done | bytes 131104 | tf_op jit(solution)/shard_map/ppermute | solution.py:403
  56.4 2.5 %collective-permute-start.10 = (bf16[4,8,32,128]{3,2,1,0:T(8,128)(2,1)S(1)}, bf16[4,8,32,128]{3,2,1,0:T(8,128)(2,1)S(1)}, u32[]{:S(2)}, u32[]{:S(2)}) collective-permute-start(bf16[4,8,32,128]{3,2,1,0:T(8,128)(2,1)S(1)} %get-tuple-element.59.refs_0_), channel_id=1, source_target_pairs={{0,128},{16,144},{2,130},{18,146},{4,132},{20,148},{6,134},{22,150... | collective-permute-start | bytes 786440 | tf_op jit(solution)/shard_map/ppermute | solution.py:403
  60.8 4.7 %collective-permute-done.10 = bf16[4,8,32,128]{3,2,1,0:T(8,128)(2,1)S(1)} collective-permute-done((bf16[4,8,32,128]{3,2,1,0:T(8,128)(2,1)S(1)}, bf16[4,8,32,128]{3,2,1,0:T(8,128)(2,1)S(1)}, u32[]{:S(2)}, u32[]{:S(2)}) %collective-permute-start.10) | collective-permute-done | bytes 262176 | tf_op jit(solution)/shard_map/ppermute | solution.py:403
  65.5 5.0 %collective-permute-done.11 = bf16[4,8,32,128]{3,2,1,0:T(8,128)(2,1)S(1)} collective-permute-done((bf16[4,8,32,128]{3,2,1,0:T(8,128)(2,1)S(1)}, bf16[4,8,32,128]{3,2,1,0:T(8,128)(2,1)S(1)}, u32[]{:S(2)}, u32[]{:S(2)}) %collective-permute-start.11) | collective-permute-done | bytes 262176 | tf_op jit(solution)/shard_map/ppermute | solution.py:403
  73.8 2.0 %collective-permute-start.17 = (bf16[4,8,32,128]{3,2,1,0:T(8,128)(2,1)}, bf16[4,8,32,128]{3,2,1,0:T(8,128)(2,1)S(1)}, u32[]{:S(2)}, u32[]{:S(2)}) collective-permute-start(bf16[4,8,32,128]{3,2,1,0:T(8,128)(2,1)} %get-tuple-element.58), channel_id=1, source_target_pairs={{0,128},{16,144},{2,130},{18,146},{4,132},{20,148},{6,134},{22,150... | collective-permute-start | bytes 786440 | tf_op jit(solution)/shard_map/ppermute | solution.py:403
  75.8 1.6 %collective-permute-start.18 = (bf16[4,8,32,128]{3,2,1,0:T(8,128)(2,1)}, bf16[4,8,32,128]{3,2,1,0:T(8,128)(2,1)S(1)}, u32[]{:S(2)}, u32[]{:S(2)}) collective-permute-start(bf16[4,8,32,128]{3,2,1,0:T(8,128)(2,1)} %get-tuple-element.58), channel_id=1, source_target_pairs={{0,192},{16,208},{2,194},{18,210},{4,196},{20,212},{6,198},{22,214... | collective-permute-start | bytes 786440 | tf_op jit(solution)/shard_map/ppermute | solution.py:403
  77.4 5.9 %encode_band1.1 = (bf16[4,144,512]{2,1,0:T(8,128)(2,1)S(1)}, bf16[512,2048]{1,0:T(8,128)(2,1)S(1)}) custom-call(s32[5]{0:T(128)S(1)} %stack.81.place_ref, bf16[4,144,512]{2,1,0:T(8,128)(2,1)S(1)} %bitcast.42, f32[1,512]{1,0:T(1,128)S(1)} %bitcast.46, bf16[144,144]{1,0:T(8,128)(2,1)S(1)} %copy-done.9, bf16[144,144]{1,0:T(8,128)(2,1)S(1)} %copy-done.3, ...), custom_call_target="tpu_custom_call" | custom-call | flops 2000000000 | bytes 4000000 | tf_op jit(solution)/shard_map/encode_band1/pallas_call | solution.py:278
  83.3 5.0 %encode_band0.1 = bf16[4,144,512]{2,1,0:T(8,128)(2,1)S(1)} custom-call(s32[5]{0:T(128)S(1)} %stack.81.place_ref, bf16[4,144,512]{2,1,0:T(8,128)(2,1)S(1)} %bitcast.41, f32[1,512]{1,0:T(1,128)S(1)} %bitcast.47, bf16[144,144]{1,0:T(8,128)(2,1)S(1)} %copy-done.9, bf16[144,144]{1,0:T(8,128)(2,1)S(1)} %copy-done.3, bf16[512,2048]{1,0:T(8,128)(2,1)S(1)} %get-tuple-element.47.refs_0_), custom_call_target="tpu_custom_call" | custom-call | flops 2000000000 | bytes 4000000 | tf_op jit(solution)/shard_map/encode_band0/pallas_call | solution.py:278
  88.5 1.3 collective-permute-start.20
  89.9 2.7 %collective-permute-start.19 = (bf16[4,9,6,512]{3,2,1,0:T(8,128)(2,1)S(1)}, bf16[4,9,6,512]{3,2,1,0:T(8,128)(2,1)S(1)}, u32[]{:S(2)}, u32[]{:S(2)}) collective-permute-start(bf16[4,9,6,512]{3,2,1,0:T(8,128)(2,1)S(1)} %pad_maximum_fusion.7), channel_id=1, source_target_pairs={{0,1},{1,2},{2,3},{3,4},{4,5},{5,6},{6,7},{7,8},{8,9},{9,10},{10,1... | collective-permute-start | bytes 663560 | tf_op jit(solution)/shard_map/ppermute | solution.py:391
  93.2 1.9 %collective-permute-start.14 = (bf16[4,3,6,512]{3,2,1,0:T(8,128)(2,1)S(1)}, bf16[4,3,6,512]{3,2,1,0:T(8,128)(2,1)S(1)}, u32[]{:S(2)}, u32[]{:S(2)}) collective-permute-start(bf16[4,3,6,512]{3,2,1,0:T(8,128)(2,1)S(1)} %slice.73), channel_id=1, source_target_pairs={{0,17},{1,18},{2,19},{3,20},{4,21},{5,22},{6,23},{7,24},{8,25},{9,... | collective-permute-start | bytes 221192 | tf_op jit(solution)/shard_map/ppermute | solution.py:391
  95.1 9.4 %collective-permute-done.14 = bf16[4,3,6,512]{3,2,1,0:T(8,128)(2,1)S(1)} collective-permute-done((bf16[4,3,6,512]{3,2,1,0:T(8,128)(2,1)S(1)}, bf16[4,3,6,512]{3,2,1,0:T(8,128)(2,1)S(1)}, u32[]{:S(2)}, u32[]{:S(2)}) %collective-permute-start.14) | collective-permute-done | bytes 73760 | tf_op jit(solution)/shard_map/ppermute | solution.py:391
  105.2 3.4 %copy-done = bf16[64,4,128,128]{3,2,1,0:T(8,128)(2,1)S(1)} copy-done((bf16[64,4,128,128]{3,2,1,0:T(8,128)(2,1)S(1)}, bf16[64,4,128,128]{3,2,1,0:T(8,128)(2,1)}, u32[]{:S(2)}) %copy-start) | copy-done | bytes 8388632
  108.6 8.3 %merge_split.1 = (bf16[4,288,512]{2,1,0:T(8,128)(2,1)S(1)}, bf16[512,2048]{1,0:T(8,128)(2,1)S(1)}) custom-call(s32[5]{0:T(128)S(1)} %stack.81.place_ref, bf16[4,2,144,512]{3,2,1,0:T(8,128)(2,1)S(1)} %bitcast.34, f32[1,2048]{1,0:T(1,128)S(1)} %bitcast.43, f32[1,512]{1,0:T(1,128)S(1)} %bitcast.44, bf16[8,2,4,4,128,128]{5,4,3,2,1,0:T(8,128)(2,1)S(1)} %bitcast.33, ...), custom_call_target="tpu_custom_call" | custom-call | tf_op jit(solution)/shard_map/merge_split/pallas_call | solution.py:308
  117.0 10.4 %decode.1 = bf16[4,2,144,512]{3,2,1,0:T(8,128)(2,1)} custom-call(bf16[4,4,72,512]{3,2,1,0:T(8,128)(2,1)S(1)} %bitcast.37, f32[1,512]{1,0:T(1,128)S(1)} %bitcast.45, bf16[512,2048]{1,0:T(8,128)(2,1)S(1)} %get-tuple-element.54.w_ref, bf16[288,288]{1,0:T(8,128)(2,1)S(1)} %copy-done.2, bf16[144,144]{1,0:T(8,128)(2,1)S(1)} %copy-done.4), custom_call_target="tpu_custom_call" | custom-call | tf_op jit(solution)/shard_map/decode/pallas_call | solution.py:355
  (82 shorter events, 16.6 us)
Async XLA Ops:
  6.5 17.0 %copy-start.11 = (bf16[4,12,24,512]{3,2,1,0:T(8,128)(2,1)S(1)}, bf16[4,12,24,512]{3,2,1,0:T(8,128)(2,1)}, u32[]{:S(2)}) copy-start(bf16[4,12,24,512]{3,2,1,0:T(8,128)(2,1)} %param.18) | copy-start | bytes 3538948
  9.3 14.3 %collective-permute-start = (bf16[64,128]{1,0:T(8,128)(2,1)S(1)}, bf16[64,128]{1,0:T(8,128)(2,1)S(1)}, u32[]{:S(2)}, u32[]{:S(2)}) collective-permute-start(bf16[64,128]{1,0:T(8,128)(2,1)S(1)} %maximum_maximum_fusion), channel_id=1, source_target_pairs={{0,2},{16,18},{2,4},{18,20},{4,6},{20,22},{6,8},{22,24},{8,10},{24... | collective-permute-start | bytes 49160 | tf_op jit(solution)/shard_map/ppermute | solution.py:403
  11.8 11.8 %collective-permute-start.1 = (bf16[64,128]{1,0:T(8,128)(2,1)S(1)}, bf16[64,128]{1,0:T(8,128)(2,1)S(1)}, u32[]{:S(2)}, u32[]{:S(2)}) collective-permute-start(bf16[64,128]{1,0:T(8,128)(2,1)S(1)} %maximum_maximum_fusion), channel_id=1, source_target_pairs={{0,14},{16,30},{2,0},{18,16},{4,2},{20,18},{6,4},{22,20},{8,6},{24... | collective-permute-start | bytes 49160 | tf_op jit(solution)/shard_map/ppermute | solution.py:403
  16.7 19.1 %all-to-all-start = ((bf16[16,128,128]{2,1,0:T(8,128)(2,1)}), bf16[16,128,128]{2,1,0:T(8,128)(2,1)S(1)}, u32[]{:S(2)}, u32[]{:S(2)}) async-start(bf16[16,128,128]{2,1,0:T(8,128)(2,1)} %broadcast_in_dim.2), calls=%async_computation | async-start | bytes 1048576 | tf_op jit(solution)/shard_map/all_to_all | solution.py:423
  23.5 81.7 %all-gather.3.cloned.1.call-start = ((), (), s32[]{:S(2)}) async-start(), calls=%async_computation.1 | async-start | bytes 8912896 | tf_op jit(solution)/shard_map/all_gather | solution.py:431
  23.6 12.1 %collective-permute-start.4 = (bf16[4,3,24,512]{3,2,1,0:T(8,128)(2,1)S(1)}, bf16[4,3,24,512]{3,2,1,0:T(8,128)(2,1)S(1)}, u32[]{:S(2)}, u32[]{:S(2)}) collective-permute-start(bf16[4,3,24,512]{3,2,1,0:T(8,128)(2,1)S(1)} %get-tuple-element.32), channel_id=1, source_target_pairs={{0,240},{16,0},{32,16},{48,32},{64,48},{80,64},{96,80},{112,96},{1... | collective-permute-start | bytes 884744 | tf_op jit(solution)/shard_map/ppermute | solution.py:391
  24.9 6.6 %collective-permute-start.2 = (bf16[3,64,128]{2,1,0:T(8,128)(2,1)S(1)}, bf16[3,64,128]{2,1,0:T(8,128)(2,1)S(1)}, u32[]{:S(2)}, u32[]{:S(2)}) collective-permute-start(bf16[3,64,128]{2,1,0:T(8,128)(2,1)S(1)} %pad_maximum_fusion.8), channel_id=1, source_target_pairs={{0,6},{16,22},{2,8},{18,24},{4,10},{20,26},{6,12},{22,28},{8,14},{... | collective-permute-start | bytes 147464 | tf_op jit(solution)/shard_map/ppermute | solution.py:403
  26.5 4.9 %collective-permute-start.3 = (bf16[2,64,128]{2,1,0:T(8,128)(2,1)S(1)}, bf16[2,64,128]{2,1,0:T(8,128)(2,1)S(1)}, u32[]{:S(2)}, u32[]{:S(2)}) collective-permute-start(bf16[2,64,128]{2,1,0:T(8,128)(2,1)S(1)} %slice.57), channel_id=1, source_target_pairs={{0,10},{16,26},{2,12},{18,28},{4,14},{20,30},{6,0},{22,16},{8,2},{... | collective-permute-start | bytes 98312 | tf_op jit(solution)/shard_map/ppermute | solution.py:403
  36.7 18.6 %collective-permute-start.8 = (bf16[4,12,6,512]{3,2,1,0:T(8,128)(2,1)S(1)}, bf16[4,12,6,512]{3,2,1,0:T(8,128)(2,1)S(1)}, u32[]{:S(2)}, u32[]{:S(2)}) collective-permute-start(bf16[4,12,6,512]{3,2,1,0:T(8,128)(2,1)S(1)} %pad_maximum_fusion.6), channel_id=1, source_target_pairs={{0,15},{1,0},{2,1},{3,2},{4,3},{5,4},{6,5},{7,6},{8,7},{9,8},{10,9... | collective-permute-start | bytes 884744 | tf_op jit(solution)/shard_map/ppermute | solution.py:391
  40.2 13.5 %collective-permute-start.5 = (bf16[8,64,128]{2,1,0:T(8,128)(2,1)S(1)}, bf16[8,64,128]{2,1,0:T(8,128)(2,1)S(1)}, u32[]{:S(2)}, u32[]{:S(2)}) collective-permute-start(bf16[8,64,128]{2,1,0:T(8,128)(2,1)S(1)} %constant_dynamic-update-slice_fusion), channel_id=1, source_target_pairs={{0,32},{16,48},{2,34},{18,50},{4,36},{20,52},{6,38},{22,54},{8,40}... | collective-permute-start | bytes 393224 | tf_op jit(solution)/shard_map/ppermute | solution.py:403
  41.3 13.3 %collective-permute-start.6 = (bf16[8,64,128]{2,1,0:T(8,128)(2,1)S(1)}, bf16[8,64,128]{2,1,0:T(8,128)(2,1)S(1)}, u32[]{:S(2)}, u32[]{:S(2)}) collective-permute-start(bf16[8,64,128]{2,1,0:T(8,128)(2,1)S(1)} %constant_dynamic-update-slice_fusion), channel_id=1, source_target_pairs={{0,1},{16,17},{2,3},{18,19},{4,5},{20,21},{6,7},{22,23},{8,9},{24,... | collective-permute-start | bytes 393224 | tf_op jit(solution)/shard_map/ppermute | solution.py:403
  41.3 14.0 %collective-permute-start.7 = (bf16[8,64,128]{2,1,0:T(8,128)(2,1)S(1)}, bf16[8,64,128]{2,1,0:T(8,128)(2,1)S(1)}, u32[]{:S(2)}, u32[]{:S(2)}) collective-permute-start(bf16[8,64,128]{2,1,0:T(8,128)(2,1)S(1)} %constant_dynamic-update-slice_fusion), channel_id=1, source_target_pairs={{0,33},{16,49},{2,35},{18,51},{4,37},{20,53},{6,39},{22,55},{8,41}... | collective-permute-start | bytes 393224 | tf_op jit(solution)/shard_map/ppermute | solution.py:403
  56.4 9.2 %collective-permute-start.10 = (bf16[4,8,32,128]{3,2,1,0:T(8,128)(2,1)S(1)}, bf16[4,8,32,128]{3,2,1,0:T(8,128)(2,1)S(1)}, u32[]{:S(2)}, u32[]{:S(2)}) collective-permute-start(bf16[4,8,32,128]{3,2,1,0:T(8,128)(2,1)S(1)} %get-tuple-element.59.refs_0_), channel_id=1, source_target_pairs={{0,128},{16,144},{2,130},{18,146},{4,132},{20,148},{6,134},{22,150... | collective-permute-start | bytes 786440 | tf_op jit(solution)/shard_map/ppermute | solution.py:403
  58.9 11.7 %collective-permute-start.11 = (bf16[4,8,32,128]{3,2,1,0:T(8,128)(2,1)S(1)}, bf16[4,8,32,128]{3,2,1,0:T(8,128)(2,1)S(1)}, u32[]{:S(2)}, u32[]{:S(2)}) collective-permute-start(bf16[4,8,32,128]{3,2,1,0:T(8,128)(2,1)S(1)} %get-tuple-element.59.refs_0_), channel_id=1, source_target_pairs={{0,192},{16,208},{2,194},{18,210},{4,196},{20,212},{6,198},{22,214... | collective-permute-start | bytes 786440 | tf_op jit(solution)/shard_map/ppermute | solution.py:403
  59.7 12.1 %collective-permute-start.9 = (bf16[4,8,32,128]{3,2,1,0:T(8,128)(2,1)S(1)}, bf16[4,8,32,128]{3,2,1,0:T(8,128)(2,1)S(1)}, u32[]{:S(2)}, u32[]{:S(2)}) collective-permute-start(bf16[4,8,32,128]{3,2,1,0:T(8,128)(2,1)S(1)} %get-tuple-element.59.refs_0_), channel_id=1, source_target_pairs={{0,64},{16,80},{2,66},{18,82},{4,68},{20,84},{6,70},{22,86},{8,72}... | collective-permute-start | bytes 786440 | tf_op jit(solution)/shard_map/ppermute | solution.py:403
  71.9 5.4 %collective-permute-start.13 = (bf16[3,4,8,32,128]{4,3,2,1,0:T(8,128)(2,1)S(1)}, bf16[3,4,8,32,128]{4,3,2,1,0:T(8,128)(2,1)S(1)}, u32[]{:S(2)}, u32[]{:S(2)}) collective-permute-start(bf16[3,4,8,32,128]{4,3,2,1,0:T(8,128)(2,1)S(1)} %pad_maximum_fusion.2.refs_1_), channel_id=1, source_target_pairs={{0,16},{16,0},{2,18},{18,2},{4,20},{20,4},{6,22},{22,6},{8,24},{24... | collective-permute-start | bytes 2359304 | tf_op jit(solution)/shard_map/ppermute | solution.py:403
  72.4 4.9 %collective-permute-start.12 = (bf16[4,8,32,128]{3,2,1,0:T(8,128)(2,1)S(1)}, bf16[4,8,32,128]{3,2,1,0:T(8,128)(2,1)S(1)}, u32[]{:S(2)}, u32[]{:S(2)}) collective-permute-start(bf16[4,8,32,128]{3,2,1,0:T(8,128)(2,1)S(1)} %get-tuple-element.59.refs_0_), channel_id=1, source_target_pairs={{0,16},{16,0},{2,18},{18,2},{4,20},{20,4},{6,22},{22,6},{8,24},{24... | collective-permute-start | bytes 786440 | tf_op jit(solution)/shard_map/ppermute | solution.py:403
  72.6 15.7 %collective-permute-start.16 = (bf16[4,8,32,128]{3,2,1,0:T(8,128)(2,1)}, bf16[4,8,32,128]{3,2,1,0:T(8,128)(2,1)S(1)}, u32[]{:S(2)}, u32[]{:S(2)}) collective-permute-start(bf16[4,8,32,128]{3,2,1,0:T(8,128)(2,1)} %get-tuple-element.58), channel_id=1, source_target_pairs={{0,64},{16,80},{2,66},{18,82},{4,68},{20,84},{6,70},{22,86},{8,72}... | collective-permute-start | bytes 786440 | tf_op jit(solution)/shard_map/ppermute | solution.py:403
  73.8 14.5 %collective-permute-start.17 = (bf16[4,8,32,128]{3,2,1,0:T(8,128)(2,1)}, bf16[4,8,32,128]{3,2,1,0:T(8,128)(2,1)S(1)}, u32[]{:S(2)}, u32[]{:S(2)}) collective-permute-start(bf16[4,8,32,128]{3,2,1,0:T(8,128)(2,1)} %get-tuple-element.58), channel_id=1, source_target_pairs={{0,128},{16,144},{2,130},{18,146},{4,132},{20,148},{6,134},{22,150... | collective-permute-start | bytes 786440 | tf_op jit(solution)/shard_map/ppermute | solution.py:403
  75.8 12.5 %collective-permute-start.18 = (bf16[4,8,32,128]{3,2,1,0:T(8,128)(2,1)}, bf16[4,8,32,128]{3,2,1,0:T(8,128)(2,1)S(1)}, u32[]{:S(2)}, u32[]{:S(2)}) collective-permute-start(bf16[4,8,32,128]{3,2,1,0:T(8,128)(2,1)} %get-tuple-element.58), channel_id=1, source_target_pairs={{0,192},{16,208},{2,194},{18,210},{4,196},{20,212},{6,198},{22,214... | collective-permute-start | bytes 786440 | tf_op jit(solution)/shard_map/ppermute | solution.py:403
  88.5 16.7 %collective-permute-start.20 = (bf16[4,4,8,32,128]{4,3,2,1,0:T(8,128)(2,1)S(1)}, bf16[4,4,8,32,128]{4,3,2,1,0:T(8,128)(2,1)S(1)}, u32[]{:S(2)}, u32[]{:S(2)}) collective-permute-start(bf16[4,4,8,32,128]{4,3,2,1,0:T(8,128)(2,1)S(1)} %pad_maximum_fusion.1.own_ref), channel_id=1, source_target_pairs={{0,16},{16,0},{2,18},{18,2},{4,20},{20,4},{6,22},{22,6},{8,24},{24... | collective-permute-start | bytes 3145736 | tf_op jit(solution)/shard_map/ppermute | solution.py:403
  89.9 14.6 %collective-permute-start.19 = (bf16[4,9,6,512]{3,2,1,0:T(8,128)(2,1)S(1)}, bf16[4,9,6,512]{3,2,1,0:T(8,128)(2,1)S(1)}, u32[]{:S(2)}, u32[]{:S(2)}) collective-permute-start(bf16[4,9,6,512]{3,2,1,0:T(8,128)(2,1)S(1)} %pad_maximum_fusion.7), channel_id=1, source_target_pairs={{0,1},{1,2},{2,3},{3,4},{4,5},{5,6},{6,7},{7,8},{8,9},{9,10},{10,1... | collective-permute-start | bytes 663560 | tf_op jit(solution)/shard_map/ppermute | solution.py:391
  92.6 12.0 %collective-permute-start.15 = (bf16[4,3,18,512]{3,2,1,0:T(8,128)(2,1)S(1)}, bf16[4,3,18,512]{3,2,1,0:T(8,128)(2,1)S(1)}, u32[]{:S(2)}, u32[]{:S(2)}) collective-permute-start(bf16[4,3,18,512]{3,2,1,0:T(8,128)(2,1)S(1)} %slice.74), channel_id=1, source_target_pairs={{0,16},{16,32},{32,48},{48,64},{64,80},{80,96},{96,112},{112,128},... | collective-permute-start | bytes 663560 | tf_op jit(solution)/shard_map/ppermute | solution.py:391
  93.2 11.4 %collective-permute-start.14 = (bf16[4,3,6,512]{3,2,1,0:T(8,128)(2,1)S(1)}, bf16[4,3,6,512]{3,2,1,0:T(8,128)(2,1)S(1)}, u32[]{:S(2)}, u32[]{:S(2)}) collective-permute-start(bf16[4,3,6,512]{3,2,1,0:T(8,128)(2,1)S(1)} %slice.73), channel_id=1, source_target_pairs={{0,17},{1,18},{2,19},{3,20},{4,21},{5,22},{6,23},{7,24},{8,25},{9,... | collective-permute-start | bytes 221192 | tf_op jit(solution)/shard_map/ppermute | solution.py:391
  (12 other events, 120.1 us)
Sparse Core Ops, SparseCore 0:
  36.7 55.6 all-gather.2
